TPU v7x, 32 devices: a whole 2x2x4 slice. The times are simulated.
32 devices in a mesh: grp: 2 (over x), span: 16 (over z, y, core).
Axes of the slice: x: 2, y: 2, z: 4, core: 2. Of those that a mesh axis runs over, the one named last changes fastest.
Arguments:
- first_exposure: bfloat16 [1920, 96, 192], P(('grp', 'span')), parts along dimension 0, may hold values from 0 to 30
- second_exposure: bfloat16 [1920, 96, 192], P(('grp', 'span')), parts along dimension 0, may hold values from 0 to 30
- windows: int32 [256], P(('grp', 'span')), parts along dimension 0, may hold values from 0 to 10239, as said below
- shifts: int32 [3, 256], P(None, ('grp', 'span')), parts along dimension 1, may hold values from -8 to 8, as said below
Outputs:
- smoothed_update: float32 [3, 160, 128], P(None, ('grp', 'span')), parts along dimension 1
There are 2 independent parts, one for each index of `grp`. A program takes and returns all parts, laid end to end along the dimension named above; each array names one. Nothing has to cross between parts.
Inputs may be any that keep to these rules, and one draw needn't show every extreme that they name: The windows of one device are distinct nodes whose spanwise grid row j has j // 5 equal to that device's index along span; exactly 4 of them have j % 5 < 2. `shifts`: row 0 is the spanwise shift (at most 3 in size), row 1 the wall-normal one (at most 4 in size), row 2 the streamwise one (at most 8 in size).
All inputs are finite; a program needn't handle non-finite values.
Results may differ from a plain program's by a relative error of at most 0.0022.
Values may be sent and summed in bfloat16 or wider, within the bound.
No kernel may reach another device: no remote copies, remote signals or barrier semaphores. Data moves between devices by JAX's collectives and lax.ppermute only.
A program may use at most 128 MiB of HBM per device.

v0:
```python
import jax
import jax.numpy as jnp
from jax import lax
from jax.sharding import PartitionSpec as P

W = 48
STRIDE = 12
CY = 60
DYM = 3
DZM = 4
DXM = 8
GZ = 8
GX = 16
GZX = 128


SHARP = 80.0
EPSILON = 1e-06


def padded_2(block, sides, width):
    for axis, dim in sides:
        count = lax.axis_size(axis)
        forward = [(i, i + 1) for i in range(count - 1)]
        backward = [(target, source) for source, target in forward]
        low = lax.ppermute(
            lax.slice_in_dim(block, block.shape[dim] - width, None, axis=dim), axis, forward
        )
        high = lax.ppermute(lax.slice_in_dim(block, 0, width, axis=dim), axis, backward)
        block = jnp.concatenate([low, block, high], axis=dim)
    return block


def decode(nodes, shifts):
    half_width = W // 2
    node_row = nodes // GZX
    node_rest = nodes % GZX
    node_deep = node_rest // GX
    node_along = node_rest % GX
    centre_y = STRIDE * node_row + STRIDE // 2
    centre_z = STRIDE * node_deep + STRIDE // 2
    centre_x = STRIDE * node_along + STRIDE // 2
    start_y = centre_y + shifts[0] - half_width - 1
    start_z = centre_z + shifts[1] - half_width - 1
    start_x = centre_x + shifts[2] - half_width - 1
    source_tile = start_y // CY
    return (centre_y, centre_z, centre_x, start_y, start_z, start_x, source_tile)


def correlate(first_windows, second_blocks):
    window_count = first_windows.shape[0]
    first_wide = first_windows.astype(jnp.float32)
    first_centred = (first_wide - jnp.mean(first_wide, axis=(1, 2, 3), keepdims=True)).astype(
        jnp.bfloat16
    )
    second_wide = second_blocks.astype(jnp.float32)
    second_centred = (second_wide - jnp.mean(second_wide, axis=(1, 2, 3), keepdims=True)).astype(
        jnp.bfloat16
    )
    first_back = first_centred.astype(jnp.float32)
    second_back = second_centred.astype(jnp.float32)
    energy_first = jnp.mean(first_back * first_back, axis=(1, 2, 3))
    energy_second = jnp.mean(second_back * second_back, axis=(1, 2, 3))
    normaliser = float(W) ** 3 * jnp.sqrt((energy_first + EPSILON) * (energy_second + EPSILON))
    flat_first = first_centred.reshape(window_count, W, W * W)
    collected = []
    for lag_z in range(3):
        for lag_x in range(3):
            shifted_piece = second_centred[:, :, lag_z : lag_z + W, lag_x : lag_x + W].reshape(
                window_count, W + 2, W * W
            )
            product = jnp.einsum(
                "wyp,wqp->wyq", flat_first, shifted_piece, preferred_element_type=jnp.float32
            )
            for lag_y in range(3):
                collected.append(
                    jnp.sum(jnp.diagonal(product, offset=lag_y, axis1=1, axis2=2), axis=1)
                )
    coherence = (
        jnp.stack(collected, axis=1).reshape(window_count, 3, 3, 3)
        / normaliser[:, None, None, None]
    )
    weights = jnp.exp(SHARP * coherence)
    weight_sum = jnp.sum(weights, axis=(1, 2, 3))
    lag_values = jnp.array([-1.0, 0.0, 1.0], jnp.float32)
    along_y = jnp.sum(weights * lag_values[None, None, None, :], axis=(1, 2, 3)) / weight_sum
    along_z = jnp.sum(weights * lag_values[None, :, None, None], axis=(1, 2, 3)) / weight_sum
    along_x = jnp.sum(weights * lag_values[None, None, :, None], axis=(1, 2, 3)) / weight_sum
    return jnp.stack([along_y, along_z, along_x])


def shards(first_exposure, second_exposure, windows, shifts):
    half_width = W // 2
    device = lax.axis_index("span")
    tile_rows = CY // STRIDE
    pad_z = half_width + 1 + DZM
    pad_x = half_width + 1 + DXM
    decoded = decode(windows, shifts)
    centre_y, centre_z, centre_x, start_y, start_z, start_x, source_tile = decoded
    first_ext = padded_2(first_exposure, (("span", 0),), half_width)
    first_pad = jnp.pad(first_ext, ((0, 0), (half_width, half_width), (half_width, half_width)))

    def cut_first(local_y, local_z, local_x):
        return lax.dynamic_slice(first_pad, (local_y, local_z, local_x), (W, W, W))

    first_windows = jax.vmap(cut_first)(centre_y - CY * device, centre_z, centre_x)
    reach = half_width + 1 + DYM - STRIDE // 2
    second_ext = padded_2(second_exposure, (("span", 0),), reach)
    second_slab = jnp.pad(second_ext, ((0, 0), (pad_z, pad_z), (pad_x, pad_x)))

    def cut_second(local_y, local_z, local_x):
        return lax.dynamic_slice(
            second_slab, (local_y + reach, local_z + pad_z, local_x + pad_x), (W + 2, W + 2, W + 2)
        )

    second_blocks = jax.vmap(cut_second)(start_y - CY * device, start_z, start_x)
    corrections = correlate(first_windows, second_blocks)
    local_nodes = windows - device * tile_rows * GZX
    update = jnp.zeros((3, tile_rows * GZX), jnp.float32).at[:, local_nodes].set(corrections)
    update = update.reshape(3, tile_rows, GZX)
    extended = padded_2(update, (("span", 1),), 1)
    field_grid = extended.reshape(3, tile_rows + 2, GZ, GX)
    centre = field_grid[:, 1:-1]
    padded = jnp.pad(centre, ((0, 0), (0, 0), (1, 1), (1, 1)))
    neighbours = field_grid[:, 2:] + field_grid[:, :-2]
    neighbours = neighbours + padded[:, :, 2:, 1:-1] + padded[:, :, :-2, 1:-1]
    neighbours = neighbours + padded[:, :, 1:-1, 2:] + padded[:, :, 1:-1, :-2]
    smoothed = 0.4 * centre + 0.1 * neighbours
    return smoothed.reshape(3, tile_rows, GZX)


def solution(mesh):
    in_specs = (
        P(("grp", "span"), None, None),
        P(("grp", "span"), None, None),
        P(("grp", "span")),
        P(None, ("grp", "span")),
    )
    out_specs = P(None, ("grp", "span"), None)
    return jax.shard_map(shards, mesh=mesh, in_specs=in_specs, out_specs=out_specs, check_vma=False)
```

profile of v0, /device:TPU:23, one launch (start us, length us, event | category | flops | bytes accessed | tf_op | source)
XLA Modules:
  0.0 358.2 jit_solution(14674295571038600519)
XLA Ops:
  0.0 3.2 fusion.49
  3.2 3.8 %collective-permute-start.2 = (bf16[22,96,192]{2,1,0:T(8,128)(2,1)}, bf16[22,96,192]{2,1,0:T(8,128)(2,1)S(1)}, u32[]{:S(2)}, u32[]{:S(2)}) collective-permute-start(bf16[22,96,192]{2,1,0:T(8,128)(2,1)} %get-tuple-element.66), channel_id=1, source_target_pairs={{0,1},{1,2},{2,3},{3,4},{4,5},{5,6},{6,7},{7,8},{8,9},{9,10},{10,1... | collective-permute-start | bytes 2433032 | tf_op jit(solution)/shard_map/ppermute | solution.py:26
  7.1 1.9 collective-permute-start.3
  9.0 1.6 fusion.50
  10.6 4.5 %collective-permute-start = (bf16[24,96,192]{2,1,0:T(8,128)(2,1)}, bf16[24,96,192]{2,1,0:T(8,128)(2,1)S(1)}, u32[]{:S(2)}, u32[]{:S(2)}) collective-permute-start(bf16[24,96,192]{2,1,0:T(8,128)(2,1)} %get-tuple-element.68), channel_id=1, source_target_pairs={{0,1},{1,2},{2,3},{3,4},{4,5},{5,6},{6,7},{7,8},{8,9},{9,10},{10,1... | collective-permute-start | bytes 2654216 | tf_op jit(solution)/shard_map/ppermute | solution.py:26
  15.1 1.9 collective-permute-start.1
  19.5 5.4 %collective-permute-done.3 = bf16[22,96,192]{2,1,0:T(8,128)(2,1)} collective-permute-done((bf16[22,96,192]{2,1,0:T(8,128)(2,1)}, bf16[22,96,192]{2,1,0:T(8,128)(2,1)}, u32[]{:S(2)}, u32[]{:S(2)}) %collective-permute-start.3) | collective-permute-done | bytes 811040 | tf_op jit(solution)/shard_map/ppermute | solution.py:29
  24.8 17.8 %select_maximum_fusion = bf16[104,154,258]{2,1,0:T(8,128)(2,1)} fusion(bf16[22,96,192]{2,1,0:T(8,128)(2,1)} %collective-permute-done.3, bf16[60,96,192]{2,1,0:T(8,128)(2,1)} %param.8, bf16[22,96,192]{2,1,0:T(8,128)(2,1)S(1)} %collective-permute-done.2), kind=kLoop, calls=%fused_computation.48 | loop fusion | flops 78510432 | bytes 12098112 | tf_op jit(solution)/shard_map/concatenate | solution.py:30
  42.6 45.0 %while.3 = (s32[]{:T(128)}, bf16[104,154,258]{2,1,0:T(8,128)(2,1)}, s32[8,3]{0,1:T(4,128)S(1)}, bf16[8,50,50,50]{3,2,1,0:T(8,128)(2,1)}, s32[]{:T(128)}) while((s32[]{:T(128)}, bf16[104,154,258]{2,1,0:T(8,128)(2,1)}, s32[8,3]{0,1:T(4,128)S(1)}, bf16[8,50,50,50]{3,2,1,0:T(8,128)(2,1)}, s32[]{:T(128)}) %tuple.64), condition=%wide.while_cond.1, body=%wide.while_body.1.sunk | while | flops 2 | bytes 1435261 | solution.py:112
  43.3 5.0 %bitcast_dynamic-update-slice_fusion.5 = bf16[8,50,50,50]{3,2,1,0:T(8,128)(2,1)} fusion(bf16[8,50,50,50]{3,2,1,0:T(8,128)(2,1)} %get-tuple-element.165, s32[]{:T(128)S(6)} %copy.264, bf16[104,154,258]{2,1,0:T(8,128)(2,1)} %get-tuple-element.168, s32[]{:T(128)} %bitcast.186, s32[]{:T(128)} %bitcast.187, s32[]{:T(128)} %bitcast.188), kind=kLoop, calls=%fused_computation.30.clone.1 | loop fusion | bytes 1435140 | tf_op jit(solution)/shard_map/vmap()/gather
  49.0 4.9 %bitcast_dynamic-update-slice_fusion.5 = bf16[8,50,50,50]{3,2,1,0:T(8,128)(2,1)} fusion(bf16[8,50,50,50]{3,2,1,0:T(8,128)(2,1)} %get-tuple-element.165, s32[]{:T(128)S(6)} %copy.264, bf16[104,154,258]{2,1,0:T(8,128)(2,1)} %get-tuple-element.168, s32[]{:T(128)} %bitcast.186, s32[]{:T(128)} %bitcast.187, s32[]{:T(128)} %bitcast.188), kind=kLoop, calls=%fused_computation.30.clone.1 | loop fusion | bytes 1435140 | tf_op jit(solution)/shard_map/vmap()/gather
  54.5 4.9 %bitcast_dynamic-update-slice_fusion.5 = bf16[8,50,50,50]{3,2,1,0:T(8,128)(2,1)} fusion(bf16[8,50,50,50]{3,2,1,0:T(8,128)(2,1)} %get-tuple-element.165, s32[]{:T(128)S(6)} %copy.264, bf16[104,154,258]{2,1,0:T(8,128)(2,1)} %get-tuple-element.168, s32[]{:T(128)} %bitcast.186, s32[]{:T(128)} %bitcast.187, s32[]{:T(128)} %bitcast.188), kind=kLoop, calls=%fused_computation.30.clone.1 | loop fusion | bytes 1435140 | tf_op jit(solution)/shard_map/vmap()/gather
  60.1 5.0 %bitcast_dynamic-update-slice_fusion.5 = bf16[8,50,50,50]{3,2,1,0:T(8,128)(2,1)} fusion(bf16[8,50,50,50]{3,2,1,0:T(8,128)(2,1)} %get-tuple-element.165, s32[]{:T(128)S(6)} %copy.264, bf16[104,154,258]{2,1,0:T(8,128)(2,1)} %get-tuple-element.168, s32[]{:T(128)} %bitcast.186, s32[]{:T(128)} %bitcast.187, s32[]{:T(128)} %bitcast.188), kind=kLoop, calls=%fused_computation.30.clone.1 | loop fusion | bytes 1435140 | tf_op jit(solution)/shard_map/vmap()/gather
  65.8 5.0 %bitcast_dynamic-update-slice_fusion.5 = bf16[8,50,50,50]{3,2,1,0:T(8,128)(2,1)} fusion(bf16[8,50,50,50]{3,2,1,0:T(8,128)(2,1)} %get-tuple-element.165, s32[]{:T(128)S(6)} %copy.264, bf16[104,154,258]{2,1,0:T(8,128)(2,1)} %get-tuple-element.168, s32[]{:T(128)} %bitcast.186, s32[]{:T(128)} %bitcast.187, s32[]{:T(128)} %bitcast.188), kind=kLoop, calls=%fused_computation.30.clone.1 | loop fusion | bytes 1435140 | tf_op jit(solution)/shard_map/vmap()/gather
  71.4 5.0 %bitcast_dynamic-update-slice_fusion.5 = bf16[8,50,50,50]{3,2,1,0:T(8,128)(2,1)} fusion(bf16[8,50,50,50]{3,2,1,0:T(8,128)(2,1)} %get-tuple-element.165, s32[]{:T(128)S(6)} %copy.264, bf16[104,154,258]{2,1,0:T(8,128)(2,1)} %get-tuple-element.168, s32[]{:T(128)} %bitcast.186, s32[]{:T(128)} %bitcast.187, s32[]{:T(128)} %bitcast.188), kind=kLoop, calls=%fused_computation.30.clone.1 | loop fusion | bytes 1435140 | tf_op jit(solution)/shard_map/vmap()/gather
  77.0 5.0 %bitcast_dynamic-update-slice_fusion.5 = bf16[8,50,50,50]{3,2,1,0:T(8,128)(2,1)} fusion(bf16[8,50,50,50]{3,2,1,0:T(8,128)(2,1)} %get-tuple-element.165, s32[]{:T(128)S(6)} %copy.264, bf16[104,154,258]{2,1,0:T(8,128)(2,1)} %get-tuple-element.168, s32[]{:T(128)} %bitcast.186, s32[]{:T(128)} %bitcast.187, s32[]{:T(128)} %bitcast.188), kind=kLoop, calls=%fused_computation.30.clone.1 | loop fusion | bytes 1435140 | tf_op jit(solution)/shard_map/vmap()/gather
  82.7 5.0 %bitcast_dynamic-update-slice_fusion.5 = bf16[8,50,50,50]{3,2,1,0:T(8,128)(2,1)} fusion(bf16[8,50,50,50]{3,2,1,0:T(8,128)(2,1)} %get-tuple-element.165, s32[]{:T(128)S(6)} %copy.264, bf16[104,154,258]{2,1,0:T(8,128)(2,1)} %get-tuple-element.168, s32[]{:T(128)} %bitcast.186, s32[]{:T(128)} %bitcast.187, s32[]{:T(128)} %bitcast.188), kind=kLoop, calls=%fused_computation.30.clone.1 | loop fusion | bytes 1435140 | tf_op jit(solution)/shard_map/vmap()/gather
  87.7 4.2 %convert_reduce_fusion = f32[8]{0:T(128)S(1)} fusion(bf16[8,50,50,50]{3,2,1,0:T(8,128)(2,1)} %get-tuple-element.22), kind=kLoop, calls=%fused_computation.47 | loop fusion | flops 1999992 | bytes 2000032 | tf_op jit(solution)/shard_map/reduce_sum | solution.py:57
  92.0 3.5 multiply_reduce_fusion
  95.4 16.6 %fusion.48 = (bf16[8,50,48,48]{3,2,1,0:T(8,128)(2,1)}, bf16[8,50,48,48]{3,2,1,0:T(8,128)(2,1)}, bf16[8,50,48,48]{3,2,1,0:T(8,128)(2,1)}, bf16[8,50,48,48]{3,2,1,...) fusion(bf16[8,50,50,50]{3,2,1,0:T(8,128)(2,1)S(1)} %get-tuple-e, ...), kind=kLoop, calls=%fused_computation.163 | loop fusion | bytes 33177600 | tf_op jit(solution)/shard_map/slice | solution.py:69
  112.0 20.7 %reshape.433 = bf16[8,50,2304]{2,1,0:T(8,128)(2,1)} reshape(bf16[8,50,48,48]{3,2,1,0:T(8,128)(2,1)} %get-tuple-element.57) | data formatting | bytes 3686400 | tf_op jit(solution)/shard_map/reshape | solution.py:69
  132.7 7.9 %reshape.432 = bf16[8,50,2304]{2,1,0:T(8,128)(2,1)} reshape(bf16[8,50,48,48]{3,2,1,0:T(8,128)(2,1)} %get-tuple-element.58) | data formatting | bytes 3686400 | tf_op jit(solution)/shard_map/reshape | solution.py:69
  140.6 7.9 %reshape.431 = bf16[8,50,2304]{2,1,0:T(8,128)(2,1)} reshape(bf16[8,50,48,48]{3,2,1,0:T(8,128)(2,1)} %get-tuple-element.59) | data formatting | bytes 3686400 | tf_op jit(solution)/shard_map/reshape | solution.py:69
  148.5 7.9 %reshape.430 = bf16[8,50,2304]{2,1,0:T(8,128)(2,1)} reshape(bf16[8,50,48,48]{3,2,1,0:T(8,128)(2,1)} %get-tuple-element.60) | data formatting | bytes 3686400 | tf_op jit(solution)/shard_map/reshape | solution.py:69
  156.4 7.9 %reshape.429 = bf16[8,50,2304]{2,1,0:T(8,128)(2,1)} reshape(bf16[8,50,48,48]{3,2,1,0:T(8,128)(2,1)} %get-tuple-element.61) | data formatting | bytes 3686400 | tf_op jit(solution)/shard_map/reshape | solution.py:69
  164.3 7.9 %reshape.428 = bf16[8,50,2304]{2,1,0:T(8,128)(2,1)} reshape(bf16[8,50,48,48]{3,2,1,0:T(8,128)(2,1)} %get-tuple-element.62) | data formatting | bytes 3686400 | tf_op jit(solution)/shard_map/reshape | solution.py:69
  172.1 7.9 %reshape.427 = bf16[8,50,2304]{2,1,0:T(8,128)(2,1)} reshape(bf16[8,50,48,48]{3,2,1,0:T(8,128)(2,1)} %get-tuple-element.63) | data formatting | bytes 3686400 | tf_op jit(solution)/shard_map/reshape | solution.py:69
  180.0 7.9 %reshape.426 = bf16[8,50,2304]{2,1,0:T(8,128)(2,1)} reshape(bf16[8,50,48,48]{3,2,1,0:T(8,128)(2,1)} %get-tuple-element.64) | data formatting | bytes 3686400 | tf_op jit(solution)/shard_map/reshape | solution.py:69
  187.9 7.9 %reshape.425 = bf16[8,50,2304]{2,1,0:T(8,128)(2,1)} reshape(bf16[8,50,48,48]{3,2,1,0:T(8,128)(2,1)} %get-tuple-element.65) | data formatting | bytes 3686400 | tf_op jit(solution)/shard_map/reshape | solution.py:69
  195.8 11.9 %select_maximum_fusion.2 = bf16[108,144,240]{2,1,0:T(8,128)(2,1)} fusion(bf16[24,96,192]{2,1,0:T(8,128)(2,1)} %collective-permute-done.1, bf16[60,96,192]{2,1,0:T(8,128)(2,1)} %param.7, bf16[24,96,192]{2,1,0:T(8,128)(2,1)S(1)} %collective-permute-done), kind=kLoop, calls=%fused_computation.57 | loop fusion | flops 70917120 | bytes 11446272 | tf_op jit(solution)/shard_map/concatenate | solution.py:30
  207.7 42.5 %while.2 = (s32[]{:T(128)}, bf16[108,144,240]{2,1,0:T(8,128)(2,1)}, s32[8,3]{0,1:T(4,128)S(1)}, bf16[8,48,48,48]{3,2,1,0:T(8,128)(2,1)}, s32[]{:T(128)}) while((s32[]{:T(128)}, bf16[108,144,240]{2,1,0:T(8,128)(2,1)}, s32[8,3]{0,1:T(4,128)S(1)}, bf16[8,48,48,48]{3,2,1,0:T(8,128)(2,1)}, s32[]{:T(128)}) %tuple.61), condition=%wide.while_cond, body=%wide.while_body.sunk | while | flops 2 | bytes 1181309 | solution.py:104
  208.4 4.5 %bitcast_dynamic-update-slice_fusion.4 = bf16[8,48,48,48]{3,2,1,0:T(8,128)(2,1)} fusion(bf16[8,48,48,48]{3,2,1,0:T(8,128)(2,1)} %get-tuple-element.150, s32[]{:T(128)S(6)} %copy.258, bf16[108,144,240]{2,1,0:T(8,128)(2,1)} %get-tuple-element.153, s32[]{:T(128)} %bitcast.182, s32[]{:T(128)} %bitcast.183, s32[]{:T(128)} %bitcast.184), kind=kLoop, calls=%fused_computation.28.clone.1 | loop fusion | bytes 1181188 | tf_op jit(solution)/shard_map/vmap()/gather
  213.5 4.7 %bitcast_dynamic-update-slice_fusion.4 = bf16[8,48,48,48]{3,2,1,0:T(8,128)(2,1)} fusion(bf16[8,48,48,48]{3,2,1,0:T(8,128)(2,1)} %get-tuple-element.150, s32[]{:T(128)S(6)} %copy.258, bf16[108,144,240]{2,1,0:T(8,128)(2,1)} %get-tuple-element.153, s32[]{:T(128)} %bitcast.182, s32[]{:T(128)} %bitcast.183, s32[]{:T(128)} %bitcast.184), kind=kLoop, calls=%fused_computation.28.clone.1 | loop fusion | bytes 1181188 | tf_op jit(solution)/shard_map/vmap()/gather
  218.9 4.5 %bitcast_dynamic-update-slice_fusion.4 = bf16[8,48,48,48]{3,2,1,0:T(8,128)(2,1)} fusion(bf16[8,48,48,48]{3,2,1,0:T(8,128)(2,1)} %get-tuple-element.150, s32[]{:T(128)S(6)} %copy.258, bf16[108,144,240]{2,1,0:T(8,128)(2,1)} %get-tuple-element.153, s32[]{:T(128)} %bitcast.182, s32[]{:T(128)} %bitcast.183, s32[]{:T(128)} %bitcast.184), kind=kLoop, calls=%fused_computation.28.clone.1 | loop fusion | bytes 1181188 | tf_op jit(solution)/shard_map/vmap()/gather
  224.1 4.7 %bitcast_dynamic-update-slice_fusion.4 = bf16[8,48,48,48]{3,2,1,0:T(8,128)(2,1)} fusion(bf16[8,48,48,48]{3,2,1,0:T(8,128)(2,1)} %get-tuple-element.150, s32[]{:T(128)S(6)} %copy.258, bf16[108,144,240]{2,1,0:T(8,128)(2,1)} %get-tuple-element.153, s32[]{:T(128)} %bitcast.182, s32[]{:T(128)} %bitcast.183, s32[]{:T(128)} %bitcast.184), kind=kLoop, calls=%fused_computation.28.clone.1 | loop fusion | bytes 1181188 | tf_op jit(solution)/shard_map/vmap()/gather
  229.5 4.5 %bitcast_dynamic-update-slice_fusion.4 = bf16[8,48,48,48]{3,2,1,0:T(8,128)(2,1)} fusion(bf16[8,48,48,48]{3,2,1,0:T(8,128)(2,1)} %get-tuple-element.150, s32[]{:T(128)S(6)} %copy.258, bf16[108,144,240]{2,1,0:T(8,128)(2,1)} %get-tuple-element.153, s32[]{:T(128)} %bitcast.182, s32[]{:T(128)} %bitcast.183, s32[]{:T(128)} %bitcast.184), kind=kLoop, calls=%fused_computation.28.clone.1 | loop fusion | bytes 1181188 | tf_op jit(solution)/shard_map/vmap()/gather
  234.7 4.8 %bitcast_dynamic-update-slice_fusion.4 = bf16[8,48,48,48]{3,2,1,0:T(8,128)(2,1)} fusion(bf16[8,48,48,48]{3,2,1,0:T(8,128)(2,1)} %get-tuple-element.150, s32[]{:T(128)S(6)} %copy.258, bf16[108,144,240]{2,1,0:T(8,128)(2,1)} %get-tuple-element.153, s32[]{:T(128)} %bitcast.182, s32[]{:T(128)} %bitcast.183, s32[]{:T(128)} %bitcast.184), kind=kLoop, calls=%fused_computation.28.clone.1 | loop fusion | bytes 1181188 | tf_op jit(solution)/shard_map/vmap()/gather
  240.1 4.7 %bitcast_dynamic-update-slice_fusion.4 = bf16[8,48,48,48]{3,2,1,0:T(8,128)(2,1)} fusion(bf16[8,48,48,48]{3,2,1,0:T(8,128)(2,1)} %get-tuple-element.150, s32[]{:T(128)S(6)} %copy.258, bf16[108,144,240]{2,1,0:T(8,128)(2,1)} %get-tuple-element.153, s32[]{:T(128)} %bitcast.182, s32[]{:T(128)} %bitcast.183, s32[]{:T(128)} %bitcast.184), kind=kLoop, calls=%fused_computation.28.clone.1 | loop fusion | bytes 1181188 | tf_op jit(solution)/shard_map/vmap()/gather
  245.5 4.7 %bitcast_dynamic-update-slice_fusion.4 = bf16[8,48,48,48]{3,2,1,0:T(8,128)(2,1)} fusion(bf16[8,48,48,48]{3,2,1,0:T(8,128)(2,1)} %get-tuple-element.150, s32[]{:T(128)S(6)} %copy.258, bf16[108,144,240]{2,1,0:T(8,128)(2,1)} %get-tuple-element.153, s32[]{:T(128)} %bitcast.182, s32[]{:T(128)} %bitcast.183, s32[]{:T(128)} %bitcast.184), kind=kLoop, calls=%fused_computation.28.clone.1 | loop fusion | bytes 1181188 | tf_op jit(solution)/shard_map/vmap()/gather
  250.2 3.5 convert_reduce_fusion.1
  253.7 8.1 %reshape.199 = f32[8,48,2304]{2,1,0:T(8,128)} reshape(bf16[8,48,48,48]{3,2,1,0:T(8,128)(2,1)} %get-tuple-element.14) | data formatting | bytes 5308416 | tf_op jit(solution)/shard_map/convert_element_type | solution.py:52
  261.9 4.8 %multiply_reduce_fusion.1 = f32[8]{0:T(128)} fusion(bf16[8,48,48,48]{3,2,1,0:T(8,128)(2,1)} %get-tuple-element.14, f32[8]{0:T(128)S(1)} %broadcast_multiply_fusion.1), kind=kLoop, calls=%fused_computation.55 | loop fusion | flops 5308408 | bytes 1769536 | tf_op jit(solution)/shard_map/reduce_sum | solution.py:62
  267.0 1.3 copy-done.3
  269.6 1.7 gather_fusion.26
  271.3 1.7 gather_fusion.25
  273.0 2.2 fusion.59
  275.2 1.6 copy.199
  276.8 2.6 gather_fusion.24
  279.4 2.0 gather_fusion.23
  281.4 1.7 gather_fusion.8
  283.1 2.6 gather_fusion.7
  285.7 2.2 fusion.58
  288.5 1.7 gather_fusion.22
  291.2 1.7 gather_fusion.6
  292.8 2.2 fusion.57
  295.7 0.9 gather_fusion.20
  298.5 2.2 fusion.56
  304.4 2.2 fusion.55
  307.3 0.9 gather_fusion.16
  310.1 2.2 fusion.54
  315.8 2.2 fusion.53
  321.7 2.3 fusion.52
  331.7 22.3 %collective-permute-start.4 = (f32[3,1,128]{2,1,0:T(1,128)S(1)}, f32[3,1,128]{2,1,0:T(1,128)S(1)}, u32[]{:S(2)}, u32[]{:S(2)}) collective-permute-start(f32[3,1,128]{2,1,0:T(1,128)S(1)} %copy.252), channel_id=1, source_target_pairs={{1,0},{2,1},{3,2},{4,3},{5,4},{6,5},{7,6},{8,7},{9,8},{10,9},{11,1... | collective-permute-start | bytes 4616 | tf_op jit(solution)/shard_map/ppermute | solution.py:29
  354.1 1.9 collective-permute-start.5
  (190 shorter events, 41.5 us)
Async XLA Ops:
  0.0 9.0 %copy-start.2 = (bf16[60,96,192]{2,1,0:T(8,128)(2,1)S(1)}, bf16[60,96,192]{2,1,0:T(8,128)(2,1)}, u32[]{:S(2)}) copy-start(bf16[60,96,192]{2,1,0:T(8,128)(2,1)} %param.7) | copy-start | bytes 6635524
  3.2 13.9 %copy-start.14 = (s32[3,8]{1,0:T(4,128)S(1)}, s32[3,8]{1,0:T(4,128)}, u32[]{:S(2)}) copy-start(s32[3,8]{1,0:T(4,128)} %param.10) | copy-start | bytes 292
  3.2 13.9 %copy-start.17 = (s32[8]{0:T(128)S(1)}, s32[8]{0:T(128)}, u32[]{:S(2)}) copy-start(s32[8]{0:T(128)} %param.9) | copy-start | bytes 100
  3.2 14.4 %copy-start.11 = (f32[3]{0:T(128)S(1)}, f32[3]{0:T(128)}, u32[]{:S(2)}) copy-start(f32[3]{0:T(128)} %constant.178.clone) | copy-start | bytes 40
  3.2 16.3 %collective-permute-start.2 = (bf16[22,96,192]{2,1,0:T(8,128)(2,1)}, bf16[22,96,192]{2,1,0:T(8,128)(2,1)S(1)}, u32[]{:S(2)}, u32[]{:S(2)}) collective-permute-start(bf16[22,96,192]{2,1,0:T(8,128)(2,1)} %get-tuple-element.66), channel_id=1, source_target_pairs={{0,1},{1,2},{2,3},{3,4},{4,5},{5,6},{6,7},{7,8},{8,9},{9,10},{10,1... | collective-permute-start | bytes 2433032 | tf_op jit(solution)/shard_map/ppermute | solution.py:26
  7.1 17.8 %collective-permute-start.3 = (bf16[22,96,192]{2,1,0:T(8,128)(2,1)}, bf16[22,96,192]{2,1,0:T(8,128)(2,1)}, u32[]{:S(2)}, u32[]{:S(2)}) collective-permute-start(bf16[22,96,192]{2,1,0:T(8,128)(2,1)} %get-tuple-element.67), channel_id=1, source_target_pairs={{1,0},{2,1},{3,2},{4,3},{5,4},{6,5},{7,6},{8,7},{9,8},{10,9},{11,1... | collective-permute-start | bytes 2433032 | tf_op jit(solution)/shard_map/ppermute | solution.py:29
  10.6 185.2 %collective-permute-start = (bf16[24,96,192]{2,1,0:T(8,128)(2,1)}, bf16[24,96,192]{2,1,0:T(8,128)(2,1)S(1)}, u32[]{:S(2)}, u32[]{:S(2)}) collective-permute-start(bf16[24,96,192]{2,1,0:T(8,128)(2,1)} %get-tuple-element.68), channel_id=1, source_target_pairs={{0,1},{1,2},{2,3},{3,4},{4,5},{5,6},{6,7},{7,8},{8,9},{9,10},{10,1... | collective-permute-start | bytes 2654216 | tf_op jit(solution)/shard_map/ppermute | solution.py:26
  15.1 180.7 %collective-permute-start.1 = (bf16[24,96,192]{2,1,0:T(8,128)(2,1)}, bf16[24,96,192]{2,1,0:T(8,128)(2,1)}, u32[]{:S(2)}, u32[]{:S(2)}) collective-permute-start(bf16[24,96,192]{2,1,0:T(8,128)(2,1)} %get-tuple-element.69), channel_id=1, source_target_pairs={{1,0},{2,1},{3,2},{4,3},{5,4},{6,5},{7,6},{8,7},{9,8},{10,9},{11,1... | collective-permute-start | bytes 2654216 | tf_op jit(solution)/shard_map/ppermute | solution.py:29
  87.7 4.3 %copy-start = (bf16[8,50,50,50]{3,2,1,0:T(8,128)(2,1)S(1)}, bf16[8,50,50,50]{3,2,1,0:T(8,128)(2,1)}, u32[]{:S(2)}) copy-start(bf16[8,50,50,50]{3,2,1,0:T(8,128)(2,1)} %get-tuple-element.22) | copy-start | bytes 6000004
  261.9 4.9 %copy-start.1 = (f32[8,48,2304]{2,1,0:T(8,128)S(1)}, f32[8,48,2304]{2,1,0:T(8,128)}, u32[]{:S(2)}) copy-start(f32[8,48,2304]{2,1,0:T(8,128)} %reshape.199) | copy-start | bytes 10616836
  266.7 1.6 copy-start.3
  318.7 8.8 %copy-start.8 = (f32[48,8]{1,0:T(8,128)S(1)}, f32[48,8]{1,0:T(8,128)}, u32[]{:S(2)}) copy-start(f32[48,8]{1,0:T(8,128)} %gather_fusion.25) | copy-start | bytes 4612
  318.7 9.0 %copy-start.6 = (f32[48,8]{1,0:T(8,128)S(1)}, f32[48,8]{1,0:T(8,128)}, u32[]{:S(2)}) copy-start(f32[48,8]{1,0:T(8,128)} %gather_fusion.24) | copy-start | bytes 4612
  319.7 8.2 %copy-start.7 = (f32[48,8]{1,0:T(8,128)S(1)}, f32[48,8]{1,0:T(8,128)}, u32[]{:S(2)}) copy-start(f32[48,8]{1,0:T(8,128)} %gather_fusion.7) | copy-start | bytes 4612
  320.6 7.4 %copy-start.5 = (f32[48,8]{1,0:T(8,128)S(1)}, f32[48,8]{1,0:T(8,128)}, u32[]{:S(2)}) copy-start(f32[48,8]{1,0:T(8,128)} %gather_fusion.22) | copy-start | bytes 4612
  320.6 7.5 %copy-start.4 = (f32[48,8]{1,0:T(8,128)S(1)}, f32[48,8]{1,0:T(8,128)}, u32[]{:S(2)}) copy-start(f32[48,8]{1,0:T(8,128)} %gather_fusion.6) | copy-start | bytes 4612
  321.6 5.8 %copy-start.9 = (f32[48,8]{1,0:T(8,128)S(1)}, f32[48,8]{1,0:T(8,128)}, u32[]{:S(2)}) copy-start(f32[48,8]{1,0:T(8,128)} %gather_fusion.26) | copy-start | bytes 4612
  321.6 5.9 %copy-start.10 = (f32[48,8]{1,0:T(8,128)S(1)}, f32[48,8]{1,0:T(8,128)}, u32[]{:S(2)}) copy-start(f32[48,8]{1,0:T(8,128)} %gather_fusion.8) | copy-start | bytes 4612
  321.6 8.7 %copy-start.15 = (f32[8]{0:T(128)S(1)}, f32[8]{0:T(128)}, u32[]{:S(2)}) copy-start(f32[8]{0:T(128)} %get-tuple-element.43) | copy-start | bytes 100
  321.6 8.7 %copy-start.16 = (f32[8]{0:T(128)S(1)}, f32[8]{0:T(128)}, u32[]{:S(2)}) copy-start(f32[8]{0:T(128)} %multiply_reduce_fusion.1) | copy-start | bytes 100
  321.6 8.8 %copy-start.12 = (f32[27]{0:T(128)S(1)}, f32[27]{0:T(128)}, u32[]{:S(2)}) copy-start(f32[27]{0:T(128)} %mul.118) | copy-start | bytes 328
  321.6 8.8 %copy-start.13 = (f32[27]{0:T(128)S(1)}, f32[27]{0:T(128)}, u32[]{:S(2)}) copy-start(f32[27]{0:T(128)} %mul.114) | copy-start | bytes 328
  331.7 24.6 %collective-permute-start.4 = (f32[3,1,128]{2,1,0:T(1,128)S(1)}, f32[3,1,128]{2,1,0:T(1,128)S(1)}, u32[]{:S(2)}, u32[]{:S(2)}) collective-permute-start(f32[3,1,128]{2,1,0:T(1,128)S(1)} %copy.252), channel_id=1, source_target_pairs={{1,0},{2,1},{3,2},{4,3},{5,4},{6,5},{7,6},{8,7},{9,8},{10,9},{11,1... | collective-permute-start | bytes 4616 | tf_op jit(solution)/shard_map/ppermute | solution.py:29
  354.1 3.1 collective-permute-start.5
where the time goes:
time: 365 us; the launch traced here: 358 us
  local copies, waits for them, and re-layouts  249 us (68%)
  other arithmetic  47.6 us (13%)
  starting transfers between devices  36.4 us (10%)
  matrix products  18.6 us (5%)
  waiting for transfers between devices  6.36 us (2%)
    gather x48, local copies, waits for them, and re-layouts  87.5 us
    reshape x9, local copies, waits for them, and re-layouts, correlate(): second_centred[:, :, lag_z:lag_z + W, lag_x:lag_x + W]  83.8 us
    gather x27, local copies, waits for them, and re-layouts, correlate(): jnp.diagonal(product, offset=lag_y, axis1=1, axis2=2)  33.5 us
    concatenate x2, other arithmetic, padded_2(): block = jnp.concatenate([low, block, high], axis=dim)  29.7 us
    ppermute x3, starting transfers between devices, padded_2(): lax.ppermute(lax.slice_in_dim(block, 0, width, axis=dim), axis, backward)  26.1 us
    dot_general x9, matrix products, correlate(): jnp.einsum('wyp,wqp->wyq', flat_first, shifted_piece, preferred_element_t...  18.6 us
    slice x1, local copies, waits for them, and re-layouts, correlate(): second_centred[:, :, lag_z:lag_z + W, lag_x:lag_x + W]  16.6 us
    ppermute x3, starting transfers between devices, padded_2(): lax.ppermute(lax.slice_in_dim(block, block.shape[dim] - width, None, axis...  10.3 us
  transfers between devices with their start and end apart: 6, of which 3 were waited for; matrix products, arithmetic and copies ran while one was open for 49% of the time, Pallas kernels for 0%

commit v1 on v0

v1 whole, which is shorter than its diff:
```python
import jax
import jax.numpy as jnp
from jax import lax
from jax.experimental import pallas as pl
from jax.experimental.pallas import tpu as pltpu
from jax.sharding import PartitionSpec as P

W = 48
STRIDE = 12
DYM = 3
GX = 16
GZX = 128
SHARP = 80.0
EPSILON = 1e-06

HALF = W // 2
BLOCK = W + 2
REACH = DYM + 1
LANES = 128
HOP = 64
CHUNK = 6
ROWS_A = 64
ROWS_B = 80
PAD_A = CHUNK
PAD_B = CHUNK + REACH
PIECES = 4
SLOT = 4


def window_of(s, own, win_ref, shift_ref, low_ref, high_ref):
    group = s // own
    idx = s - group * own

    def pick(mine, below, above):
        return jnp.where(group == 0, mine, jnp.where(group == 1, below, above))

    node = pick(win_ref[idx], low_ref[0, idx], high_ref[0, idx])
    dy = pick(shift_ref[0, idx], low_ref[1, idx], high_ref[1, idx])
    dz = pick(shift_ref[1, idx], low_ref[2, idx], high_ref[2, idx])
    dx = pick(shift_ref[2, idx], low_ref[3, idx], high_ref[3, idx])
    return group, node, dy, dz, dx


def correlate_kernel(
    win_ref, shift_ref, low_ref, high_ref, first_hbm, second_hbm, below_hbm, above_hbm,
    out_ref, raw_a, raw_b, fr_a, fr_b, acc, sum_a, sq_a, sum_b, sq_b, sem_a, sem_b, sem_h,
):
    own = win_ref.shape[0]
    planes, deep, along = first_hbm.shape
    tile_rows = planes // STRIDE
    device = lax.axis_index("span")
    last = lax.axis_size("span") - 1
    piece = planes // PIECES

    def copy_a(i):
        return pltpu.make_async_copy(
            first_hbm.at[pl.ds(i * piece, piece)], raw_a.at[pl.ds(i * piece, piece)], sem_a.at[i])

    def copy_b(i):
        return pltpu.make_async_copy(
            second_hbm.at[pl.ds(i * piece, piece)],
            raw_b.at[pl.ds(REACH + i * piece, piece)], sem_b.at[i])

    copy_below = pltpu.make_async_copy(below_hbm, raw_b.at[pl.ds(0, REACH)], sem_h.at[0])
    copy_above = pltpu.make_async_copy(above_hbm, raw_b.at[pl.ds(REACH + planes, REACH)], sem_h.at[1])
    for i in range(PIECES):
        copy_a(i).start()
    copy_below.start()
    for i in range(PIECES):
        copy_b(i).start()
    copy_above.start()

    zero_a = jnp.zeros((2, CHUNK, deep, LANES), jnp.bfloat16)
    fr_a[:, 0:PAD_A] = zero_a
    fr_a[:, PAD_A + planes:] = zero_a
    fr_b[:, 0:CHUNK] = zero_a
    fr_b[:, PAD_B + planes + REACH:] = zero_a
    out_ref[...] = jnp.zeros(out_ref.shape, jnp.float32)

    def frame_a(p, carry):
        v = raw_a[p]
        fr_a[0, p + PAD_A] = v[:, :LANES]
        fr_a[1, p + PAD_A] = v[:, HOP:]
        return carry

    def frame_b(p, carry):
        v = raw_b[p]
        fr_b[0, p + CHUNK] = v[:, :LANES]
        fr_b[1, p + CHUNK] = v[:, HOP:]
        return carry

    for i in range(PIECES):
        copy_a(i).wait()
        lax.fori_loop(i * piece, (i + 1) * piece, frame_a, 0)
    copy_below.wait()
    lax.fori_loop(0, REACH, frame_b, 0)
    for i in range(PIECES):
        copy_b(i).wait()
        lax.fori_loop(REACH + i * piece, REACH + (i + 1) * piece, frame_b, 0)
    copy_above.wait()
    lax.fori_loop(REACH + planes, 2 * REACH + planes, frame_b, 0)

    def slot(s, carry):
        group, node, dy, dz, dx = window_of(s, own, win_ref, shift_ref, low_ref, high_ref)
        row = node // GZX - device * tile_rows
        rest = node % GZX
        cy = STRIDE * row + STRIDE // 2
        cz = STRIDE * (rest // GX) + STRIDE // 2
        cx = STRIDE * (rest % GX) + STRIDE // 2
        start = jnp.maximum(cy - HALF, jnp.where(device == 0, -CHUNK, 0))
        stop = jnp.minimum(cy + HALF, jnp.where(device == last, planes + CHUNK, planes))
        wanted = (
            (group == 0)
            | ((group == 1) & (row < 0) & (row >= -tile_rows))
            | ((group == 2) & (row >= tile_rows) & (row < 2 * tile_rows))
        )
        count = jnp.where(wanted, jnp.maximum(stop - start, 0) // CHUNK, 0)

        @pl.when(count > 0)
        def _():
            z_a = pl.multiple_of(jnp.clip((cz - HALF) // 16 * 16, 0, deep - ROWS_A), 16)
            sz = cz + dz - HALF - 1
            z_b = pl.multiple_of(jnp.where(sz + BLOCK <= ROWS_B, 0, deep - ROWS_B), 16)
            sx = cx + dx - HALF - 1
            f_a = jnp.where(cx + HALF <= LANES, 0, 1)
            f_b = jnp.where(sx + BLOCK <= LANES, 0, 1)
            lane16 = lax.broadcasted_iota(jnp.int32, (16, LANES), 1)
            row16 = lax.broadcasted_iota(jnp.int32, (16, LANES), 0)
            source = lane16 + HOP * f_b - dx
            turns = []
            masks = []
            for lag in range(3):
                turns.append((dx + lag - 1 + HOP * (f_a - f_b) + 2 * LANES) % LANES)
                at = source - (lag - 1)
                inside = (at >= cx - HALF) & (at < cx + HALF) & (at >= 0) & (at < along)
                tile = jnp.where(inside, 1.0, 0.0).astype(jnp.bfloat16)
                masks.append(jnp.concatenate([tile] * (ROWS_A // 16), axis=0))
            at = source - (row16 - 1)
            inside = (at >= cx - HALF) & (at < cx + HALF) & (row16 < 3)
            ones = jnp.where(inside, 1.0, 0.0).astype(jnp.bfloat16)
            ones = jnp.concatenate([ones] * CHUNK, axis=1)

            acc[...] = jnp.zeros(acc.shape, jnp.float32)
            sum_a[...] = jnp.zeros(sum_a.shape, jnp.float32)
            sq_a[...] = jnp.zeros(sq_a.shape, jnp.float32)
            sum_b[...] = jnp.zeros(sum_b.shape, jnp.float32)
            sq_b[...] = jnp.zeros(sq_b.shape, jnp.float32)

            def chunk(c, inner):
                y = start + c * CHUNK
                a = [fr_a[f_a, y + PAD_A + p, pl.ds(z_a, ROWS_A), :] for p in range(CHUNK)]
                b = [
                    fr_b[f_b, y + dy - 1 + PAD_B + p, pl.ds(z_b, ROWS_B), :]
                    for p in range(CHUNK + 2)
                ]
                left = [
                    jnp.concatenate(
                        [pltpu.roll(v, turns[lag], 1) * masks[lag] for v in a], axis=1)
                    for lag in range(3)
                ]
                left = jnp.concatenate(left + [ones], axis=0)
                right = jnp.concatenate(
                    [jnp.concatenate(b[lag:lag + CHUNK], axis=1) for lag in range(3)], axis=0)
                acc[...] += lax.dot_general(
                    left, right, (((1,), (1,)), ((), ())), preferred_element_type=jnp.float32)
                wide = [v.astype(jnp.float32) for v in a]
                sum_a[...] += sum(wide)
                sq_a[...] += sum([v * v for v in wide])
                wide = [v.astype(jnp.float32) for v in b[1:-1]]
                sum_b[...] += sum(wide)
                sq_b[...] += sum([v * v for v in wide])
                return inner

            lax.fori_loop(0, count, chunk, 0)

            for has, at in (
                (start == cy - HALF, start + dy - 1 + PAD_B),
                (stop == cy + HALF, stop + dy + PAD_B),
            ):
                @pl.when(has)
                def _():
                    v = fr_b[f_b, at, pl.ds(z_b, ROWS_B), :].astype(jnp.float32)
                    sum_b[...] += v
                    sq_b[...] += v * v

            cols = 3 * ROWS_B
            col = lax.broadcasted_iota(jnp.int32, (ROWS_A, cols), 1)
            z_row = lax.broadcasted_iota(jnp.int32, (ROWS_A, cols), 0) + z_a
            col_lag = jnp.where(col >= ROWS_B, 1, 0) + jnp.where(col >= 2 * ROWS_B, 1, 0)
            z_col = col - col_lag * ROWS_B + z_b
            z_in = (z_row >= cz - HALF) & (z_row < cz + HALF)
            gap = jnp.where(z_in, z_col - z_row - dz, 99)
            z_one = z_col[0:3] - dz
            tops = []
            lows = []
            for lag_z in range(3):
                hit = gap == lag_z - 1
                for lag_x in range(3):
                    tops.append(jnp.sum(
                        jnp.where(hit, acc[lag_x * ROWS_A:(lag_x + 1) * ROWS_A, :], 0.0),
                        axis=0, keepdims=True))
                at = z_one - (lag_z - 1)
                hit = (at >= cz - HALF) & (at < cz + HALF)
                lows.append(jnp.where(hit, acc[3 * ROWS_A:3 * ROWS_A + 3, :], 0.0))
            stack = jnp.concatenate(tops + lows, axis=0)

            lane = lax.broadcasted_iota(jnp.int32, (ROWS_A, LANES), 1) + HOP * f_a
            deep_at = lax.broadcasted_iota(jnp.int32, (ROWS_A, LANES), 0) + z_a
            hit_a = (
                (lane >= cx - HALF) & (lane < cx + HALF)
                & (deep_at >= cz - HALF) & (deep_at < cz + HALF)
            )
            lane = lax.broadcasted_iota(jnp.int32, (ROWS_B, LANES), 1) + HOP * f_b
            deep_at = lax.broadcasted_iota(jnp.int32, (ROWS_B, LANES), 0) + z_b
            hit_b = (
                (lane >= sx) & (lane < sx + BLOCK) & (deep_at >= sz) & (deep_at < sz + BLOCK)
            )
            sums = [
                jnp.sum(jnp.where(hit, ref[...], 0.0), axis=0, keepdims=True)
                for hit, ref in ((hit_a, sum_a), (hit_a, sq_a), (hit_b, sum_b), (hit_b, sq_b))
            ]
            sums = jnp.sum(jnp.concatenate(sums, axis=0), axis=1, keepdims=True)
            lag_18 = col_lag[0:18]
            out_lane = lax.broadcasted_iota(jnp.int32, (18, LANES), 1) - SLOT * s
            total = jnp.zeros((18, LANES), jnp.float32)
            for lag_y in range(3):
                part = jnp.sum(jnp.where(lag_18 == lag_y, stack, 0.0), axis=1, keepdims=True)
                total = total + jnp.where(out_lane == lag_y, part, 0.0)
            out_ref[0:18] += total
            out_ref[18:22] += jnp.where(out_lane[0:4] == 0, sums, 0.0)

        return carry

    lax.fori_loop(0, 3 * own, slot, 0)


def update_kernel(win_ref, low_ref, high_ref, mine_ref, below_ref, above_ref, out_ref):
    own = win_ref.shape[0]
    tile_rows = out_ref.shape[1]
    device = lax.axis_index("span")
    span = SLOT * own
    mine = mine_ref[...]
    below = below_ref[...]
    above = above_ref[...]
    lane = lax.broadcasted_iota(jnp.int32, mine.shape, 1)
    total = mine
    total = total + jnp.where(
        lane < span,
        pltpu.roll(below, LANES - 2 * span, 1) + pltpu.roll(above, LANES - span, 1),
        jnp.where(
            lane < 2 * span, pltpu.roll(below, span, 1),
            jnp.where(lane < 3 * span, pltpu.roll(above, 2 * span, 1), 0.0)))

    def lead(v):
        return v + pltpu.roll(v, LANES - 1, 1) + pltpu.roll(v, LANES - 2, 1)

    def spread(v):
        return v + pltpu.roll(v, 1, 1) + pltpu.roll(v, 2, 1)

    lag_lane = lane % SLOT
    stats = spread(jnp.where(lag_lane[0:4] == 0, total[18:22], 0.0))
    voxels = float(W) ** 3
    block_voxels = float(BLOCK) ** 3
    mean_a = stats[0:1] / voxels
    energy_a = jnp.maximum(stats[1:2] / voxels - mean_a * mean_a, 0.0)
    mean_b = stats[2:3] / block_voxels
    energy_b = jnp.maximum(stats[3:4] / block_voxels - mean_b * mean_b, 0.0)
    normaliser = voxels * jnp.sqrt((energy_a + EPSILON) * (energy_b + EPSILON))
    scaled = SHARP * ((total[0:9] - mean_a * total[9:18]) / normaliser)
    used = lag_lane[0:9] < 3
    scaled = jnp.where(used, scaled, -1e30)
    top = jnp.max(scaled, axis=0, keepdims=True)
    top = jnp.maximum(top, jnp.maximum(pltpu.roll(top, LANES - 1, 1), pltpu.roll(top, LANES - 2, 1)))
    top = spread(jnp.where(lag_lane[0:1] == 0, top, 0.0))
    weights = jnp.where(used, jnp.exp(scaled - top), 0.0)
    lag_row = lax.broadcasted_iota(jnp.int32, weights.shape, 0)
    lag_z = (lag_row // 3 - 1).astype(jnp.float32)
    lag_x = (lag_row % 3 - 1).astype(jnp.float32)
    column = jnp.sum(weights, axis=0, keepdims=True)
    weight_sum = lead(column)
    along_y = lead(column * (lag_lane[0:1] - 1).astype(jnp.float32)) / weight_sum
    along_z = lead(jnp.sum(weights * lag_z, axis=0, keepdims=True)) / weight_sum
    along_x = lead(jnp.sum(weights * lag_x, axis=0, keepdims=True)) / weight_sum
    corrections = (along_y, along_z, along_x)

    grid_row = lax.broadcasted_iota(jnp.int32, (8, LANES), 0) - 1
    grid_lane = lax.broadcasted_iota(jnp.int32, (8, LANES), 1)
    fields = [jnp.zeros((8, LANES), jnp.float32) for _ in range(3)]
    for s in range(3 * own):
        ref = win_ref if s < own else (low_ref if s < 2 * own else high_ref)
        node = ref[s] if s < own else ref[0, s % own]
        row = node // GZX - device * tile_rows
        if s >= 2 * own:
            row = jnp.where(row == tile_rows, row, -9)
        elif s >= own:
            row = jnp.where(row == -1, row, -9)
        hit = (grid_row == row) & (grid_lane == node % GZX)
        for comp in range(3):
            fields[comp] = jnp.where(
                hit, corrections[comp][:, SLOT * s:SLOT * s + 1], fields[comp])
    lane_z = grid_lane // GX
    lane_x = grid_lane % GX
    for comp in range(3):
        field = fields[comp]
        near = jnp.where(lane_z >= 1, pltpu.roll(field, GX, 1), 0.0)
        near = near + jnp.where(lane_z < GZX // GX - 1, pltpu.roll(field, LANES - GX, 1), 0.0)
        near = near + jnp.where(lane_x >= 1, pltpu.roll(field, 1, 1), 0.0)
        near = near + jnp.where(lane_x < GX - 1, pltpu.roll(field, LANES - 1, 1), 0.0)
        near = near[1:1 + tile_rows] + field[0:tile_rows] + field[2:2 + tile_rows]
        out_ref[comp] = 0.4 * field[1:1 + tile_rows] + 0.1 * near


def shards(first, second, windows, shifts):
    planes, deep, along = first.shape
    own = windows.shape[0]
    count = lax.axis_size("span")
    upward = [(i, i + 1) for i in range(count - 1)]
    downward = [(i + 1, i) for i in range(count - 1)]
    plan = jnp.concatenate([windows[None], shifts], axis=0)
    low_plan = lax.ppermute(plan, "span", upward)
    high_plan = lax.ppermute(plan, "span", downward)
    below = lax.ppermute(second[planes - REACH:], "span", upward)
    above = lax.ppermute(second[:REACH], "span", downward)
    smem = pl.BlockSpec(memory_space=pltpu.SMEM)
    vmem = pl.BlockSpec(memory_space=pltpu.VMEM)
    hbm = pl.BlockSpec(memory_space=pl.ANY)
    sums = pl.pallas_call(
        correlate_kernel,
        out_shape=jax.ShapeDtypeStruct((24, LANES), jnp.float32),
        in_specs=[smem] * 4 + [hbm] * 4,
        out_specs=vmem,
        scratch_shapes=[
            pltpu.VMEM((planes, deep, along), jnp.bfloat16),
            pltpu.VMEM((planes + 2 * REACH, deep, along), jnp.bfloat16),
            pltpu.VMEM((2, planes + 2 * PAD_A, deep, LANES), jnp.bfloat16),
            pltpu.VMEM((2, planes + 2 * PAD_B, deep, LANES), jnp.bfloat16),
            pltpu.VMEM((3 * ROWS_A + 16, 3 * ROWS_B), jnp.float32),
            pltpu.VMEM((ROWS_A, LANES), jnp.float32),
            pltpu.VMEM((ROWS_A, LANES), jnp.float32),
            pltpu.VMEM((ROWS_B, LANES), jnp.float32),
            pltpu.VMEM((ROWS_B, LANES), jnp.float32),
            pltpu.SemaphoreType.DMA((PIECES,)),
            pltpu.SemaphoreType.DMA((PIECES,)),
            pltpu.SemaphoreType.DMA((2,)),
        ],
        compiler_params=pltpu.CompilerParams(vmem_limit_bytes=48 << 20),
        name="partial_sums",
    )(windows, shifts, low_plan, high_plan, first, second, below, above)
    below_sums = lax.ppermute(sums, "span", upward)
    above_sums = lax.ppermute(sums, "span", downward)
    return pl.pallas_call(
        update_kernel,
        out_shape=jax.ShapeDtypeStruct((3, planes // STRIDE, GZX), jnp.float32),
        in_specs=[smem] * 3 + [vmem] * 3,
        out_specs=vmem,
        name="smoothed_update",
    )(windows, low_plan, high_plan, sums, below_sums, above_sums)


def solution(mesh):
    in_specs = (
        P(("grp", "span"), None, None),
        P(("grp", "span"), None, None),
        P(("grp", "span")),
        P(None, ("grp", "span")),
    )
    out_specs = P(None, ("grp", "span"), None)
    return jax.shard_map(shards, mesh=mesh, in_specs=in_specs, out_specs=out_specs, check_vma=False)
```

time: 365 us -> 71.5 us (0.20)
  the two profiles are of different devices: /device:TPU:23 before, /device:TPU:16 now
where the time goes in v1:
time: 71.5 us; the launch traced here: 70.9 us
  Pallas kernels  37.9 us (53%)
  starting transfers between devices  18.2 us (25%)
  waiting for transfers between devices  7.83 us (11%)
  local copies, waits for them, and re-layouts  6.13 us (9%)
    pallas_call x1, Pallas kernels, shards(): pl.pallas_call(correlate_kernel, out_shape=jax.ShapeDtypeStruct((24, LANE...  35.7 us
    ppermute x1, starting transfers between devices, shards(): above_sums = lax.ppermute(sums, 'span', downward)  5.14 us
    ppermute x1, starting transfers between devices, shards(): high_plan = lax.ppermute(plan, 'span', downward)  4.53 us
    ppermute x1, waiting for transfers between devices, shards(): below_sums = lax.ppermute(sums, 'span', upward)  3.96 us
    ppermute x1, waiting for transfers between devices, shards(): low_plan = lax.ppermute(plan, 'span', upward)  3.85 us
    unnamed x16, local copies, waits for them, and re-layouts  3.78 us
    ppermute x1, starting transfers between devices, shards(): above = lax.ppermute(second[:REACH], 'span', downward)  2.75 us
    pallas_call x1, Pallas kernels, shards(): pl.pallas_call(update_kernel, out_shape=jax.ShapeDtypeStruct((3, planes /...  2.21 us
  transfers between devices with their start and end apart: 6, of which 2 were waited for; matrix products, arithmetic and copies ran while one was open for 1% of the time, Pallas kernels for 0%

profile of v1, /device:TPU:16, one launch (start us, length us, event | category | flops | bytes accessed | tf_op | source)
XLA Modules:
  0.0 70.9 jit_solution(7939625253407183307)
XLA Ops:
  0.0 1.0 %fusion = (bf16[4,96,192]{2,1,0:T(8,128)(2,1)S(1)}, bf16[4,96,192]{2,1,0:T(8,128)(2,1)S(1)}) fusion(bf16[60,96,192]{2,1,0:T(8,128)(2,1)} %second_hbm.1), kind=kLoop, calls=%fused_computation.1 | loop fusion | bytes 589824 | tf_op jit(solution)/shard_map/slice | solution.py:323
  1.1 2.8 %collective-permute-start.3 = (bf16[4,96,192]{2,1,0:T(8,128)(2,1)S(1)}, bf16[4,96,192]{2,1,0:T(8,128)(2,1)S(1)}, u32[]{:S(2)}, u32[]{:S(2)}) collective-permute-start(bf16[4,96,192]{2,1,0:T(8,128)(2,1)S(1)} %get-tuple-element.5), channel_id=1, source_target_pairs={{1,0},{2,1},{3,2},{4,3},{5,4},{6,5},{7,6},{8,7},{9,8},{10,9},{11,1... | collective-permute-start | bytes 442376 | tf_op jit(solution)/shard_map/ppermute | solution.py:323
  3.8 1.9 %collective-permute-start.2 = (bf16[4,96,192]{2,1,0:T(8,128)(2,1)S(1)}, bf16[4,96,192]{2,1,0:T(8,128)(2,1)S(1)}, u32[]{:S(2)}, u32[]{:S(2)}) collective-permute-start(bf16[4,96,192]{2,1,0:T(8,128)(2,1)S(1)} %get-tuple-element.6), channel_id=1, source_target_pairs={{0,1},{1,2},{2,3},{3,4},{4,5},{5,6},{6,7},{7,8},{8,9},{9,10},{10,1... | collective-permute-start | bytes 442376 | tf_op jit(solution)/shard_map/ppermute | solution.py:322
  5.7 0.7 pad_add_fusion
  6.4 4.5 %collective-permute-start.1 = (s32[4,8]{1,0:T(4,128)S(1)}, s32[4,8]{1,0:T(4,128)S(1)}, u32[]{:S(2)}, u32[]{:S(2)}) collective-permute-start(s32[4,8]{1,0:T(4,128)S(1)} %pad_add_fusion), channel_id=1, source_target_pairs={{1,0},{2,1},{3,2},{4,3},{5,4},{6,5},{7,6},{8,7},{9,8},{10,9},{11,1... | collective-permute-start | bytes 392 | tf_op jit(solution)/shard_map/ppermute | solution.py:321
  11.0 1.9 %collective-permute-start = (s32[4,8]{1,0:T(4,128)S(1)}, s32[4,8]{1,0:T(4,128)S(1)}, u32[]{:S(2)}, u32[]{:S(2)}) collective-permute-start(s32[4,8]{1,0:T(4,128)S(1)} %pad_add_fusion), channel_id=1, source_target_pairs={{0,1},{1,2},{2,3},{3,4},{4,5},{5,6},{6,7},{7,8},{8,9},{9,10},{10,1... | collective-permute-start | bytes 392 | tf_op jit(solution)/shard_map/ppermute | solution.py:320
  12.9 0.0 collective-permute-done.1.high_ref
  12.9 0.0 copy-start.3
  12.9 3.9 %collective-permute-done.low_ref = s32[4,8]{1,0:T(4,128)S(1)} collective-permute-done((s32[4,8]{1,0:T(4,128)S(1)}, s32[4,8]{1,0:T(4,128)S(1)}, u32[]{:S(2)}, u32[]{:S(2)}) %collective-permute-start) | collective-permute-done | bytes 160 | tf_op jit(solution)/shard_map/ppermute | solution.py:320
  16.8 0.0 copy-start.4
  16.8 0.0 collective-permute-done.3.above_hbm
  16.8 0.0 collective-permute-done.2.below_hbm
  16.8 0.0 copy-start
  16.8 1.8 %copy-done = bf16[60,96,192]{2,1,0:T(8,128)(2,1)S(1)} copy-done((bf16[60,96,192]{2,1,0:T(8,128)(2,1)S(1)}, bf16[60,96,192]{2,1,0:T(8,128)(2,1)}, u32[]{:S(2)}) %copy-start) | copy-done | bytes 2211864
  18.6 0.0 copy-start.2
  18.6 0.7 copy-done.2
  19.3 0.0 copy-start.5
  19.3 0.7 copy-done.5
  20.0 35.7 %partial_sums.1.mine_ref = f32[24,128]{1,0:T(8,128)S(1)} custom-call(s32[8]{0:T(128)S(1)} %copy-done.5, s32[3,8]{1,0:T(4,128)S(1)} %copy-done.2, s32[4,8]{1,0:T(4,128)S(1)} %collective-permute-done.low_ref, s32[4,8]{1,0:T(4,128)S(1)} %collective-permute-done.1.high_ref, bf16[60,96,192]{2,1,0:T(8,128)(2,1)S(1)} %copy-done, bf16[60,96,192]{2,1,0:T(8,128)(2,1)} %second_hbm.1, ...), custom_call_target="tpu_custom_call" | custom-call | tf_op jit(solution)/shard_map/partial_sums/pallas_call | solution.py:327
  55.6 0.0 copy-done.3
  55.6 0.0 copy-done.4
  55.7 0.0 copy-start.1
  55.7 5.1 %collective-permute-start.5 = (f32[24,128]{1,0:T(8,128)S(1)}, f32[24,128]{1,0:T(8,128)S(1)}, u32[]{:S(2)}, u32[]{:S(2)}) collective-permute-start(f32[24,128]{1,0:T(8,128)S(1)} %partial_sums.1.mine_ref), channel_id=1, source_target_pairs={{1,0},{2,1},{3,2},{4,3},{5,4},{6,5},{7,6},{8,7},{9,8},{10,9},{11,1... | collective-permute-start | bytes 36872 | tf_op jit(solution)/shard_map/ppermute | solution.py:350
  60.8 1.9 %collective-permute-start.4 = (f32[24,128]{1,0:T(8,128)S(1)}, f32[24,128]{1,0:T(8,128)S(1)}, u32[]{:S(2)}, u32[]{:S(2)}) collective-permute-start(f32[24,128]{1,0:T(8,128)S(1)} %partial_sums.1.mine_ref), channel_id=1, source_target_pairs={{0,1},{1,2},{2,3},{3,4},{4,5},{5,6},{6,7},{7,8},{8,9},{9,10},{10,1... | collective-permute-start | bytes 36872 | tf_op jit(solution)/shard_map/ppermute | solution.py:349
  62.7 0.0 collective-permute-done.5.above_ref
  62.8 0.0 copy-start.6
  62.8 4.0 %collective-permute-done.4.below_ref = f32[24,128]{1,0:T(8,128)S(1)} collective-permute-done((f32[24,128]{1,0:T(8,128)S(1)}, f32[24,128]{1,0:T(8,128)S(1)}, u32[]{:S(2)}, u32[]{:S(2)}) %collective-permute-start.4) | collective-permute-done | bytes 12320 | tf_op jit(solution)/shard_map/ppermute | solution.py:349
  66.7 0.0 copy-done.1
  66.7 0.0 copy-done.6
  66.7 0.0 copy-start.7
  66.7 0.6 copy-done.7
  67.3 2.2 %smoothed_update.1 = f32[3,5,128]{2,1,0:T(8,128)} custom-call(s32[8]{0:T(128)} %win_ref.3, s32[4,8]{1,0:T(4,128)} %copy-done.4, s32[4,8]{1,0:T(4,128)} %copy-done.3, f32[24,128]{1,0:T(8,128)} %copy-done.1, f32[24,128]{1,0:T(8,128)} %copy-done.7, f32[24,128]{1,0:T(8,128)} %copy-done.6), custom_call_target="tpu_custom_call" | custom-call | tf_op jit(solution)/shard_map/smoothed_update/pallas_call | solution.py:351
  69.5 1.3 %copy.5 = f32[3,5,128]{2,0,1:T(4,128)} copy(f32[3,5,128]{2,1,0:T(8,128)} %smoothed_update.1) | data formatting | bytes 15360 | tf_op jit(solution)/shard_map/smoothed_update/pallas_call | solution.py:351
Async XLA Ops:
  1.1 15.7 %collective-permute-start.3 = (bf16[4,96,192]{2,1,0:T(8,128)(2,1)S(1)}, bf16[4,96,192]{2,1,0:T(8,128)(2,1)S(1)}, u32[]{:S(2)}, u32[]{:S(2)}) collective-permute-start(bf16[4,96,192]{2,1,0:T(8,128)(2,1)S(1)} %get-tuple-element.5), channel_id=1, source_target_pairs={{1,0},{2,1},{3,2},{4,3},{5,4},{6,5},{7,6},{8,7},{9,8},{10,9},{11,1... | collective-permute-start | bytes 442376 | tf_op jit(solution)/shard_map/ppermute | solution.py:323
  3.8 13.0 %collective-permute-start.2 = (bf16[4,96,192]{2,1,0:T(8,128)(2,1)S(1)}, bf16[4,96,192]{2,1,0:T(8,128)(2,1)S(1)}, u32[]{:S(2)}, u32[]{:S(2)}) collective-permute-start(bf16[4,96,192]{2,1,0:T(8,128)(2,1)S(1)} %get-tuple-element.6), channel_id=1, source_target_pairs={{0,1},{1,2},{2,3},{3,4},{4,5},{5,6},{6,7},{7,8},{8,9},{9,10},{10,1... | collective-permute-start | bytes 442376 | tf_op jit(solution)/shard_map/ppermute | solution.py:322
  6.4 6.5 %collective-permute-start.1 = (s32[4,8]{1,0:T(4,128)S(1)}, s32[4,8]{1,0:T(4,128)S(1)}, u32[]{:S(2)}, u32[]{:S(2)}) collective-permute-start(s32[4,8]{1,0:T(4,128)S(1)} %pad_add_fusion), channel_id=1, source_target_pairs={{1,0},{2,1},{3,2},{4,3},{5,4},{6,5},{7,6},{8,7},{9,8},{10,9},{11,1... | collective-permute-start | bytes 392 | tf_op jit(solution)/shard_map/ppermute | solution.py:321
  11.0 5.8 %collective-permute-start = (s32[4,8]{1,0:T(4,128)S(1)}, s32[4,8]{1,0:T(4,128)S(1)}, u32[]{:S(2)}, u32[]{:S(2)}) collective-permute-start(s32[4,8]{1,0:T(4,128)S(1)} %pad_add_fusion), channel_id=1, source_target_pairs={{0,1},{1,2},{2,3},{3,4},{4,5},{5,6},{6,7},{7,8},{8,9},{9,10},{10,1... | collective-permute-start | bytes 392 | tf_op jit(solution)/shard_map/ppermute | solution.py:320
  12.9 42.7 %copy-start.3 = (s32[4,8]{1,0:T(4,128)}, s32[4,8]{1,0:T(4,128)S(1)}, u32[]{:S(2)}) copy-start(s32[4,8]{1,0:T(4,128)S(1)} %collective-permute-done.1.high_ref) | copy-start | bytes 388
  16.8 38.9 %copy-start.4 = (s32[4,8]{1,0:T(4,128)}, s32[4,8]{1,0:T(4,128)S(1)}, u32[]{:S(2)}) copy-start(s32[4,8]{1,0:T(4,128)S(1)} %collective-permute-done.low_ref) | copy-start | bytes 388
  16.8 1.8 %copy-start = (bf16[60,96,192]{2,1,0:T(8,128)(2,1)S(1)}, bf16[60,96,192]{2,1,0:T(8,128)(2,1)}, u32[]{:S(2)}) copy-start(bf16[60,96,192]{2,1,0:T(8,128)(2,1)} %first_hbm.1) | copy-start | bytes 6635524
  18.6 0.7 copy-start.2
  19.3 0.7 copy-start.5
  55.7 11.1 %copy-start.1 = (f32[24,128]{1,0:T(8,128)}, f32[24,128]{1,0:T(8,128)S(1)}, u32[]{:S(2)}) copy-start(f32[24,128]{1,0:T(8,128)S(1)} %partial_sums.1.mine_ref) | copy-start | bytes 36868
  55.7 7.1 %collective-permute-start.5 = (f32[24,128]{1,0:T(8,128)S(1)}, f32[24,128]{1,0:T(8,128)S(1)}, u32[]{:S(2)}, u32[]{:S(2)}) collective-permute-start(f32[24,128]{1,0:T(8,128)S(1)} %partial_sums.1.mine_ref), channel_id=1, source_target_pairs={{1,0},{2,1},{3,2},{4,3},{5,4},{6,5},{7,6},{8,7},{9,8},{10,9},{11,1... | collective-permute-start | bytes 36872 | tf_op jit(solution)/shard_map/ppermute | solution.py:350
  60.8 5.9 %collective-permute-start.4 = (f32[24,128]{1,0:T(8,128)S(1)}, f32[24,128]{1,0:T(8,128)S(1)}, u32[]{:S(2)}, u32[]{:S(2)}) collective-permute-start(f32[24,128]{1,0:T(8,128)S(1)} %partial_sums.1.mine_ref), channel_id=1, source_target_pairs={{0,1},{1,2},{2,3},{3,4},{4,5},{5,6},{6,7},{7,8},{8,9},{9,10},{10,1... | collective-permute-start | bytes 36872 | tf_op jit(solution)/shard_map/ppermute | solution.py:349
  62.8 4.0 %copy-start.6 = (f32[24,128]{1,0:T(8,128)}, f32[24,128]{1,0:T(8,128)S(1)}, u32[]{:S(2)}) copy-start(f32[24,128]{1,0:T(8,128)S(1)} %collective-permute-done.5.above_ref) | copy-start | bytes 36868
  66.7 0.6 copy-start.7

commit v2 on v1

v2 whole, which is shorter than its diff:
```python
import functools

import jax
import jax.numpy as jnp
from jax import lax
from jax.experimental import pallas as pl
from jax.experimental.pallas import tpu as pltpu
from jax.sharding import PartitionSpec as P

W = 48
STRIDE = 12
DYM = 3
GX = 16
GZX = 128
SHARP = 80.0
EPSILON = 1e-06

HALF = W // 2
BLOCK = W + 2
REACH = DYM + 1
LANES = 128
HOP = 64
CHUNK = 6
ROWS_A = 64
ROWS_B = 80
PAD_A = CHUNK
PAD_B = CHUNK + REACH
PIECES = 4
SLOT = 4
PLAN_ROWS = 16
FIELDS = 16
PAIR = 2


def send_kernel(win_ref, shift_ref, second_hbm, pair_ref, other_ref, sems):
    planes = second_hbm.shape[0]
    even = lax.axis_index("span") % 2 == 0
    top = planes - REACH

    def fetch(start, target, i):
        return pltpu.make_async_copy(
            second_hbm.at[pl.ds(start, REACH)], target.at[pl.ds(0, REACH)], sems.at[i])

    to_pair = fetch(jnp.where(even, top, 0), pair_ref, 0)
    to_other = fetch(jnp.where(even, 0, top), other_ref, 1)
    to_pair.start()
    to_other.start()
    node = win_ref[...]
    rows = jnp.concatenate([node // 256, node % 256, shift_ref[...]], axis=0)
    rows = rows.astype(jnp.float32).astype(jnp.bfloat16)
    for ref in (pair_ref, other_ref):
        ref[REACH, 0:PLAN_ROWS, :] = jnp.zeros((PLAN_ROWS, ref.shape[2]), jnp.bfloat16)
        ref[REACH, 0:rows.shape[0], 0:node.shape[1]] = rows
    to_pair.wait()
    to_other.wait()


def correlate_kernel(
    win_ref, shift_ref, first_hbm, second_hbm, pair_hbm, other_hbm,
    out_ref, raw_a, raw_b, fr_a, fr_b, acc, sum_a, sq_a, sum_b, sq_b, masks, plan_in, plan_int,
    plan, table, units, sem_a, sem_b, sem_h, sem_p,
):
    own = win_ref.shape[0]
    planes, deep, along = first_hbm.shape
    tile_rows = planes // STRIDE
    device = lax.axis_index("span")
    last = lax.axis_size("span") - 1
    even = device % 2 == 0
    piece = planes // PIECES

    def copy_a(i):
        return pltpu.make_async_copy(
            first_hbm.at[pl.ds(i * piece, piece)], raw_a.at[pl.ds(i * piece, piece)], sem_a.at[i])

    def copy_b(i):
        return pltpu.make_async_copy(
            second_hbm.at[pl.ds(i * piece, piece)],
            raw_b.at[pl.ds(REACH + i * piece, piece)], sem_b.at[i])

    low_at, high_at = 0, REACH + planes
    pair_at = jnp.where(even, high_at, low_at)
    other_at = jnp.where(even, low_at, high_at)
    pair_side = jnp.where(even, 1, 0)
    halo = [
        pltpu.make_async_copy(
            ref.at[pl.ds(0, REACH)], raw_b.at[pl.ds(at, REACH)], sem_h.at[i])
        for i, (ref, at) in enumerate(((pair_hbm, pair_at), (other_hbm, other_at)))
    ]
    plans = [
        pltpu.make_async_copy(
            ref.at[REACH, pl.ds(0, PLAN_ROWS)], plan_in.at[side], sem_p.at[i])
        for i, (ref, side) in enumerate(((pair_hbm, pair_side), (other_hbm, 1 - pair_side)))
    ]
    for c in plans:
        c.start()
    for i in range(PIECES):
        copy_a(i).start()
    for i in range(PIECES):
        copy_b(i).start()
    for c in halo:
        c.start()
    for c in plans:
        c.wait()
    plan_int[...] = plan_in[:, 0:8, 0:LANES].astype(jnp.float32).astype(jnp.int32)
    to_scalar = pltpu.make_async_copy(plan_int, plan, sem_p.at[2])
    to_scalar.start()

    @pl.when((device == 0) | (device == last))
    def _():
        zero = jnp.zeros((2, CHUNK, deep, LANES), jnp.bfloat16)
        fr_a[:, 0:PAD_A] = zero
        fr_a[:, PAD_A + planes:] = zero
        fr_b[:, 0:CHUNK] = zero
        fr_b[:, PAD_B + planes + REACH:] = zero

    out_ref[...] = jnp.zeros(out_ref.shape, jnp.float32)
    to_scalar.wait()

    def prepare(s, total):
        group = s // own
        idx = s - group * own
        side = jnp.maximum(group - 1, 0)
        mine = group == 0

        def pick(own_value, row):
            return jnp.where(mine, own_value, plan[side, row, idx])

        node = jnp.where(mine, win_ref[idx], plan[side, 0, idx] * 256 + plan[side, 1, idx])
        dy = pick(shift_ref[0, idx], 2)
        dz = pick(shift_ref[1, idx], 3)
        dx = pick(shift_ref[2, idx], 4)
        row = node // GZX - device * tile_rows
        rest = node % GZX
        cy = STRIDE * row + STRIDE // 2
        cz = STRIDE * (rest // GX) + STRIDE // 2
        cx = STRIDE * (rest % GX) + STRIDE // 2
        start = jnp.maximum(cy - HALF, jnp.where(device == 0, -CHUNK, 0))
        stop = jnp.minimum(cy + HALF, jnp.where(device == last, planes + CHUNK, planes))
        wanted = (
            mine
            | ((group == 1) & (row < 0) & (row >= -tile_rows))
            | ((group == 2) & (row >= tile_rows) & (row < 2 * tile_rows))
        )
        count = jnp.where(wanted, jnp.maximum(stop - start, 0) // CHUNK, 0)
        target = jnp.where(
            mine | ((group == 1) & (row == -1)) | ((group == 2) & (row == tile_rows)),
            (row + 1) * GZX + rest, -1)
        lane_out = lax.broadcasted_iota(jnp.int32, (1, LANES), 1)
        out_ref[22:23, :] = jnp.where(
            lane_out == SLOT * s, target.astype(jnp.float32), out_ref[22:23, :])
        table[s, 0] = count

        @pl.when(count > 0)
        def _():
            z_a = jnp.clip((cz - HALF) // 16 * 16, 0, deep - ROWS_A)
            sz = cz + dz - HALF - 1
            z_b = jnp.where(sz + BLOCK <= ROWS_B, 0, deep - ROWS_B)
            sx = cx + dx - HALF - 1
            f_a = jnp.where(cx + HALF <= LANES, 0, 1)
            f_b = jnp.where(sx + BLOCK <= LANES, 0, 1)
            for at, value in enumerate((f_a, z_a, f_b, z_b, dy, dz, dx, cy, cz, cx, start, stop)):
                table[s, at + 1] = value
            lane16 = lax.broadcasted_iota(jnp.int32, (16, LANES), 1)
            row16 = lax.broadcasted_iota(jnp.int32, (16, LANES), 0)
            source = lane16 + jnp.where(lane16 < HOP, LANES * f_b, 0) - dx
            for lag in range(3):
                at = source - (lag - 1)
                inside = (at >= cx - HALF) & (at < cx + HALF) & (at >= 0) & (at < along)
                masks[s, lag] = jnp.where(inside, 1.0, 0.0).astype(jnp.bfloat16)
            at = source - (row16 - 1)
            inside = (at >= cx - HALF) & (at < cx + HALF) & (row16 < 3)
            masks[s, 3] = jnp.where(inside, 1.0, 0.0).astype(jnp.bfloat16)
            for ref in (acc, sum_a, sq_a, sum_b, sq_b):
                ref[s] = jnp.zeros(ref.shape[1:], jnp.float32)

            def unit(c, at):
                units[0, at] = s
                units[1, at] = start + c * CHUNK
                return at + 1

            lax.fori_loop(0, count, unit, total)

        return total + count

    total = lax.fori_loop(0, 3 * own, prepare, 0)
    spare = 3 * own
    for at in range(FIELDS):
        table[spare, at] = 0
    for at in range(PAIR - 1):
        units[0, total + at] = spare
        units[1, total + at] = 0

    def frame(raw, fr, shift):
        def body(p, carry):
            v = raw[p]
            fr[0, p + shift] = v[:, :LANES]
            fr[1, p + shift] = jnp.concatenate([v[:, LANES:], v[:, HOP:LANES]], axis=1)
            return carry
        return body

    frame_a = frame(raw_a, fr_a, PAD_A)
    frame_b = frame(raw_b, fr_b, CHUNK)
    for i in range(PIECES):
        copy_a(i).wait()
        lax.fori_loop(i * piece, (i + 1) * piece, frame_a, 0, unroll=5)
    for i in range(PIECES):
        copy_b(i).wait()
        lax.fori_loop(REACH + i * piece, REACH + (i + 1) * piece, frame_b, 0, unroll=5)
    for c in halo:
        c.wait()
    lax.fori_loop(0, REACH, frame_b, 0, unroll=4)
    lax.fori_loop(REACH + planes, 2 * REACH + planes, frame_b, 0, unroll=4)

    def step(t, carry):
        for h in range(PAIR):
            s = units[0, PAIR * t + h]
            y = units[1, PAIR * t + h]
            f_a = table[s, 1]
            z_a = pl.multiple_of(table[s, 2], 16)
            f_b = table[s, 3]
            z_b = pl.multiple_of(table[s, 4], 16)
            dy = table[s, 5]
            dx = table[s, 7]
            a = [fr_a[f_a, y + PAD_A + p, pl.ds(z_a, ROWS_A), :] for p in range(CHUNK)]
            b = [
                fr_b[f_b, y + dy - 1 + PAD_B + p, pl.ds(z_b, ROWS_B), :]
                for p in range(CHUNK + 2)
            ]
            left = []
            for lag in range(3):
                mask = jnp.concatenate([masks[s, lag]] * (ROWS_A // 16), axis=0)
                turn = (dx + lag - 1 + LANES) % LANES
                left.append(jnp.concatenate(
                    [pltpu.roll(v, turn, 1) * mask for v in a], axis=1))
            left.append(jnp.concatenate([masks[s, 3]] * CHUNK, axis=1))
            left = jnp.concatenate(left, axis=0)
            right = jnp.concatenate(
                [jnp.concatenate(b[lag:lag + CHUNK], axis=1) for lag in range(3)], axis=0)
            acc[s] += lax.dot_general(
                left, right, (((1,), (1,)), ((), ())), preferred_element_type=jnp.float32)
            wide = [v.astype(jnp.float32) for v in a]
            sum_a[s] += sum(wide)
            sq_a[s] += sum([v * v for v in wide])
            wide = [v.astype(jnp.float32) for v in b[1:-1]]
            sum_b[s] += sum(wide)
            sq_b[s] += sum([v * v for v in wide])
        return carry

    lax.fori_loop(0, (total + PAIR - 1) // PAIR, step, 0)

    def finish(s, carry):
        @pl.when(table[s, 0] > 0)
        def _():
            f_a, z_a, f_b, z_b, dy, dz, dx, cy, cz, cx, start, stop = [
                table[s, at + 1] for at in range(12)]
            z_b = pl.multiple_of(z_b, 16)
            sz = cz + dz - HALF - 1
            sx = cx + dx - HALF - 1
            for has, at in (
                (start == cy - HALF, start + dy - 1 + PAD_B),
                (stop == cy + HALF, stop + dy + PAD_B),
            ):
                @pl.when(has)
                def _():
                    v = fr_b[f_b, at, pl.ds(z_b, ROWS_B), :].astype(jnp.float32)
                    sum_b[s] += v
                    sq_b[s] += v * v

            cols = 3 * ROWS_B
            col = lax.broadcasted_iota(jnp.int32, (ROWS_A, cols), 1)
            z_row = lax.broadcasted_iota(jnp.int32, (ROWS_A, cols), 0) + z_a
            col_lag = jnp.where(col >= ROWS_B, 1, 0) + jnp.where(col >= 2 * ROWS_B, 1, 0)
            z_col = col - col_lag * ROWS_B + z_b
            z_in = (z_row >= cz - HALF) & (z_row < cz + HALF)
            gap = jnp.where(z_in, z_col - z_row - dz, 99)
            z_one = z_col[0:3] - dz
            tops = []
            lows = []
            for lag_z in range(3):
                hit = gap == lag_z - 1
                for lag_x in range(3):
                    tops.append(jnp.sum(
                        jnp.where(hit, acc[s, lag_x * ROWS_A:(lag_x + 1) * ROWS_A, :], 0.0),
                        axis=0, keepdims=True))
                at = z_one - (lag_z - 1)
                hit = (at >= cz - HALF) & (at < cz + HALF)
                lows.append(jnp.where(hit, acc[s, 3 * ROWS_A:3 * ROWS_A + 3, :], 0.0))
            stack = jnp.concatenate(tops + lows, axis=0)

            def inside(rows, frame_at, x_from, x_count, z_at, z_from, z_count):
                lane = lax.broadcasted_iota(jnp.int32, (rows, LANES), 1)
                lane = lane + jnp.where(lane < HOP, LANES * frame_at, 0)
                z = lax.broadcasted_iota(jnp.int32, (rows, LANES), 0) + z_at
                return (
                    (lane >= x_from) & (lane < x_from + x_count)
                    & (z >= z_from) & (z < z_from + z_count)
                )

            hit_a = inside(ROWS_A, f_a, cx - HALF, W, z_a, cz - HALF, W)
            hit_b = inside(ROWS_B, f_b, sx, BLOCK, z_b, sz, BLOCK)
            sums = [
                jnp.sum(jnp.where(hit, ref[s], 0.0), axis=0, keepdims=True)
                for hit, ref in ((hit_a, sum_a), (hit_a, sq_a), (hit_b, sum_b), (hit_b, sq_b))
            ]
            sums = jnp.sum(jnp.concatenate(sums, axis=0), axis=1, keepdims=True)
            lag_18 = col_lag[0:18]
            out_lane = lax.broadcasted_iota(jnp.int32, (18, LANES), 1) - SLOT * s
            total = jnp.zeros((18, LANES), jnp.float32)
            for lag_y in range(3):
                part = jnp.sum(jnp.where(lag_18 == lag_y, stack, 0.0), axis=1, keepdims=True)
                total = total + jnp.where(out_lane == lag_y, part, 0.0)
            out_ref[0:18] += total
            out_ref[18:22] += jnp.where(out_lane[0:4] == 0, sums, 0.0)

        return carry

    lax.fori_loop(0, 3 * own, finish, 0)


def update_kernel(own, mine_ref, pair_ref, other_ref, out_ref):
    tile_rows = out_ref.shape[0]
    even = lax.axis_index("span") % 2 == 0
    mine = mine_ref[...]
    pair = pair_ref[...]
    other = other_ref[...]
    below = jnp.where(even, other, pair)
    above = jnp.where(even, pair, other)
    span = SLOT * own
    lane = lax.broadcasted_iota(jnp.int32, mine.shape, 1)
    total = mine
    total = total + jnp.where(
        lane < span,
        pltpu.roll(below, LANES - 2 * span, 1) + pltpu.roll(above, LANES - span, 1),
        jnp.where(
            lane < 2 * span, pltpu.roll(below, span, 1),
            jnp.where(lane < 3 * span, pltpu.roll(above, 2 * span, 1), 0.0)))

    def lead(v):
        return v + pltpu.roll(v, LANES - 1, 1) + pltpu.roll(v, LANES - 2, 1)

    def spread(v):
        return v + pltpu.roll(v, 1, 1) + pltpu.roll(v, 2, 1)

    lag_lane = lane % SLOT
    stats = spread(jnp.where(lag_lane[0:4] == 0, total[18:22], 0.0))
    voxels = float(W) ** 3
    block_voxels = float(BLOCK) ** 3
    mean_a = stats[0:1] / voxels
    energy_a = jnp.maximum(stats[1:2] / voxels - mean_a * mean_a, 0.0)
    mean_b = stats[2:3] / block_voxels
    energy_b = jnp.maximum(stats[3:4] / block_voxels - mean_b * mean_b, 0.0)
    normaliser = voxels * jnp.sqrt((energy_a + EPSILON) * (energy_b + EPSILON))
    scaled = SHARP * ((total[0:9] - mean_a * total[9:18]) / normaliser)
    used = lag_lane[0:9] < 3
    scaled = jnp.where(used, scaled, -1e30)
    top = jnp.max(scaled, axis=0, keepdims=True)
    top = jnp.maximum(top, jnp.maximum(pltpu.roll(top, LANES - 1, 1), pltpu.roll(top, LANES - 2, 1)))
    top = spread(jnp.where(lag_lane[0:1] == 0, top, 0.0))
    weights = jnp.where(used, jnp.exp(scaled - top), 0.0)
    lag_row = lax.broadcasted_iota(jnp.int32, weights.shape, 0)
    lag_z = (lag_row // 3 - 1).astype(jnp.float32)
    lag_x = (lag_row % 3 - 1).astype(jnp.float32)
    column = jnp.sum(weights, axis=0, keepdims=True)
    weight_sum = lead(column)
    along_y = lead(column * (lag_lane[0:1] - 1).astype(jnp.float32)) / weight_sum
    along_z = lead(jnp.sum(weights * lag_z, axis=0, keepdims=True)) / weight_sum
    along_x = lead(jnp.sum(weights * lag_x, axis=0, keepdims=True)) / weight_sum
    corrections = (along_y, along_z, along_x)

    grid_lane = lax.broadcasted_iota(jnp.int32, (8, LANES), 1)
    place = lax.broadcasted_iota(jnp.int32, (8, LANES), 0) * GZX + grid_lane
    target = mine[22:23].astype(jnp.int32)
    fields = [jnp.zeros((8, LANES), jnp.float32) for _ in range(3)]
    for s in range(3 * own):
        hit = place == target[:, SLOT * s:SLOT * s + 1]
        for comp in range(3):
            fields[comp] = jnp.where(
                hit, corrections[comp][:, SLOT * s:SLOT * s + 1], fields[comp])
    lane_z = grid_lane // GX
    lane_x = grid_lane % GX
    for comp in range(3):
        field = fields[comp]
        near = jnp.where(lane_z >= 1, pltpu.roll(field, GX, 1), 0.0)
        near = near + jnp.where(lane_z < GZX // GX - 1, pltpu.roll(field, LANES - GX, 1), 0.0)
        near = near + jnp.where(lane_x >= 1, pltpu.roll(field, 1, 1), 0.0)
        near = near + jnp.where(lane_x < GX - 1, pltpu.roll(field, LANES - 1, 1), 0.0)
        near = near[1:1 + tile_rows] + field[0:tile_rows] + field[2:2 + tile_rows]
        out_ref[:, comp, :] = 0.4 * field[1:1 + tile_rows] + 0.1 * near


def shards(first, second, windows, shifts):
    planes, deep, along = first.shape
    own = windows.shape[0]
    count = lax.axis_size("span")
    pairs = [(i, i ^ 1) for i in range(count)]
    others = [(i, i + 1) for i in range(1, count - 1, 2)]
    others = others + [(b, a) for a, b in others]
    smem = pl.BlockSpec(memory_space=pltpu.SMEM)
    vmem = pl.BlockSpec(memory_space=pltpu.VMEM)
    hbm = pl.BlockSpec(memory_space=pl.ANY)
    message = jax.ShapeDtypeStruct((REACH + 1, deep, along), second.dtype)
    to_pair, to_other = pl.pallas_call(
        send_kernel,
        out_shape=(message, message),
        in_specs=[vmem, vmem, hbm],
        out_specs=(vmem, vmem),
        scratch_shapes=[pltpu.SemaphoreType.DMA((2,))],
        name="planes_to_send",
    )(windows[None], shifts, second)
    to_other = lax.ppermute(to_other, "span", others)
    to_pair = lax.ppermute(to_pair, "span", pairs)
    sums = pl.pallas_call(
        correlate_kernel,
        out_shape=jax.ShapeDtypeStruct((24, LANES), jnp.float32),
        in_specs=[smem] * 2 + [hbm] * 4,
        out_specs=vmem,
        scratch_shapes=[
            pltpu.VMEM((planes, deep, along), jnp.bfloat16),
            pltpu.VMEM((planes + 2 * REACH, deep, along), jnp.bfloat16),
            pltpu.VMEM((2, planes + 2 * PAD_A, deep, LANES), jnp.bfloat16),
            pltpu.VMEM((2, planes + 2 * PAD_B, deep, LANES), jnp.bfloat16),
            pltpu.VMEM((3 * own + 1, 3 * ROWS_A + 16, 3 * ROWS_B), jnp.float32),
            pltpu.VMEM((3 * own + 1, ROWS_A, LANES), jnp.float32),
            pltpu.VMEM((3 * own + 1, ROWS_A, LANES), jnp.float32),
            pltpu.VMEM((3 * own + 1, ROWS_B, LANES), jnp.float32),
            pltpu.VMEM((3 * own + 1, ROWS_B, LANES), jnp.float32),
            pltpu.VMEM((3 * own + 1, 4, 16, LANES), jnp.bfloat16),
            pltpu.VMEM((2, PLAN_ROWS, along), jnp.bfloat16),
            pltpu.VMEM((2, 8, LANES), jnp.int32),
            pltpu.SMEM((2, 8, LANES), jnp.int32),
            pltpu.SMEM((3 * own + 1, FIELDS), jnp.int32),
            pltpu.SMEM((2, 3 * own * (W // CHUNK + 1) + PAIR), jnp.int32),
            pltpu.SemaphoreType.DMA((PIECES,)),
            pltpu.SemaphoreType.DMA((PIECES,)),
            pltpu.SemaphoreType.DMA((2,)),
            pltpu.SemaphoreType.DMA((3,)),
        ],
        compiler_params=pltpu.CompilerParams(vmem_limit_bytes=60 << 20),
        name="partial_sums",
    )(windows, shifts, first, second, to_pair, to_other)
    other_sums = lax.ppermute(sums, "span", others)
    pair_sums = lax.ppermute(sums, "span", pairs)
    field = pl.pallas_call(
        functools.partial(update_kernel, own),
        out_shape=jax.ShapeDtypeStruct((planes // STRIDE, 3, GZX), jnp.float32),
        in_specs=[vmem] * 3,
        out_specs=vmem,
        name="smoothed_update",
    )(sums, pair_sums, other_sums)
    return jnp.transpose(field, (1, 0, 2))


def solution(mesh):
    in_specs = (
        P(("grp", "span"), None, None),
        P(("grp", "span"), None, None),
        P(("grp", "span")),
        P(None, ("grp", "span")),
    )
    out_specs = P(None, ("grp", "span"), None)
    return jax.shard_map(shards, mesh=mesh, in_specs=in_specs, out_specs=out_specs, check_vma=False)
```

time: 71.5 us -> 50 us (0.70)
  the two profiles are of different devices: /device:TPU:16 before, /device:TPU:3 now
where the time goes in v2:
time: 50 us; the launch traced here: 49.7 us
  Pallas kernels  29.5 us (59%)
  starting transfers between devices  10.8 us (22%)
  waiting for transfers between devices  7.55 us (15%)
  local copies, waits for them, and re-layouts  1.88 us (4%)
    pallas_call x1, Pallas kernels, shards(): pl.pallas_call(correlate_kernel, out_shape=jax.ShapeDtypeStruct((24, LANE...  24.9 us
    ppermute x1, starting transfers between devices, shards(): other_sums = lax.ppermute(sums, 'span', others)  6.91 us
    ppermute x1, waiting for transfers between devices, shards(): to_other = lax.ppermute(to_other, 'span', others)  6.05 us
    ppermute x1, starting transfers between devices, shards(): to_other = lax.ppermute(to_other, 'span', others)  3.05 us
    pallas_call x1, Pallas kernels, shards(): pl.pallas_call(send_kernel, out_shape=(message, message), in_specs=[vmem,...  2.52 us
    pallas_call x1, Pallas kernels, shards(): pl.pallas_call(functools.partial(update_kernel, own), out_shape=jax.Shape...  2.07 us
    unnamed x8, local copies, waits for them, and re-layouts  1.88 us
    ppermute x1, waiting for transfers between devices, shards(): other_sums = lax.ppermute(sums, 'span', others)  1.5 us
  transfers between devices with their start and end apart: 4, of which 2 were waited for; matrix products, arithmetic and copies ran while one was open for 0% of the time, Pallas kernels for 0%

profile of v2, /device:TPU:3, one launch (start us, length us, event | category | flops | bytes accessed | tf_op | source)
XLA Modules:
  0.0 49.7 jit_solution(3428496280423635236)
XLA Ops:
  0.0 2.5 %planes_to_send.1 = (bf16[5,96,192]{2,1,0:T(8,128)(2,1)}, bf16[5,96,192]{2,1,0:T(8,128)(2,1)}) custom-call(s32[1,8]{1,0:T(1,128)} %bitcast.2, s32[3,8]{1,0:T(4,128)} %shift_ref.3, bf16[60,96,192]{2,1,0:T(8,128)(2,1)} %second_hbm.3), custom_call_target="tpu_custom_call" | custom-call | tf_op jit(solution)/shard_map/planes_to_send/pallas_call | solution.py:402
  2.5 0.7 %collective-permute-start = (bf16[5,96,192]{2,1,0:T(8,128)(2,1)}, bf16[5,96,192]{2,1,0:T(8,128)(2,1)S(1)}, u32[]{:S(2)}, u32[]{:S(2)}) collective-permute-start(bf16[5,96,192]{2,1,0:T(8,128)(2,1)} %get-tuple-element.7), channel_id=1, source_target_pairs={{0,1},{1,0},{2,3},{3,2},{4,5},{5,4},{6,7},{7,6},{8,9},{9,8},{10,11... | collective-permute-start | bytes 552968 | tf_op jit(solution)/shard_map/ppermute | solution.py:411
  3.3 3.0 %collective-permute-start.1 = (bf16[5,96,192]{2,1,0:T(8,128)(2,1)}, bf16[5,96,192]{2,1,0:T(8,128)(2,1)S(1)}, u32[]{:S(2)}, u32[]{:S(2)}) collective-permute-start(bf16[5,96,192]{2,1,0:T(8,128)(2,1)} %get-tuple-element.8), channel_id=1, source_target_pairs={{1,2},{3,4},{5,6},{7,8},{9,10},{11,12},{13,14},{2,1},{4,3},{6,5},{... | collective-permute-start | bytes 552968 | tf_op jit(solution)/shard_map/ppermute | solution.py:410
  6.3 0.0 collective-permute-done.pair_hbm
  6.3 0.0 copy-start
  6.3 6.0 %collective-permute-done.1.other_hbm = bf16[5,96,192]{2,1,0:T(8,128)(2,1)S(1)} collective-permute-done((bf16[5,96,192]{2,1,0:T(8,128)(2,1)}, bf16[5,96,192]{2,1,0:T(8,128)(2,1)S(1)}, u32[]{:S(2)}, u32[]{:S(2)}) %collective-permute-start.1) | collective-permute-done | bytes 184352 | tf_op jit(solution)/shard_map/ppermute | solution.py:410
  12.4 0.0 copy-done
  12.4 0.0 copy-start.1
  12.4 0.7 %copy-done.1 = bf16[5,96,192]{2,1,0:T(8,128)(2,1)} copy-done((bf16[5,96,192]{2,1,0:T(8,128)(2,1)}, bf16[5,96,192]{2,1,0:T(8,128)(2,1)S(1)}, u32[]{:S(2)}) %copy-start.1) | copy-done | bytes 184344
  13.1 24.9 %partial_sums.1.mine_ref = f32[24,128]{1,0:T(8,128)} custom-call(s32[8]{0:T(128)} %win_ref.1, s32[3,8]{1,0:T(4,128)} %shift_ref.3, bf16[60,96,192]{2,1,0:T(8,128)(2,1)} %first_hbm.1, bf16[60,96,192]{2,1,0:T(8,128)(2,1)} %second_hbm.3, bf16[5,96,192]{2,1,0:T(8,128)(2,1)} %copy-done, bf16[5,96,192]{2,1,0:T(8,128)(2,1)} %copy-done.1), custom_call_target="tpu_custom_call" | custom-call | tf_op jit(solution)/shard_map/partial_sums/pallas_call | solution.py:412
  38.0 6.9 %collective-permute-start.3 = (f32[24,128]{1,0:T(8,128)}, f32[24,128]{1,0:T(8,128)S(1)}, u32[]{:S(2)}, u32[]{:S(2)}) collective-permute-start(f32[24,128]{1,0:T(8,128)} %partial_sums.1.mine_ref), channel_id=1, source_target_pairs={{1,2},{3,4},{5,6},{7,8},{9,10},{11,12},{13,14},{2,1},{4,3},{6,5},{... | collective-permute-start | bytes 36872 | tf_op jit(solution)/shard_map/ppermute | solution.py:441
  44.9 0.1 collective-permute-start.2
  45.0 1.5 %collective-permute-done.3.other_ref = f32[24,128]{1,0:T(8,128)S(1)} collective-permute-done((f32[24,128]{1,0:T(8,128)}, f32[24,128]{1,0:T(8,128)S(1)}, u32[]{:S(2)}, u32[]{:S(2)}) %collective-permute-start.3) | collective-permute-done | bytes 12320 | tf_op jit(solution)/shard_map/ppermute | solution.py:441
  46.5 0.0 copy-start.2
  46.5 0.0 collective-permute-done.2.pair_ref
  46.5 0.6 %copy-done.2 = f32[24,128]{1,0:T(8,128)} copy-done((f32[24,128]{1,0:T(8,128)}, f32[24,128]{1,0:T(8,128)S(1)}, u32[]{:S(2)}) %copy-start.2) | copy-done | bytes 12312
  47.1 0.0 copy-start.3
  47.1 0.6 %copy-done.3 = f32[24,128]{1,0:T(8,128)} copy-done((f32[24,128]{1,0:T(8,128)}, f32[24,128]{1,0:T(8,128)S(1)}, u32[]{:S(2)}) %copy-start.3) | copy-done | bytes 12312
  47.7 2.1 %smoothed_update.1 = f32[5,3,128]{2,1,0:T(4,128)} custom-call(f32[24,128]{1,0:T(8,128)} %partial_sums.1.mine_ref, f32[24,128]{1,0:T(8,128)} %copy-done.3, f32[24,128]{1,0:T(8,128)} %copy-done.2), custom_call_target="tpu_custom_call" | custom-call | tf_op jit(solution)/shard_map/smoothed_update/pallas_call | solution.py:443
Async XLA Ops:
  2.5 3.8 %collective-permute-start = (bf16[5,96,192]{2,1,0:T(8,128)(2,1)}, bf16[5,96,192]{2,1,0:T(8,128)(2,1)S(1)}, u32[]{:S(2)}, u32[]{:S(2)}) collective-permute-start(bf16[5,96,192]{2,1,0:T(8,128)(2,1)} %get-tuple-element.7), channel_id=1, source_target_pairs={{0,1},{1,0},{2,3},{3,2},{4,5},{5,4},{6,7},{7,6},{8,9},{9,8},{10,11... | collective-permute-start | bytes 552968 | tf_op jit(solution)/shard_map/ppermute | solution.py:411
  3.3 9.1 %collective-permute-start.1 = (bf16[5,96,192]{2,1,0:T(8,128)(2,1)}, bf16[5,96,192]{2,1,0:T(8,128)(2,1)S(1)}, u32[]{:S(2)}, u32[]{:S(2)}) collective-permute-start(bf16[5,96,192]{2,1,0:T(8,128)(2,1)} %get-tuple-element.8), channel_id=1, source_target_pairs={{1,2},{3,4},{5,6},{7,8},{9,10},{11,12},{13,14},{2,1},{4,3},{6,5},{... | collective-permute-start | bytes 552968 | tf_op jit(solution)/shard_map/ppermute | solution.py:410
  6.3 6.1 %copy-start = (bf16[5,96,192]{2,1,0:T(8,128)(2,1)}, bf16[5,96,192]{2,1,0:T(8,128)(2,1)S(1)}, u32[]{:S(2)}) copy-start(bf16[5,96,192]{2,1,0:T(8,128)(2,1)S(1)} %collective-permute-done.pair_hbm) | copy-start | bytes 552964
  12.4 0.7 %copy-start.1 = (bf16[5,96,192]{2,1,0:T(8,128)(2,1)}, bf16[5,96,192]{2,1,0:T(8,128)(2,1)S(1)}, u32[]{:S(2)}) copy-start(bf16[5,96,192]{2,1,0:T(8,128)(2,1)S(1)} %collective-permute-done.1.other_hbm) | copy-start | bytes 552964
  38.0 8.5 %collective-permute-start.3 = (f32[24,128]{1,0:T(8,128)}, f32[24,128]{1,0:T(8,128)S(1)}, u32[]{:S(2)}, u32[]{:S(2)}) collective-permute-start(f32[24,128]{1,0:T(8,128)} %partial_sums.1.mine_ref), channel_id=1, source_target_pairs={{1,2},{3,4},{5,6},{7,8},{9,10},{11,12},{13,14},{2,1},{4,3},{6,5},{... | collective-permute-start | bytes 36872 | tf_op jit(solution)/shard_map/ppermute | solution.py:441
  44.9 1.6 %collective-permute-start.2 = (f32[24,128]{1,0:T(8,128)}, f32[24,128]{1,0:T(8,128)S(1)}, u32[]{:S(2)}, u32[]{:S(2)}) collective-permute-start(f32[24,128]{1,0:T(8,128)} %partial_sums.1.mine_ref), channel_id=1, source_target_pairs={{0,1},{1,0},{2,3},{3,2},{4,5},{5,4},{6,7},{7,6},{8,9},{9,8},{10,11... | collective-permute-start | bytes 36872 | tf_op jit(solution)/shard_map/ppermute | solution.py:442
  46.5 0.6 %copy-start.2 = (f32[24,128]{1,0:T(8,128)}, f32[24,128]{1,0:T(8,128)S(1)}, u32[]{:S(2)}) copy-start(f32[24,128]{1,0:T(8,128)S(1)} %collective-permute-done.3.other_ref) | copy-start | bytes 36868
  47.1 0.6 %copy-start.3 = (f32[24,128]{1,0:T(8,128)}, f32[24,128]{1,0:T(8,128)S(1)}, u32[]{:S(2)}) copy-start(f32[24,128]{1,0:T(8,128)S(1)} %collective-permute-done.2.pair_ref) | copy-start | bytes 36868

commit v3 on v2

--- a/solution.py
+++ b/solution.py
@@ -29,7 +29,9 @@
 SLOT = 4
 PLAN_ROWS = 16
 FIELDS = 16
-PAIR = 2
+PAIR = 4
+CLOSE = 2
+FAR = 4096
 
 
 def send_kernel(win_ref, shift_ref, second_hbm, pair_ref, other_ref, sems):
@@ -57,8 +59,8 @@
 
 def correlate_kernel(
     win_ref, shift_ref, first_hbm, second_hbm, pair_hbm, other_hbm,
-    out_ref, raw_a, raw_b, fr_a, fr_b, acc, sum_a, sq_a, sum_b, sq_b, masks, plan_in, plan_int,
-    plan, table, units, sem_a, sem_b, sem_h, sem_p,
+    out_ref, raw_a, raw_b, fr_a, fr_b, acc, sq_a, sq_b, masks, gap_base, plan_in,
+    plan_int, plan, table, units, active, sem_a, sem_b, sem_h, sem_p,
 ):
     own = win_ref.shape[0]
     planes, deep, along = first_hbm.shape
@@ -99,24 +101,24 @@
         copy_b(i).start()
     for c in halo:
         c.start()
-    for c in plans:
-        c.wait()
-    plan_int[...] = plan_in[:, 0:8, 0:LANES].astype(jnp.float32).astype(jnp.int32)
-    to_scalar = pltpu.make_async_copy(plan_int, plan, sem_p.at[2])
-    to_scalar.start()
 
     @pl.when((device == 0) | (device == last))
     def _():
-        zero = jnp.zeros((2, CHUNK, deep, LANES), jnp.bfloat16)
-        fr_a[:, 0:PAD_A] = zero
-        fr_a[:, PAD_A + planes:] = zero
-        fr_b[:, 0:CHUNK] = zero
-        fr_b[:, PAD_B + planes + REACH:] = zero
+        zero = jnp.zeros((2, 2, CHUNK, deep, LANES), jnp.bfloat16)
+        fr_a[:, :, 0:PAD_A] = zero
+        fr_a[:, :, PAD_A + planes:] = zero
+        fr_b[:, :, 0:CHUNK] = zero
+        fr_b[:, :, PAD_B + planes + REACH:] = zero
 
     out_ref[...] = jnp.zeros(out_ref.shape, jnp.float32)
-    to_scalar.wait()
-
-    def prepare(s, total):
+    col = lax.broadcasted_iota(jnp.int32, gap_base.shape, 1)
+    col_lag = jnp.where(col >= ROWS_B, 1, 0) + jnp.where(col >= 2 * ROWS_B, 1, 0)
+    gap_base[...] = jnp.where(
+        col < 3 * ROWS_B,
+        col - col_lag * ROWS_B - lax.broadcasted_iota(jnp.int32, gap_base.shape, 0), FAR)
+
+    def prepare(s, carry):
+        total, alive = carry
         group = s // own
         idx = s - group * own
         side = jnp.maximum(group - 1, 0)
@@ -148,7 +150,6 @@
         lane_out = lax.broadcasted_iota(jnp.int32, (1, LANES), 1)
         out_ref[22:23, :] = jnp.where(
             lane_out == SLOT * s, target.astype(jnp.float32), out_ref[22:23, :])
-        table[s, 0] = count
 
         @pl.when(count > 0)
         def _():
@@ -158,163 +159,211 @@
             sx = cx + dx - HALF - 1
             f_a = jnp.where(cx + HALF <= LANES, 0, 1)
             f_b = jnp.where(sx + BLOCK <= LANES, 0, 1)
-            for at, value in enumerate((f_a, z_a, f_b, z_b, dy, dz, dx, cy, cz, cx, start, stop)):
-                table[s, at + 1] = value
+            has_first = jnp.where(start == cy - HALF, 1, 0)
+            has_last = jnp.where(stop == cy + HALF, 1, 0)
+            for at, value in enumerate(
+                (f_a, z_a, f_b, z_b, dy, dz, (dx + LANES) % LANES, cz,
+                 start + dy - 1 + PAD_B, stop + dy + PAD_B, has_first, has_last)
+            ):
+                table[s, at] = value
+            active[alive] = s
             lane16 = lax.broadcasted_iota(jnp.int32, (16, LANES), 1)
             row16 = lax.broadcasted_iota(jnp.int32, (16, LANES), 0)
-            source = lane16 + jnp.where(lane16 < HOP, LANES * f_b, 0) - dx
-            for lag in range(3):
-                at = source - (lag - 1)
-                inside = (at >= cx - HALF) & (at < cx + HALF) & (at >= 0) & (at < along)
-                masks[s, lag] = jnp.where(inside, 1.0, 0.0).astype(jnp.bfloat16)
-            at = source - (row16 - 1)
-            inside = (at >= cx - HALF) & (at < cx + HALF) & (row16 < 3)
-            masks[s, 3] = jnp.where(inside, 1.0, 0.0).astype(jnp.bfloat16)
-            for ref in (acc, sum_a, sq_a, sum_b, sq_b):
+            lag16 = row16 - 1
+            wide16 = row16 == 3
+            from16 = jnp.where(wide16, sx, cx + dx + lag16 - HALF)
+            upto16 = from16 + jnp.where(wide16, BLOCK, jnp.where(row16 < 3, W, 0))
+            for half in range(2):
+                lane = (lane16 + half * HOP) % LANES
+                low = jnp.where(lane < HOP, LANES, 0)
+                x_a = lane + low * f_a
+                x_b = lane + low * f_b
+                inside = (x_a >= cx - HALF) & (x_a < cx + HALF)
+                masks[s, half] = jnp.where(inside, 1.0, 0.0).astype(jnp.bfloat16)
+                inside = (x_b >= sx) & (x_b < sx + BLOCK)
+                masks[s, 2 + half] = jnp.where(inside, 1.0, 0.0).astype(jnp.bfloat16)
+                inside = (x_b >= from16) & (x_b < upto16)
+                masks[s, 4 + half] = jnp.where(inside, 1.0, 0.0).astype(jnp.bfloat16)
+            for ref in (acc, sq_a, sq_b):
                 ref[s] = jnp.zeros(ref.shape[1:], jnp.float32)
-
-            def unit(c, at):
-                units[0, at] = s
-                units[1, at] = start + c * CHUNK
-                return at + 1
-
-            lax.fori_loop(0, count, unit, total)
-
-        return total + count
-
-    total = lax.fori_loop(0, 3 * own, prepare, 0)
+            for c in range(W // CHUNK // 2):
+                both = jnp.where(2 * c + 1 < count, 1, 0)
+                units[total + c] = s + (start + 2 * CHUNK * c + 64) * 256 + both * 65536
+
+        return total + (count + 1) // 2, alive + jnp.where(count > 0, 1, 0)
+
+    carry = lax.fori_loop(0, own, prepare, (0, 0))
+    for c in plans:
+        c.wait()
+    plan_int[...] = plan_in[:, 0:8, 0:LANES].astype(jnp.float32).astype(jnp.int32)
+    to_scalar = pltpu.make_async_copy(plan_int, plan, sem_p.at[2])
+    to_scalar.start()
+
+    def frame(raw, fr, shift):
+        def body(p, carry):
+            v = raw[p]
+            low = v[:, :LANES]
+            high = jnp.concatenate([v[:, LANES:], v[:, HOP:LANES]], axis=1)
+            fr[0, 0, p + shift] = low
+            fr[0, 1, p + shift] = high
+            fr[1, 0, p + shift] = pltpu.roll(low, HOP, 1)
+            fr[1, 1, p + shift] = pltpu.roll(high, HOP, 1)
+            return carry
+        return body
+
+    frame_a = frame(raw_a, fr_a, PAD_A)
+    frame_b = frame(raw_b, fr_b, CHUNK)
+    for i in range(PIECES):
+        copy_a(i).wait()
+        lax.fori_loop(i * piece, (i + 1) * piece, frame_a, 0, unroll=piece)
+    to_scalar.wait()
+    total, alive = lax.fori_loop(own, 3 * own, prepare, carry)
     spare = 3 * own
     for at in range(FIELDS):
         table[spare, at] = 0
     for at in range(PAIR - 1):
-        units[0, total + at] = spare
-        units[1, total + at] = 0
-
-    def frame(raw, fr, shift):
-        def body(p, carry):
-            v = raw[p]
-            fr[0, p + shift] = v[:, :LANES]
-            fr[1, p + shift] = jnp.concatenate([v[:, LANES:], v[:, HOP:LANES]], axis=1)
-            return carry
-        return body
-
-    frame_a = frame(raw_a, fr_a, PAD_A)
-    frame_b = frame(raw_b, fr_b, CHUNK)
-    for i in range(PIECES):
-        copy_a(i).wait()
-        lax.fori_loop(i * piece, (i + 1) * piece, frame_a, 0, unroll=5)
+        units[total + at] = spare + 64 * 256
+    for at in range(CLOSE - 1):
+        active[alive + at] = spare
     for i in range(PIECES):
         copy_b(i).wait()
-        lax.fori_loop(REACH + i * piece, REACH + (i + 1) * piece, frame_b, 0, unroll=5)
+        lax.fori_loop(REACH + i * piece, REACH + (i + 1) * piece, frame_b, 0, unroll=piece)
     for c in halo:
         c.wait()
-    lax.fori_loop(0, REACH, frame_b, 0, unroll=4)
-    lax.fori_loop(REACH + planes, 2 * REACH + planes, frame_b, 0, unroll=4)
+    lax.fori_loop(0, REACH, frame_b, 0, unroll=REACH)
+    lax.fori_loop(REACH + planes, 2 * REACH + planes, frame_b, 0, unroll=REACH)
+
+    ones = jnp.where(
+        lax.broadcasted_iota(jnp.int32, (16, CHUNK * LANES), 0) == 0, 1.0, 0.0
+    ).astype(jnp.bfloat16)
 
     def step(t, carry):
         for h in range(PAIR):
-            s = units[0, PAIR * t + h]
-            y = units[1, PAIR * t + h]
-            f_a = table[s, 1]
-            z_a = pl.multiple_of(table[s, 2], 16)
-            f_b = table[s, 3]
-            z_b = pl.multiple_of(table[s, 4], 16)
-            dy = table[s, 5]
-            dx = table[s, 7]
-            a = [fr_a[f_a, y + PAD_A + p, pl.ds(z_a, ROWS_A), :] for p in range(CHUNK)]
+            code = units[PAIR * t + h]
+            s = code % 256
+            y = (code // 256) % 256 - 64
+            both = code // 65536
+            y_two = y + both * CHUNK
+            keep = both.astype(jnp.float32).astype(jnp.bfloat16)
+            f_a = table[s, 0]
+            z_a = pl.multiple_of(table[s, 1], 16)
+            f_b = table[s, 2]
+            z_b = pl.multiple_of(table[s, 3], 16)
+            dy = table[s, 4]
+            dx = table[s, 6]
+
+            def tall(at, rows, scale=None):
+                v = masks[s, at]
+                v = v if scale is None else v * scale
+                return jnp.concatenate([v] * (rows // 16), axis=0)
+
+            one_a, two_a = tall(0, ROWS_A), tall(1, ROWS_A, keep)
+            one_b, two_b = tall(2, ROWS_B), tall(3, ROWS_B, keep)
+            a = [
+                fr_a[0, f_a, y + PAD_A + p, pl.ds(z_a, ROWS_A), :] * one_a
+                + fr_a[1, f_a, y_two + PAD_A + p, pl.ds(z_a, ROWS_A), :] * two_a
+                for p in range(CHUNK)
+            ]
             b = [
-                fr_b[f_b, y + dy - 1 + PAD_B + p, pl.ds(z_b, ROWS_B), :]
+                fr_b[0, f_b, y + dy - 1 + PAD_B + p, pl.ds(z_b, ROWS_B), :] * one_b
+                + fr_b[1, f_b, y_two + dy - 1 + PAD_B + p, pl.ds(z_b, ROWS_B), :] * two_b
                 for p in range(CHUNK + 2)
             ]
-            left = []
-            for lag in range(3):
-                mask = jnp.concatenate([masks[s, lag]] * (ROWS_A // 16), axis=0)
-                turn = (dx + lag - 1 + LANES) % LANES
-                left.append(jnp.concatenate(
-                    [pltpu.roll(v, turn, 1) * mask for v in a], axis=1))
-            left.append(jnp.concatenate([masks[s, 3]] * CHUNK, axis=1))
+            left = [
+                jnp.concatenate(
+                    [pltpu.roll(v, (dx + lag - 1 + LANES) % LANES, 1) for v in a], axis=1)
+                for lag in range(3)
+            ]
+            left.append(jnp.concatenate([masks[s, 4] + masks[s, 5] * keep] * CHUNK, axis=1))
             left = jnp.concatenate(left, axis=0)
-            right = jnp.concatenate(
-                [jnp.concatenate(b[lag:lag + CHUNK], axis=1) for lag in range(3)], axis=0)
+            right = [jnp.concatenate(b[lag:lag + CHUNK], axis=1) for lag in range(3)]
+            right = jnp.concatenate(right + [ones], axis=0)
             acc[s] += lax.dot_general(
                 left, right, (((1,), (1,)), ((), ())), preferred_element_type=jnp.float32)
             wide = [v.astype(jnp.float32) for v in a]
-            sum_a[s] += sum(wide)
             sq_a[s] += sum([v * v for v in wide])
             wide = [v.astype(jnp.float32) for v in b[1:-1]]
-            sum_b[s] += sum(wide)
             sq_b[s] += sum([v * v for v in wide])
         return carry
 
     lax.fori_loop(0, (total + PAIR - 1) // PAIR, step, 0)
 
-    def finish(s, carry):
-        @pl.when(table[s, 0] > 0)
-        def _():
-            f_a, z_a, f_b, z_b, dy, dz, dx, cy, cz, cx, start, stop = [
-                table[s, at + 1] for at in range(12)]
+    cols = 2 * LANES
+    z_row = lax.broadcasted_iota(jnp.int32, (ROWS_A, LANES), 0)
+    col_one = lax.broadcasted_iota(jnp.int32, (1, cols), 1)
+    lag_one = jnp.where(col_one >= ROWS_B, 1, 0) + jnp.where(col_one >= 2 * ROWS_B, 1, 0)
+    lag_one = lag_one + jnp.where(col_one >= 3 * ROWS_B, 1, 0)
+    z_one = col_one - lag_one * ROWS_B
+    lag_18 = jnp.broadcast_to(lag_one, (18, cols))
+    lane_18 = lax.broadcasted_iota(jnp.int32, (18, LANES), 1)
+    lane_4 = lax.broadcasted_iota(jnp.int32, (4, LANES), 1)
+    z_b_row = lax.broadcasted_iota(jnp.int32, (ROWS_B, LANES), 0)
+
+    def finish(t, carry):
+        for h in range(CLOSE):
+            s = active[CLOSE * t + h]
+            f_a, z_a, f_b, z_b, dy, dz, dx, cz, at_first, at_last, has_first, has_last = [
+                table[s, at] for at in range(12)]
             z_b = pl.multiple_of(z_b, 16)
             sz = cz + dz - HALF - 1
-            sx = cx + dx - HALF - 1
-            for has, at in (
-                (start == cy - HALF, start + dy - 1 + PAD_B),
-                (stop == cy + HALF, stop + dy + PAD_B),
-            ):
-                @pl.when(has)
-                def _():
-                    v = fr_b[f_b, at, pl.ds(z_b, ROWS_B), :].astype(jnp.float32)
-                    sum_b[s] += v
-                    sq_b[s] += v * v
-
-            cols = 3 * ROWS_B
-            col = lax.broadcasted_iota(jnp.int32, (ROWS_A, cols), 1)
-            z_row = lax.broadcasted_iota(jnp.int32, (ROWS_A, cols), 0) + z_a
-            col_lag = jnp.where(col >= ROWS_B, 1, 0) + jnp.where(col >= 2 * ROWS_B, 1, 0)
-            z_col = col - col_lag * ROWS_B + z_b
-            z_in = (z_row >= cz - HALF) & (z_row < cz + HALF)
-            gap = jnp.where(z_in, z_col - z_row - dz, 99)
-            z_one = z_col[0:3] - dz
+            z_from = cz - HALF - z_a
+            z_in = (z_row >= z_from) & (z_row < z_from + W)
+            gap = [
+                jnp.where(z_in, gap_base[:, i * LANES:(i + 1) * LANES], FAR) for i in range(2)
+            ]
+            offset = z_a + dz - z_b
             tops = []
             lows = []
             for lag_z in range(3):
-                hit = gap == lag_z - 1
+                hit = [g == offset + lag_z - 1 for g in gap]
                 for lag_x in range(3):
-                    tops.append(jnp.sum(
-                        jnp.where(hit, acc[s, lag_x * ROWS_A:(lag_x + 1) * ROWS_A, :], 0.0),
-                        axis=0, keepdims=True))
-                at = z_one - (lag_z - 1)
-                hit = (at >= cz - HALF) & (at < cz + HALF)
-                lows.append(jnp.where(hit, acc[s, 3 * ROWS_A:3 * ROWS_A + 3, :], 0.0))
+                    part = [
+                        jnp.sum(jnp.where(
+                            hit[i],
+                            acc[s, lag_x * ROWS_A:(lag_x + 1) * ROWS_A,
+                                i * LANES:(i + 1) * LANES], 0.0), axis=0, keepdims=True)
+                        for i in range(2)
+                    ]
+                    tops.append(jnp.concatenate(part, axis=1))
+                low = cz - HALF + dz + lag_z - 1 - z_b
+                inside = (z_one >= low) & (z_one < low + W)
+                lows.append(jnp.where(inside, acc[s, 3 * ROWS_A:3 * ROWS_A + 3, :], 0.0))
             stack = jnp.concatenate(tops + lows, axis=0)
 
-            def inside(rows, frame_at, x_from, x_count, z_at, z_from, z_count):
-                lane = lax.broadcasted_iota(jnp.int32, (rows, LANES), 1)
-                lane = lane + jnp.where(lane < HOP, LANES * frame_at, 0)
-                z = lax.broadcasted_iota(jnp.int32, (rows, LANES), 0) + z_at
-                return (
-                    (lane >= x_from) & (lane < x_from + x_count)
-                    & (z >= z_from) & (z < z_from + z_count)
-                )
-
-            hit_a = inside(ROWS_A, f_a, cx - HALF, W, z_a, cz - HALF, W)
-            hit_b = inside(ROWS_B, f_b, sx, BLOCK, z_b, sz, BLOCK)
+            z_b_in = (z_b_row >= sz - z_b) & (z_b_row < sz - z_b + BLOCK)
+            mask = jnp.concatenate([masks[s, 2].astype(jnp.float32)] * (ROWS_B // 16), axis=0)
+            mask = jnp.where(z_b_in, mask, 0.0)
+            ends = [
+                fr_b[0, f_b, at, pl.ds(z_b, ROWS_B), :].astype(jnp.float32)
+                * (mask * has.astype(jnp.float32))
+                for at, has in ((at_first, has_first), (at_last, has_last))
+            ]
+            low = sz - z_b
+            inside = (z_one >= low) & (z_one < low + BLOCK) & (lag_one == 1)
+            row_b = jnp.where(inside, acc[s, 3 * ROWS_A + 3:3 * ROWS_A + 4, :], 0.0)
+            row_a = jnp.sum(jnp.where(
+                z_in & (z_row * 0 + lax.broadcasted_iota(
+                    jnp.int32, (ROWS_A, LANES), 1) == 3 * ROWS_B - LANES),
+                acc[s, ROWS_A:2 * ROWS_A, LANES:], 0.0), axis=0, keepdims=True)
             sums = [
-                jnp.sum(jnp.where(hit, ref[s], 0.0), axis=0, keepdims=True)
-                for hit, ref in ((hit_a, sum_a), (hit_a, sq_a), (hit_b, sum_b), (hit_b, sq_b))
+                row_a,
+                jnp.sum(jnp.where(z_in, sq_a[s], 0.0), axis=0, keepdims=True),
+                jnp.sum(ends[0] + ends[1], axis=0, keepdims=True)
+                + row_b[:, :LANES] + row_b[:, LANES:],
+                jnp.sum(
+                    jnp.where(z_b_in, sq_b[s], 0.0) + (ends[0] * ends[0] + ends[1] * ends[1]),
+                    axis=0, keepdims=True),
             ]
             sums = jnp.sum(jnp.concatenate(sums, axis=0), axis=1, keepdims=True)
-            lag_18 = col_lag[0:18]
-            out_lane = lax.broadcasted_iota(jnp.int32, (18, LANES), 1) - SLOT * s
-            total = jnp.zeros((18, LANES), jnp.float32)
+            total_18 = jnp.zeros((18, LANES), jnp.float32)
             for lag_y in range(3):
                 part = jnp.sum(jnp.where(lag_18 == lag_y, stack, 0.0), axis=1, keepdims=True)
-                total = total + jnp.where(out_lane == lag_y, part, 0.0)
-            out_ref[0:18] += total
-            out_ref[18:22] += jnp.where(out_lane[0:4] == 0, sums, 0.0)
-
+                total_18 = total_18 + jnp.where(lane_18 == SLOT * s + lag_y, part, 0.0)
+            out_ref[0:18] += total_18
+            out_ref[18:22] += jnp.where(lane_4 == SLOT * s, sums, 0.0)
         return carry
 
-    lax.fori_loop(0, 3 * own, finish, 0)
+    lax.fori_loop(0, (alive + CLOSE - 1) // CLOSE, finish, 0)
 
 
 def update_kernel(own, mine_ref, pair_ref, other_ref, out_ref):
@@ -417,19 +466,19 @@
         scratch_shapes=[
             pltpu.VMEM((planes, deep, along), jnp.bfloat16),
             pltpu.VMEM((planes + 2 * REACH, deep, along), jnp.bfloat16),
-            pltpu.VMEM((2, planes + 2 * PAD_A, deep, LANES), jnp.bfloat16),
-            pltpu.VMEM((2, planes + 2 * PAD_B, deep, LANES), jnp.bfloat16),
-            pltpu.VMEM((3 * own + 1, 3 * ROWS_A + 16, 3 * ROWS_B), jnp.float32),
-            pltpu.VMEM((3 * own + 1, ROWS_A, LANES), jnp.float32),
+            pltpu.VMEM((2, 2, planes + 2 * PAD_A, deep, LANES), jnp.bfloat16),
+            pltpu.VMEM((2, 2, planes + 2 * PAD_B, deep, LANES), jnp.bfloat16),
+            pltpu.VMEM((3 * own + 1, 3 * ROWS_A + 16, 2 * LANES), jnp.float32),
             pltpu.VMEM((3 * own + 1, ROWS_A, LANES), jnp.float32),
             pltpu.VMEM((3 * own + 1, ROWS_B, LANES), jnp.float32),
-            pltpu.VMEM((3 * own + 1, ROWS_B, LANES), jnp.float32),
-            pltpu.VMEM((3 * own + 1, 4, 16, LANES), jnp.bfloat16),
+            pltpu.VMEM((3 * own + 1, 6, 16, LANES), jnp.bfloat16),
+            pltpu.VMEM((ROWS_A, 2 * LANES), jnp.int32),
             pltpu.VMEM((2, PLAN_ROWS, along), jnp.bfloat16),
             pltpu.VMEM((2, 8, LANES), jnp.int32),
             pltpu.SMEM((2, 8, LANES), jnp.int32),
             pltpu.SMEM((3 * own + 1, FIELDS), jnp.int32),
-            pltpu.SMEM((2, 3 * own * (W // CHUNK + 1) + PAIR), jnp.int32),
+            pltpu.SMEM((3 * own * (W // CHUNK) + PAIR,), jnp.int32),
+            pltpu.SMEM((3 * own + CLOSE,), jnp.int32),
             pltpu.SemaphoreType.DMA((PIECES,)),
             pltpu.SemaphoreType.DMA((PIECES,)),
             pltpu.SemaphoreType.DMA((2,)),

time: 50 us -> 42.2 us (0.84)
  the two profiles are of different devices: /device:TPU:3 before, /device:TPU:1 now
where the time goes in v3:
time: 42.2 us; the launch traced here: 42.1 us
  Pallas kernels  22.4 us (53%)
  starting transfers between devices  10.2 us (24%)
  waiting for transfers between devices  7.55 us (18%)
  local copies, waits for them, and re-layouts  1.88 us (4%)
    pallas_call x1, Pallas kernels, shards(): pl.pallas_call(correlate_kernel, out_shape=jax.ShapeDtypeStruct((24, LANE...  17.8 us
    ppermute x1, waiting for transfers between devices, shards(): to_other = lax.ppermute(to_other, 'span', others)  6.05 us
    ppermute x1, starting transfers between devices, shards(): other_sums = lax.ppermute(sums, 'span', others)  5.5 us
    ppermute x1, starting transfers between devices, shards(): to_other = lax.ppermute(to_other, 'span', others)  4.49 us
    pallas_call x1, Pallas kernels, shards(): pl.pallas_call(send_kernel, out_shape=(message, message), in_specs=[vmem,...  2.52 us
    pallas_call x1, Pallas kernels, shards(): pl.pallas_call(functools.partial(update_kernel, own), out_shape=jax.Shape...  2.07 us
    unnamed x8, local copies, waits for them, and re-layouts  1.88 us
    ppermute x1, waiting for transfers between devices, shards(): other_sums = lax.ppermute(sums, 'span', others)  1.5 us
  transfers between devices with their start and end apart: 4, of which 2 were waited for; matrix products, arithmetic and copies ran while one was open for 0% of the time, Pallas kernels for 0%

profile of v3, /device:TPU:1, one launch (start us, length us, event | category | flops | bytes accessed | tf_op | source)
XLA Modules:
  0.0 42.1 jit_solution(10569521503547603877)
XLA Ops:
  0.0 2.5 %planes_to_send.1 = (bf16[5,96,192]{2,1,0:T(8,128)(2,1)}, bf16[5,96,192]{2,1,0:T(8,128)(2,1)}) custom-call(s32[1,8]{1,0:T(1,128)} %bitcast.2, s32[3,8]{1,0:T(4,128)} %shift_ref.3, bf16[60,96,192]{2,1,0:T(8,128)(2,1)} %second_hbm.3), custom_call_target="tpu_custom_call" | custom-call | tf_op jit(solution)/shard_map/planes_to_send/pallas_call | solution.py:451
  2.5 0.1 collective-permute-start
  2.7 4.5 %collective-permute-start.1 = (bf16[5,96,192]{2,1,0:T(8,128)(2,1)}, bf16[5,96,192]{2,1,0:T(8,128)(2,1)S(1)}, u32[]{:S(2)}, u32[]{:S(2)}) collective-permute-start(bf16[5,96,192]{2,1,0:T(8,128)(2,1)} %get-tuple-element.8), channel_id=1, source_target_pairs={{1,2},{3,4},{5,6},{7,8},{9,10},{11,12},{13,14},{2,1},{4,3},{6,5},{... | collective-permute-start | bytes 552968 | tf_op jit(solution)/shard_map/ppermute | solution.py:459
  7.2 0.0 collective-permute-done.pair_hbm
  7.2 0.0 copy-start
  7.2 6.0 %collective-permute-done.1.other_hbm = bf16[5,96,192]{2,1,0:T(8,128)(2,1)S(1)} collective-permute-done((bf16[5,96,192]{2,1,0:T(8,128)(2,1)}, bf16[5,96,192]{2,1,0:T(8,128)(2,1)S(1)}, u32[]{:S(2)}, u32[]{:S(2)}) %collective-permute-start.1) | collective-permute-done | bytes 184352 | tf_op jit(solution)/shard_map/ppermute | solution.py:459
  13.2 0.0 copy-done
  13.2 0.0 copy-start.1
  13.2 0.7 %copy-done.1 = bf16[5,96,192]{2,1,0:T(8,128)(2,1)} copy-done((bf16[5,96,192]{2,1,0:T(8,128)(2,1)}, bf16[5,96,192]{2,1,0:T(8,128)(2,1)S(1)}, u32[]{:S(2)}) %copy-start.1) | copy-done | bytes 184344
  13.9 17.8 %partial_sums.1.mine_ref = f32[24,128]{1,0:T(8,128)} custom-call(s32[8]{0:T(128)} %win_ref.1, s32[3,8]{1,0:T(4,128)} %shift_ref.3, bf16[60,96,192]{2,1,0:T(8,128)(2,1)} %first_hbm.1, bf16[60,96,192]{2,1,0:T(8,128)(2,1)} %second_hbm.3, bf16[5,96,192]{2,1,0:T(8,128)(2,1)} %copy-done, bf16[5,96,192]{2,1,0:T(8,128)(2,1)} %copy-done.1), custom_call_target="tpu_custom_call" | custom-call | tf_op jit(solution)/shard_map/partial_sums/pallas_call | solution.py:461
  31.8 5.5 %collective-permute-start.3 = (f32[24,128]{1,0:T(8,128)}, f32[24,128]{1,0:T(8,128)S(1)}, u32[]{:S(2)}, u32[]{:S(2)}) collective-permute-start(f32[24,128]{1,0:T(8,128)} %partial_sums.1.mine_ref), channel_id=1, source_target_pairs={{1,2},{3,4},{5,6},{7,8},{9,10},{11,12},{13,14},{2,1},{4,3},{6,5},{... | collective-permute-start | bytes 36872 | tf_op jit(solution)/shard_map/ppermute | solution.py:490
  37.3 0.1 collective-permute-start.2
  37.3 1.5 %collective-permute-done.3.other_ref = f32[24,128]{1,0:T(8,128)S(1)} collective-permute-done((f32[24,128]{1,0:T(8,128)}, f32[24,128]{1,0:T(8,128)S(1)}, u32[]{:S(2)}, u32[]{:S(2)}) %collective-permute-start.3) | collective-permute-done | bytes 12320 | tf_op jit(solution)/shard_map/ppermute | solution.py:490
  38.8 0.0 copy-start.2
  38.8 0.0 collective-permute-done.2.pair_ref
  38.8 0.6 %copy-done.2 = f32[24,128]{1,0:T(8,128)} copy-done((f32[24,128]{1,0:T(8,128)}, f32[24,128]{1,0:T(8,128)S(1)}, u32[]{:S(2)}) %copy-start.2) | copy-done | bytes 12312
  39.4 0.0 copy-start.3
  39.4 0.6 %copy-done.3 = f32[24,128]{1,0:T(8,128)} copy-done((f32[24,128]{1,0:T(8,128)}, f32[24,128]{1,0:T(8,128)S(1)}, u32[]{:S(2)}) %copy-start.3) | copy-done | bytes 12312
  40.0 2.1 %smoothed_update.1 = f32[5,3,128]{2,1,0:T(4,128)} custom-call(f32[24,128]{1,0:T(8,128)} %partial_sums.1.mine_ref, f32[24,128]{1,0:T(8,128)} %copy-done.3, f32[24,128]{1,0:T(8,128)} %copy-done.2), custom_call_target="tpu_custom_call" | custom-call | tf_op jit(solution)/shard_map/smoothed_update/pallas_call | solution.py:492
Async XLA Ops:
  2.5 4.6 %collective-permute-start = (bf16[5,96,192]{2,1,0:T(8,128)(2,1)}, bf16[5,96,192]{2,1,0:T(8,128)(2,1)S(1)}, u32[]{:S(2)}, u32[]{:S(2)}) collective-permute-start(bf16[5,96,192]{2,1,0:T(8,128)(2,1)} %get-tuple-element.7), channel_id=1, source_target_pairs={{0,1},{1,0},{2,3},{3,2},{4,5},{5,4},{6,7},{7,6},{8,9},{9,8},{10,11... | collective-permute-start | bytes 552968 | tf_op jit(solution)/shard_map/ppermute | solution.py:460
  2.7 10.6 %collective-permute-start.1 = (bf16[5,96,192]{2,1,0:T(8,128)(2,1)}, bf16[5,96,192]{2,1,0:T(8,128)(2,1)S(1)}, u32[]{:S(2)}, u32[]{:S(2)}) collective-permute-start(bf16[5,96,192]{2,1,0:T(8,128)(2,1)} %get-tuple-element.8), channel_id=1, source_target_pairs={{1,2},{3,4},{5,6},{7,8},{9,10},{11,12},{13,14},{2,1},{4,3},{6,5},{... | collective-permute-start | bytes 552968 | tf_op jit(solution)/shard_map/ppermute | solution.py:459
  7.2 6.1 %copy-start = (bf16[5,96,192]{2,1,0:T(8,128)(2,1)}, bf16[5,96,192]{2,1,0:T(8,128)(2,1)S(1)}, u32[]{:S(2)}) copy-start(bf16[5,96,192]{2,1,0:T(8,128)(2,1)S(1)} %collective-permute-done.pair_hbm) | copy-start | bytes 552964
  13.2 0.7 %copy-start.1 = (bf16[5,96,192]{2,1,0:T(8,128)(2,1)}, bf16[5,96,192]{2,1,0:T(8,128)(2,1)S(1)}, u32[]{:S(2)}) copy-start(bf16[5,96,192]{2,1,0:T(8,128)(2,1)S(1)} %collective-permute-done.1.other_hbm) | copy-start | bytes 552964
  31.8 7.1 %collective-permute-start.3 = (f32[24,128]{1,0:T(8,128)}, f32[24,128]{1,0:T(8,128)S(1)}, u32[]{:S(2)}, u32[]{:S(2)}) collective-permute-start(f32[24,128]{1,0:T(8,128)} %partial_sums.1.mine_ref), channel_id=1, source_target_pairs={{1,2},{3,4},{5,6},{7,8},{9,10},{11,12},{13,14},{2,1},{4,3},{6,5},{... | collective-permute-start | bytes 36872 | tf_op jit(solution)/shard_map/ppermute | solution.py:490
  37.3 1.6 %collective-permute-start.2 = (f32[24,128]{1,0:T(8,128)}, f32[24,128]{1,0:T(8,128)S(1)}, u32[]{:S(2)}, u32[]{:S(2)}) collective-permute-start(f32[24,128]{1,0:T(8,128)} %partial_sums.1.mine_ref), channel_id=1, source_target_pairs={{0,1},{1,0},{2,3},{3,2},{4,5},{5,4},{6,7},{7,6},{8,9},{9,8},{10,11... | collective-permute-start | bytes 36872 | tf_op jit(solution)/shard_map/ppermute | solution.py:491
  38.8 0.6 %copy-start.2 = (f32[24,128]{1,0:T(8,128)}, f32[24,128]{1,0:T(8,128)S(1)}, u32[]{:S(2)}) copy-start(f32[24,128]{1,0:T(8,128)S(1)} %collective-permute-done.3.other_ref) | copy-start | bytes 36868
  39.4 0.6 %copy-start.3 = (f32[24,128]{1,0:T(8,128)}, f32[24,128]{1,0:T(8,128)S(1)}, u32[]{:S(2)}) copy-start(f32[24,128]{1,0:T(8,128)S(1)} %collective-permute-done.2.pair_ref) | copy-start | bytes 36868

commit v4 on v3

v4 whole, which is shorter than its diff:
```python
import functools

import jax
import jax.numpy as jnp
from jax import lax
from jax.experimental import pallas as pl
from jax.experimental.pallas import tpu as pltpu
from jax.sharding import PartitionSpec as P

W = 48
STRIDE = 12
DYM = 3
GX = 16
GZX = 128
SHARP = 80.0
EPSILON = 1e-06

HALF = W // 2
BLOCK = W + 2
REACH = DYM + 1
LANES = 128
HOP = 64
CHUNK = 6
ROWS_A = 64
ROWS_B = 80
PAD_A = CHUNK
PAD_B = CHUNK + REACH
PIECES = 4
SLOT = 4
PLAN_ROWS = 16
FIELDS = 16
PAIR = 4
CLOSE = 2
FAR = 4096


def table_kernel(gap_ref):
    row = lax.broadcasted_iota(jnp.int32, gap_ref.shape, 0)
    col = lax.broadcasted_iota(jnp.int32, gap_ref.shape, 1)
    lag = jnp.where(col >= ROWS_B, 1, 0) + jnp.where(col >= 2 * ROWS_B, 1, 0)
    gap_ref[...] = jnp.where(col < 3 * ROWS_B, col - lag * ROWS_B - row, FAR)


def send_kernel(win_ref, shift_ref, gap_ref, second_hbm, pair_ref, other_ref, plan_ref, sems):
    planes, deep, along = second_hbm.shape
    even = lax.axis_index("span") % 2 == 0
    top = planes - REACH
    copies = [
        pltpu.make_async_copy(
            second_hbm.at[start + p], target.at[pl.ds(p * deep, deep)], sems.at[side, p])
        for side, (start, target) in enumerate((
            (jnp.where(even, top, 0), pair_ref), (jnp.where(even, 0, top), other_ref)))
        for p in range(REACH)
    ]
    for c in copies:
        c.start()
    node = win_ref[...]
    own = node.shape[1]
    plan_ref[...] = jnp.zeros(plan_ref.shape, jnp.int32)
    plan_ref[0:5, 0:own] = jnp.concatenate([node // 256, node % 256, shift_ref[...]], axis=0)
    plan = plan_ref[...].astype(jnp.float32).astype(jnp.bfloat16)
    base = REACH * deep
    for ref in (pair_ref, other_ref):
        ref[base:base + 8, 0:LANES] = plan
    for c in copies:
        c.wait()


def plan_of(plan, group, idx):
    node = plan[group, 0, idx] * 256 + plan[group, 1, idx]
    return node, plan[group, 2, idx], plan[group, 3, idx], plan[group, 4, idx]


def decode(plan, s, own, planes):
    device = lax.axis_index("span")
    last = lax.axis_size("span") - 1
    tile_rows = planes // STRIDE
    group = s // own
    node, dy, dz, dx = plan_of(plan, group, s - group * own)
    row = node // GZX - device * tile_rows
    rest = node % GZX
    cy = STRIDE * row + STRIDE // 2
    cz = STRIDE * (rest // GX) + STRIDE // 2
    cx = STRIDE * (rest % GX) + STRIDE // 2
    start = jnp.maximum(cy - HALF, jnp.where(device == 0, -CHUNK, 0))
    stop = jnp.minimum(cy + HALF, jnp.where(device == last, planes + CHUNK, planes))
    mine = group == 0
    wanted = (
        mine
        | ((group == 1) & (row < 0) & (row >= -tile_rows))
        | ((group == 2) & (row >= tile_rows) & (row < 2 * tile_rows))
    )
    stop = jnp.where(wanted, jnp.maximum(stop, start), start)
    target = jnp.where(
        mine | ((group == 1) & (row == -1)) | ((group == 2) & (row == tile_rows)),
        (row + 1) * GZX + rest, -1)
    return dy, dz, dx, cy, cz, cx, start, stop, target


def set_table(table, s, deep, dy, dz, dx, cy, cz, cx, start, stop):
    z_a = jnp.clip((cz - HALF) // 16 * 16, 0, deep - ROWS_A)
    sz = cz + dz - HALF - 1
    z_b = jnp.where(sz + BLOCK <= ROWS_B, 0, deep - ROWS_B)
    sx = cx + dx - HALF - 1
    f_a = jnp.where(cx + HALF <= LANES, 0, 1)
    f_b = jnp.where(sx + BLOCK <= LANES, 0, 1)
    has_first = jnp.where(start == cy - HALF, 1, 0)
    has_last = jnp.where(stop == cy + HALF, 1, 0)
    for at, value in enumerate(
        (f_a, z_a, f_b, z_b, dy, dz, (dx + LANES) % LANES, cz,
         start + dy - 1 + PAD_B, stop + dy + PAD_B, has_first, has_last)
    ):
        table[s, at] = value
    return f_a, f_b, sx


def set_masks(masks, s, f_a, f_b, sx, cx, dx):
    lane16 = lax.broadcasted_iota(jnp.int32, (16, LANES), 1)
    row16 = lax.broadcasted_iota(jnp.int32, (16, LANES), 0)
    wide16 = row16 == 3
    from16 = jnp.where(wide16, sx, cx + dx + row16 - 1 - HALF)
    upto16 = from16 + jnp.where(wide16, BLOCK, jnp.where(row16 < 3, W, 0))
    for half in range(2):
        lane = (lane16 + half * HOP) % LANES
        low = jnp.where(lane < HOP, LANES, 0)
        x_a = lane + low * f_a
        x_b = lane + low * f_b
        inside = (x_a >= cx - HALF) & (x_a < cx + HALF)
        masks[s, half] = jnp.where(inside, 1.0, 0.0).astype(jnp.bfloat16)
        inside = (x_b >= sx) & (x_b < sx + BLOCK)
        masks[s, 2 + half] = jnp.where(inside, 1.0, 0.0).astype(jnp.bfloat16)
        inside = (x_b >= from16) & (x_b < upto16)
        masks[s, 4 + half] = jnp.where(inside, 1.0, 0.0).astype(jnp.bfloat16)


def set_units(units, total, s, low, count, most):
    for c in range(most):
        both = jnp.where(2 * c + 1 < count, 1, 0)
        units[total + c] = s + (low + 2 * CHUNK * c + 64) * 256 + both * 65536
    return total + (count + 1) // 2


def frame(v, fr, at):
    low = v[:, :LANES]
    high = jnp.concatenate([v[:, LANES:], v[:, HOP:LANES]], axis=1)
    fr[0, 0, at] = low
    fr[0, 1, at] = high
    fr[1, 0, at] = pltpu.roll(low, HOP, 1)
    fr[1, 1, at] = pltpu.roll(high, HOP, 1)


def run_units(total, units, table, spare, fr_a, fr_b, acc, sq_a, sq_b, masks):
    for at in range(PAIR - 1):
        units[total + at] = spare + 64 * 256
    for at in range(FIELDS):
        table[spare, at] = 0
    ones = jnp.where(
        lax.broadcasted_iota(jnp.int32, (16, CHUNK * LANES), 0) == 0, 1.0, 0.0
    ).astype(jnp.bfloat16)

    def step(t, carry):
        for h in range(PAIR):
            code = units[PAIR * t + h]
            s = code % 256
            y = (code // 256) % 256 - 64
            both = code // 65536
            y_two = y + both * CHUNK
            keep = both.astype(jnp.float32).astype(jnp.bfloat16)
            f_a = table[s, 0]
            z_a = pl.multiple_of(table[s, 1], 16)
            f_b = table[s, 2]
            z_b = pl.multiple_of(table[s, 3], 16)
            dy = table[s, 4]
            dx = table[s, 6]

            def tall(at, rows, scale=None):
                v = masks[s, at]
                v = v if scale is None else v * scale
                return jnp.concatenate([v] * (rows // 16), axis=0)

            one_a, two_a = tall(0, ROWS_A), tall(1, ROWS_A, keep)
            one_b, two_b = tall(2, ROWS_B), tall(3, ROWS_B, keep)
            a = [
                fr_a[0, f_a, y + PAD_A + p, pl.ds(z_a, ROWS_A), :] * one_a
                + fr_a[1, f_a, y_two + PAD_A + p, pl.ds(z_a, ROWS_A), :] * two_a
                for p in range(CHUNK)
            ]
            b = [
                fr_b[0, f_b, y + dy - 1 + PAD_B + p, pl.ds(z_b, ROWS_B), :] * one_b
                + fr_b[1, f_b, y_two + dy - 1 + PAD_B + p, pl.ds(z_b, ROWS_B), :] * two_b
                for p in range(CHUNK + 2)
            ]
            left = [
                jnp.concatenate(
                    [pltpu.roll(v, (dx + lag - 1 + LANES) % LANES, 1) for v in a], axis=1)
                for lag in range(3)
            ]
            left.append(jnp.concatenate([masks[s, 4] + masks[s, 5] * keep] * CHUNK, axis=1))
            left = jnp.concatenate(left, axis=0)
            right = [jnp.concatenate(b[lag:lag + CHUNK], axis=1) for lag in range(3)]
            right = jnp.concatenate(right + [ones], axis=0)
            acc[s] += lax.dot_general(
                left, right, (((1,), (1,)), ((), ())), preferred_element_type=jnp.float32)
            wide = [v.astype(jnp.float32) for v in a]
            sq_a[s] += sum([v * v for v in wide])
            wide = [v.astype(jnp.float32) for v in b[1:-1]]
            sq_b[s] += sum([v * v for v in wide])
        return carry

    lax.fori_loop(0, (total + PAIR - 1) // PAIR, step, 0)


def inner_kernel(
    plan_ref, first_ref, second_ref, fr_a, fr_b, acc, sq_a, sq_b, masks,
    plan, table, units, sem_p,
):
    planes, deep, along = first_ref.shape
    own = (acc.shape[0] - 1) // 3
    device = lax.axis_index("span")
    last = lax.axis_size("span") - 1
    piece = planes // PIECES
    plan_copy = pltpu.make_async_copy(plan_ref, plan.at[0], sem_p)
    plan_copy.start()

    @pl.when((device == 0) | (device == last))
    def _():
        zero = jnp.zeros((2, 2, CHUNK, deep, LANES), jnp.bfloat16)
        fr_a[:, :, 0:PAD_A] = zero
        fr_a[:, :, PAD_A + planes:] = zero
        fr_b[:, :, 0:CHUNK] = zero
        fr_b[:, :, PAD_B + planes + REACH:] = zero

    for ref, fr, pad in ((first_ref, fr_a, PAD_A), (second_ref, fr_b, PAD_B)):
        def body(i, carry, ref=ref, fr=fr, pad=pad):
            for p in range(piece):
                at = i * piece + p
                frame(ref[at], fr, at + pad)
            return carry

        lax.fori_loop(0, PIECES, body, 0)

    plan_copy.wait()

    def prepare(s, total):
        dy, dz, dx, cy, cz, cx, start, stop, target = decode(plan, s, own, planes)
        f_a, f_b, sx = set_table(table, s, deep, dy, dz, dx, cy, cz, cx, start, stop)
        set_masks(masks, s, f_a, f_b, sx, cx, dx)
        for ref in (acc, sq_a, sq_b):
            ref[s] = jnp.zeros(ref.shape[1:], jnp.float32)
        low = jnp.maximum(start, CHUNK)
        count = (jnp.minimum(stop, planes - CHUNK) - low) // CHUNK
        return set_units(units, total, s, low, count, W // CHUNK // 2)

    total = lax.fori_loop(0, own, prepare, 0)
    run_units(total, units, table, 3 * own, fr_a, fr_b, acc, sq_a, sq_b, masks)


def outer_kernel(
    plan_ref, pair_ref, other_ref, gap_base, fr_a, fr_b_in, acc_in, sq_a_in, sq_b_in, masks_in,
    out_ref, fr_b, acc, sq_a, sq_b, masks,
    plan_int, plan, table, units, active, sem_p,
):
    deep = fr_a.shape[3]
    planes = fr_a.shape[2] - 2 * PAD_A
    own = (acc.shape[0] - 1) // 3
    even = lax.axis_index("span") % 2 == 0
    base = REACH * deep
    below_side = jnp.where(even, 2, 1)
    plan_int[0] = plan_ref[...]
    for ref, side in ((pair_ref, below_side), (other_ref, 3 - below_side)):
        plan_int[side] = ref[base:base + 8, 0:LANES].astype(jnp.float32).astype(jnp.int32)
    to_scalar = pltpu.make_async_copy(plan_int, plan, sem_p)
    to_scalar.start()
    low_at, high_at = CHUNK, PAD_B + planes
    pair_at = jnp.where(even, high_at, low_at)
    other_at = jnp.where(even, low_at, high_at)
    for p in range(REACH):
        frame(pair_ref[p * deep:(p + 1) * deep, :], fr_b, pair_at + p)
        frame(other_ref[p * deep:(p + 1) * deep, :], fr_b, other_at + p)
    out_ref[...] = jnp.zeros(out_ref.shape, jnp.float32)
    to_scalar.wait()

    def place(s, target):
        lane_out = lax.broadcasted_iota(jnp.int32, (1, LANES), 1)
        out_ref[22:23, :] = jnp.where(
            lane_out == SLOT * s, target.astype(jnp.float32), out_ref[22:23, :])

    def prepare_own(s, total):
        dy, dz, dx, cy, cz, cx, start, stop, target = decode(plan, s, own, planes)
        place(s, target)
        set_table(table, s, deep, dy, dz, dx, cy, cz, cx, start, stop)
        active[s] = s
        below = start < CHUNK
        low = jnp.where(below, start, planes - CHUNK)
        high = jnp.where(below, CHUNK, stop)
        count = jnp.maximum(high - low, 0) // CHUNK
        return set_units(units, total, s, low, count, 1)

    def prepare(s, carry):
        total, alive = carry
        dy, dz, dx, cy, cz, cx, start, stop, target = decode(plan, s, own, planes)
        place(s, target)
        count = (stop - start) // CHUNK

        @pl.when(count > 0)
        def _():
            f_a, f_b, sx = set_table(table, s, deep, dy, dz, dx, cy, cz, cx, start, stop)
            set_masks(masks, s, f_a, f_b, sx, cx, dx)
            for ref in (acc, sq_a, sq_b):
                ref[s] = jnp.zeros(ref.shape[1:], jnp.float32)
            active[alive] = s
            set_units(units, total, s, start, count, 2)

        return total + (count + 1) // 2, alive + jnp.where(count > 0, 1, 0)

    total = lax.fori_loop(0, own, prepare_own, 0)
    total, alive = lax.fori_loop(own, 3 * own, prepare, (total, own))
    spare = 3 * own
    for at in range(CLOSE - 1):
        active[alive + at] = spare
    run_units(total, units, table, spare, fr_a, fr_b, acc, sq_a, sq_b, masks)

    cols = 2 * LANES
    z_row = lax.broadcasted_iota(jnp.int32, (ROWS_A, LANES), 0)
    col_one = lax.broadcasted_iota(jnp.int32, (1, cols), 1)
    lag_one = jnp.where(col_one >= ROWS_B, 1, 0) + jnp.where(col_one >= 2 * ROWS_B, 1, 0)
    lag_one = lag_one + jnp.where(col_one >= 3 * ROWS_B, 1, 0)
    z_one = col_one - lag_one * ROWS_B
    lag_18 = jnp.broadcast_to(lag_one, (18, cols))
    lane_18 = lax.broadcasted_iota(jnp.int32, (18, LANES), 1)
    lane_4 = lax.broadcasted_iota(jnp.int32, (4, LANES), 1)
    z_b_row = lax.broadcasted_iota(jnp.int32, (ROWS_B, LANES), 0)

    def finish(t, carry):
        for h in range(CLOSE):
            s = active[CLOSE * t + h]
            f_a, z_a, f_b, z_b, dy, dz, dx, cz, at_first, at_last, has_first, has_last = [
                table[s, at] for at in range(12)]
            z_b = pl.multiple_of(z_b, 16)
            sz = cz + dz - HALF - 1
            z_from = cz - HALF - z_a
            z_in = (z_row >= z_from) & (z_row < z_from + W)
            gap = [
                jnp.where(z_in, gap_base[:, i * LANES:(i + 1) * LANES], FAR) for i in range(2)
            ]
            offset = z_a + dz - z_b
            tops = []
            lows = []
            for lag_z in range(3):
                hit = [g == offset + lag_z - 1 for g in gap]
                for lag_x in range(3):
                    part = [
                        jnp.sum(jnp.where(
                            hit[i],
                            acc[s, lag_x * ROWS_A:(lag_x + 1) * ROWS_A,
                                i * LANES:(i + 1) * LANES], 0.0), axis=0, keepdims=True)
                        for i in range(2)
                    ]
                    tops.append(jnp.concatenate(part, axis=1))
                low = cz - HALF + dz + lag_z - 1 - z_b
                inside = (z_one >= low) & (z_one < low + W)
                lows.append(jnp.where(inside, acc[s, 3 * ROWS_A:3 * ROWS_A + 3, :], 0.0))
            stack = jnp.concatenate(tops + lows, axis=0)

            z_b_in = (z_b_row >= sz - z_b) & (z_b_row < sz - z_b + BLOCK)
            mask = jnp.concatenate([masks[s, 2].astype(jnp.float32)] * (ROWS_B // 16), axis=0)
            mask = jnp.where(z_b_in, mask, 0.0)
            ends = [
                fr_b[0, f_b, at, pl.ds(z_b, ROWS_B), :].astype(jnp.float32)
                * (mask * has.astype(jnp.float32))
                for at, has in ((at_first, has_first), (at_last, has_last))
            ]
            low = sz - z_b
            inside = (z_one >= low) & (z_one < low + BLOCK) & (lag_one == 1)
            row_b = jnp.where(inside, acc[s, 3 * ROWS_A + 3:3 * ROWS_A + 4, :], 0.0)
            row_a = jnp.sum(jnp.where(
                z_in & (z_row * 0 + lax.broadcasted_iota(
                    jnp.int32, (ROWS_A, LANES), 1) == 3 * ROWS_B - LANES),
                acc[s, ROWS_A:2 * ROWS_A, LANES:], 0.0), axis=0, keepdims=True)
            sums = [
                row_a,
                jnp.sum(jnp.where(z_in, sq_a[s], 0.0), axis=0, keepdims=True),
                jnp.sum(ends[0] + ends[1], axis=0, keepdims=True)
                + row_b[:, :LANES] + row_b[:, LANES:],
                jnp.sum(
                    jnp.where(z_b_in, sq_b[s], 0.0) + (ends[0] * ends[0] + ends[1] * ends[1]),
                    axis=0, keepdims=True),
            ]
            sums = jnp.sum(jnp.concatenate(sums, axis=0), axis=1, keepdims=True)
            total_18 = jnp.zeros((18, LANES), jnp.float32)
            for lag_y in range(3):
                part = jnp.sum(jnp.where(lag_18 == lag_y, stack, 0.0), axis=1, keepdims=True)
                total_18 = total_18 + jnp.where(lane_18 == SLOT * s + lag_y, part, 0.0)
            out_ref[0:18] += total_18
            out_ref[18:22] += jnp.where(lane_4 == SLOT * s, sums, 0.0)
        return carry

    lax.fori_loop(0, (alive + CLOSE - 1) // CLOSE, finish, 0)


def update_kernel(own, mine_ref, pair_ref, other_ref, out_ref):
    tile_rows = out_ref.shape[0]
    even = lax.axis_index("span") % 2 == 0
    mine = mine_ref[...]
    pair = pair_ref[...]
    other = other_ref[...]
    below = jnp.where(even, other, pair)
    above = jnp.where(even, pair, other)
    span = SLOT * own
    lane = lax.broadcasted_iota(jnp.int32, mine.shape, 1)
    total = mine
    total = total + jnp.where(
        lane < span,
        pltpu.roll(below, LANES - 2 * span, 1) + pltpu.roll(above, LANES - span, 1),
        jnp.where(
            lane < 2 * span, pltpu.roll(below, span, 1),
            jnp.where(lane < 3 * span, pltpu.roll(above, 2 * span, 1), 0.0)))

    def lead(v):
        return v + pltpu.roll(v, LANES - 1, 1) + pltpu.roll(v, LANES - 2, 1)

    def spread(v):
        return v + pltpu.roll(v, 1, 1) + pltpu.roll(v, 2, 1)

    lag_lane = lane % SLOT
    stats = spread(jnp.where(lag_lane[0:4] == 0, total[18:22], 0.0))
    voxels = float(W) ** 3
    block_voxels = float(BLOCK) ** 3
    mean_a = stats[0:1] / voxels
    energy_a = jnp.maximum(stats[1:2] / voxels - mean_a * mean_a, 0.0)
    mean_b = stats[2:3] / block_voxels
    energy_b = jnp.maximum(stats[3:4] / block_voxels - mean_b * mean_b, 0.0)
    normaliser = voxels * jnp.sqrt((energy_a + EPSILON) * (energy_b + EPSILON))
    scaled = SHARP * ((total[0:9] - mean_a * total[9:18]) / normaliser)
    used = lag_lane[0:9] < 3
    scaled = jnp.where(used, scaled, -1e30)
    top = jnp.max(scaled, axis=0, keepdims=True)
    top = jnp.maximum(top, jnp.maximum(pltpu.roll(top, LANES - 1, 1), pltpu.roll(top, LANES - 2, 1)))
    top = spread(jnp.where(lag_lane[0:1] == 0, top, 0.0))
    weights = jnp.where(used, jnp.exp(scaled - top), 0.0)
    lag_row = lax.broadcasted_iota(jnp.int32, weights.shape, 0)
    lag_z = (lag_row // 3 - 1).astype(jnp.float32)
    lag_x = (lag_row % 3 - 1).astype(jnp.float32)
    column = jnp.sum(weights, axis=0, keepdims=True)
    weight_sum = lead(column)
    along_y = lead(column * (lag_lane[0:1] - 1).astype(jnp.float32)) / weight_sum
    along_z = lead(jnp.sum(weights * lag_z, axis=0, keepdims=True)) / weight_sum
    along_x = lead(jnp.sum(weights * lag_x, axis=0, keepdims=True)) / weight_sum
    corrections = (along_y, along_z, along_x)

    grid_lane = lax.broadcasted_iota(jnp.int32, (8, LANES), 1)
    place = lax.broadcasted_iota(jnp.int32, (8, LANES), 0) * GZX + grid_lane
    target = mine[22:23].astype(jnp.int32)
    fields = [jnp.zeros((8, LANES), jnp.float32) for _ in range(3)]
    for s in range(3 * own):
        hit = place == target[:, SLOT * s:SLOT * s + 1]
        for comp in range(3):
            fields[comp] = jnp.where(
                hit, corrections[comp][:, SLOT * s:SLOT * s + 1], fields[comp])
    lane_z = grid_lane // GX
    lane_x = grid_lane % GX
    for comp in range(3):
        field = fields[comp]
        near = jnp.where(lane_z >= 1, pltpu.roll(field, GX, 1), 0.0)
        near = near + jnp.where(lane_z < GZX // GX - 1, pltpu.roll(field, LANES - GX, 1), 0.0)
        near = near + jnp.where(lane_x >= 1, pltpu.roll(field, 1, 1), 0.0)
        near = near + jnp.where(lane_x < GX - 1, pltpu.roll(field, LANES - 1, 1), 0.0)
        near = near[1:1 + tile_rows] + field[0:tile_rows] + field[2:2 + tile_rows]
        out_ref[:, comp, :] = 0.4 * field[1:1 + tile_rows] + 0.1 * near


def shards(first, second, windows, shifts):
    planes, deep, along = first.shape
    own = windows.shape[0]
    slots = 3 * own + 1
    count = lax.axis_size("span")
    pairs = [(i, i ^ 1) for i in range(count)]
    others = [(i, i + 1) for i in range(1, count - 1, 2)]
    others = others + [(b, a) for a, b in others]
    vmem = pl.BlockSpec(memory_space=pltpu.VMEM)
    hbm = pl.BlockSpec(memory_space=pltpu.HBM)

    def limit(mib):
        return pltpu.CompilerParams(vmem_limit_bytes=mib << 20)

    busy = pl.CostEstimate(flops=20 * 10**9, bytes_accessed=0, transcendentals=0)
    message = jax.ShapeDtypeStruct((REACH * deep + PLAN_ROWS, along), second.dtype)
    gap = pl.pallas_call(
        table_kernel,
        out_shape=jax.ShapeDtypeStruct((ROWS_A, 2 * LANES), jnp.int32),
        out_specs=vmem,
        compiler_params=limit(4),
        cost_estimate=busy,
        name="gap_table",
    )()
    to_pair, to_other, plan = pl.pallas_call(
        send_kernel,
        out_shape=(message, message, jax.ShapeDtypeStruct((8, LANES), jnp.int32)),
        in_specs=[vmem] * 3 + [hbm],
        out_specs=(vmem,) * 3,
        scratch_shapes=[pltpu.SemaphoreType.DMA((2, REACH))],
        compiler_params=limit(4),
        cost_estimate=busy,
        name="planes_to_send",
    )(windows[None], shifts, gap, second)
    from_other = lax.ppermute(to_other, "span", others)
    from_pair = lax.ppermute(to_pair, "span", pairs)
    state = (
        jax.ShapeDtypeStruct((2, 2, planes + 2 * PAD_B, deep, LANES), jnp.bfloat16),
        jax.ShapeDtypeStruct((slots, 3 * ROWS_A + 16, 2 * LANES), jnp.float32),
        jax.ShapeDtypeStruct((slots, ROWS_A, LANES), jnp.float32),
        jax.ShapeDtypeStruct((slots, ROWS_B, LANES), jnp.float32),
        jax.ShapeDtypeStruct((slots, 6, 16, LANES), jnp.bfloat16),
    )
    scalars = [
        pltpu.SMEM((3, 8, LANES), jnp.int32),
        pltpu.SMEM((slots, FIELDS), jnp.int32),
        pltpu.SMEM((3 * own * (W // CHUNK) + PAIR,), jnp.int32),
    ]
    fr_a, *held = pl.pallas_call(
        inner_kernel,
        out_shape=(
            jax.ShapeDtypeStruct((2, 2, planes + 2 * PAD_A, deep, LANES), jnp.bfloat16), *state),
        in_specs=[vmem] * 3,
        out_specs=(vmem,) * 6,
        scratch_shapes=[
            *scalars,
            pltpu.SemaphoreType.DMA,
        ],
        compiler_params=limit(12),
        cost_estimate=pl.CostEstimate(
            flops=20 * 10**9, bytes_accessed=10 * 10**6, transcendentals=0),
        name="inner_sums",
    )(plan, first, second)
    sums, *_ = pl.pallas_call(
        outer_kernel,
        out_shape=(jax.ShapeDtypeStruct((24, LANES), jnp.float32), *state),
        in_specs=[vmem] * 10,
        out_specs=(vmem,) * 6,
        input_output_aliases={5 + i: 1 + i for i in range(5)},
        scratch_shapes=[
            pltpu.VMEM((3, 8, LANES), jnp.int32),
            *scalars,
            pltpu.SMEM((slots + CLOSE,), jnp.int32),
            pltpu.SemaphoreType.DMA,
        ],
        compiler_params=limit(12),
        name="outer_sums",
    )(plan, from_pair, from_other, gap, fr_a, *held)
    other_sums = lax.ppermute(sums, "span", others)
    pair_sums = lax.ppermute(sums, "span", pairs)
    field = pl.pallas_call(
        functools.partial(update_kernel, own),
        out_shape=jax.ShapeDtypeStruct((planes // STRIDE, 3, GZX), jnp.float32),
        in_specs=[vmem] * 3,
        out_specs=vmem,
        compiler_params=limit(4),
        name="smoothed_update",
    )(sums, pair_sums, other_sums)
    return jnp.transpose(field, (1, 0, 2))


def solution(mesh):
    in_specs = (
        P(("grp", "span"), None, None),
        P(("grp", "span"), None, None),
        P(("grp", "span")),
        P(None, ("grp", "span")),
    )
    out_specs = P(None, ("grp", "span"), None)
    return jax.shard_map(shards, mesh=mesh, in_specs=in_specs, out_specs=out_specs, check_vma=False)
```

time: 42.2 us -> 31.6 us (0.75)
  the two profiles are of different devices: /device:TPU:1 before, /device:TPU:23 now
where the time goes in v4:
time: 31.6 us; the launch traced here: 31.3 us
  Pallas kernels  19.6 us (62%)
  starting transfers between devices  7.4 us (23%)
  waiting for transfers between devices  2.43 us (8%)
  local copies, waits for them, and re-layouts  1.82 us (6%)
    pallas_call x1, Pallas kernels, shards(): pl.pallas_call(outer_kernel, out_shape=(jax.ShapeDtypeStruct((24, LANES),...  9.81 us
    pallas_call x1, Pallas kernels, shards(): pl.pallas_call(inner_kernel, out_shape=(jax.ShapeDtypeStruct((2, 2, plane...  7.8 us
    ppermute x1, starting transfers between devices, shards(): other_sums = lax.ppermute(sums, 'span', others)  3.27 us
    ppermute x1, starting transfers between devices, shards(): from_other = lax.ppermute(to_other, 'span', others)  3.18 us
    ppermute x1, waiting for transfers between devices, shards(): other_sums = lax.ppermute(sums, 'span', others)  2.42 us
    unnamed x8, local copies, waits for them, and re-layouts  1.82 us
    pallas_call x1, Pallas kernels, shards(): pl.pallas_call(functools.partial(update_kernel, own), out_shape=jax.Shape...  1.33 us
    ppermute x1, starting transfers between devices, shards(): from_pair = lax.ppermute(to_pair, 'span', pairs)  0.74 us
  transfers between devices with their start and end apart: 4, of which 1 were waited for; matrix products, arithmetic and copies ran while one was open for 0% of the time, Pallas kernels for 25%

profile of v4, /device:TPU:23, one launch (start us, length us, event | category | flops | bytes accessed | tf_op | source)
XLA Modules:
  0.0 31.3 jit_solution(16286269031741399670)
XLA Ops:
  0.0 0.0 copy-start
  0.0 0.0 copy-start.2
  0.0 0.0 copy-start.3
  0.0 1.8 %copy-done = bf16[60,96,192]{2,1,0:T(8,128)(2,1)S(1)} copy-done((bf16[60,96,192]{2,1,0:T(8,128)(2,1)S(1)}, bf16[60,96,192]{2,1,0:T(8,128)(2,1)}, u32[]{:S(2)}) %copy-start) | copy-done | bytes 2211864
  1.8 0.0 copy-done.2
  1.8 0.0 copy-done.3
  1.8 0.0 copy-start.1
  1.8 0.6 %planes_to_send.1 = (bf16[400,192]{1,0:T(8,128)(2,1)S(1)}, bf16[400,192]{1,0:T(8,128)(2,1)S(1)}, s32[8,128]{1,0:T(8,128)S(1)}) custom-call(s32[1,8]{1,0:T(1,128)S(1)} %bitcast.2, s32[3,8]{1,0:T(4,128)S(1)} %copy-done.2, s32[64,256]{1,0:T(8,128)S(1)} %gap_table.1.gap_ref.gap_base, bf16[60,96,192]{2,1,0:T(8,128)(2,1)S(1)} %copy-done), custom_call_target="tpu_custom_call" | custom-call | flops 20000000000 | tf_op jit(solution)/shard_map/planes_to_send/pallas_call | solution.py:496
  2.5 0.7 %collective-permute-start = (bf16[400,192]{1,0:T(8,128)(2,1)S(1)}, bf16[400,192]{1,0:T(8,128)(2,1)S(1)}, u32[]{:S(2)}, u32[]{:S(2)}) collective-permute-start(bf16[400,192]{1,0:T(8,128)(2,1)S(1)} %get-tuple-element.16), channel_id=1, source_target_pairs={{0,1},{1,0},{2,3},{3,2},{4,5},{5,4},{6,7},{7,6},{8,9},{9,8},{10,11... | collective-permute-start | bytes 460808 | tf_op jit(solution)/shard_map/ppermute | solution.py:507
  3.2 3.2 %collective-permute-start.1 = (bf16[400,192]{1,0:T(8,128)(2,1)S(1)}, bf16[400,192]{1,0:T(8,128)(2,1)S(1)}, u32[]{:S(2)}, u32[]{:S(2)}) collective-permute-start(bf16[400,192]{1,0:T(8,128)(2,1)S(1)} %get-tuple-element.17), channel_id=1, source_target_pairs={{1,2},{3,4},{5,6},{7,8},{9,10},{11,12},{13,14},{2,1},{4,3},{6,5},{... | collective-permute-start | bytes 460808 | tf_op jit(solution)/shard_map/ppermute | solution.py:506
  6.4 0.0 copy-done.1
  6.4 7.8 %inner_sums.1 = (bf16[2,2,72,96,128]{4,3,2,1,0:T(8,128)(2,1)S(1)}, bf16[2,2,80,96,128]{4,3,2,1,0:T(8,128)(2,1)S(1)}, f32[25,208,256]{2,1,0:T(8,128)S(1)}, f32[25...) custom-call(s32[8,128]{1,0:T(8,128)S(1)} %get-tuple-element.15.plan_ref, ...), custom_call_target="tpu_custom_call" | custom-call | flops 20000000000 | bytes 10000000 | tf_op jit(solution)/shard_map/inner_sums/pallas_call | solution.py:520
  14.2 0.0 collective-permute-done.pair_ref
  14.2 0.0 collective-permute-done.1.other_ref
  14.2 9.8 %outer_sums.1 = (f32[24,128]{1,0:T(8,128)S(1)}, bf16[2,2,80,96,128]{4,3,2,1,0:T(8,128)(2,1)S(1)}, f32[25,208,256]{2,1,0:T(8,128)S(1)}, f32[25,64,128]{2,1,0:T(8,...) custom-call(s32[8,128]{1,0:T(8,128)S(1)} %get-tuple-element.15.plan_, ...), custom_call_target="tpu_custom_call", output_to_operand_aliasing={{1}: (5, {}), {2}: (6, {}), {3}: (7, {}), {4}: (8, {}), {5}... | custom-call | tf_op jit(solution)/shard_map/outer_sums/pallas_call | solution.py:535
  24.0 3.3 %collective-permute-start.3 = (f32[24,128]{1,0:T(8,128)S(1)}, f32[24,128]{1,0:T(8,128)S(1)}, u32[]{:S(2)}, u32[]{:S(2)}) collective-permute-start(f32[24,128]{1,0:T(8,128)S(1)} %get-tuple-element.24.mine_ref), channel_id=1, source_target_pairs={{1,2},{3,4},{5,6},{7,8},{9,10},{11,12},{13,14},{2,1},{4,3},{6,5},{... | collective-permute-start | bytes 36872 | tf_op jit(solution)/shard_map/ppermute | solution.py:550
  27.3 0.2 collective-permute-start.2
  27.5 2.4 %collective-permute-done.3.other_ref = f32[24,128]{1,0:T(8,128)S(1)} collective-permute-done((f32[24,128]{1,0:T(8,128)S(1)}, f32[24,128]{1,0:T(8,128)S(1)}, u32[]{:S(2)}, u32[]{:S(2)}) %collective-permute-start.3) | collective-permute-done | bytes 12320 | tf_op jit(solution)/shard_map/ppermute | solution.py:550
  30.0 0.0 collective-permute-done.2.pair_ref
  30.0 1.3 %smoothed_update.1 = f32[5,3,128]{2,1,0:T(4,128)} custom-call(f32[24,128]{1,0:T(8,128)S(1)} %get-tuple-element.24.mine_ref, f32[24,128]{1,0:T(8,128)S(1)} %collective-permute-done.2.pair_ref, f32[24,128]{1,0:T(8,128)S(1)} %collective-permute-done.3.other_ref), custom_call_target="tpu_custom_call" | custom-call | tf_op jit(solution)/shard_map/smoothed_update/pallas_call | solution.py:552
  (1 shorter events, 0.0 us)
Async XLA Ops:
  0.0 1.8 %copy-start = (bf16[60,96,192]{2,1,0:T(8,128)(2,1)S(1)}, bf16[60,96,192]{2,1,0:T(8,128)(2,1)}, u32[]{:S(2)}) copy-start(bf16[60,96,192]{2,1,0:T(8,128)(2,1)} %second_ref.1) | copy-start | bytes 6635524
  0.0 1.8 %copy-start.2 = (s32[3,8]{1,0:T(4,128)S(1)}, s32[3,8]{1,0:T(4,128)}, u32[]{:S(2)}) copy-start(s32[3,8]{1,0:T(4,128)} %shift_ref.1) | copy-start | bytes 292
  0.0 1.8 %copy-start.3 = (s32[8]{0:T(128)S(1)}, s32[8]{0:T(128)}, u32[]{:S(2)}) copy-start(s32[8]{0:T(128)} %param.6) | copy-start | bytes 100
  1.8 4.5 %copy-start.1 = (bf16[60,96,192]{2,1,0:T(8,128)(2,1)S(1)}, bf16[60,96,192]{2,1,0:T(8,128)(2,1)}, u32[]{:S(2)}) copy-start(bf16[60,96,192]{2,1,0:T(8,128)(2,1)} %first_ref.1) | copy-start | bytes 6635524
  2.5 11.8 %collective-permute-start = (bf16[400,192]{1,0:T(8,128)(2,1)S(1)}, bf16[400,192]{1,0:T(8,128)(2,1)S(1)}, u32[]{:S(2)}, u32[]{:S(2)}) collective-permute-start(bf16[400,192]{1,0:T(8,128)(2,1)S(1)} %get-tuple-element.16), channel_id=1, source_target_pairs={{0,1},{1,0},{2,3},{3,2},{4,5},{5,4},{6,7},{7,6},{8,9},{9,8},{10,11... | collective-permute-start | bytes 460808 | tf_op jit(solution)/shard_map/ppermute | solution.py:507
  3.2 11.0 %collective-permute-start.1 = (bf16[400,192]{1,0:T(8,128)(2,1)S(1)}, bf16[400,192]{1,0:T(8,128)(2,1)S(1)}, u32[]{:S(2)}, u32[]{:S(2)}) collective-permute-start(bf16[400,192]{1,0:T(8,128)(2,1)S(1)} %get-tuple-element.17), channel_id=1, source_target_pairs={{1,2},{3,4},{5,6},{7,8},{9,10},{11,12},{13,14},{2,1},{4,3},{6,5},{... | collective-permute-start | bytes 460808 | tf_op jit(solution)/shard_map/ppermute | solution.py:506
  24.0 5.9 %collective-permute-start.3 = (f32[24,128]{1,0:T(8,128)S(1)}, f32[24,128]{1,0:T(8,128)S(1)}, u32[]{:S(2)}, u32[]{:S(2)}) collective-permute-start(f32[24,128]{1,0:T(8,128)S(1)} %get-tuple-element.24.mine_ref), channel_id=1, source_target_pairs={{1,2},{3,4},{5,6},{7,8},{9,10},{11,12},{13,14},{2,1},{4,3},{6,5},{... | collective-permute-start | bytes 36872 | tf_op jit(solution)/shard_map/ppermute | solution.py:550
  27.3 2.6 %collective-permute-start.2 = (f32[24,128]{1,0:T(8,128)S(1)}, f32[24,128]{1,0:T(8,128)S(1)}, u32[]{:S(2)}, u32[]{:S(2)}) collective-permute-start(f32[24,128]{1,0:T(8,128)S(1)} %get-tuple-element.24.mine_ref), channel_id=1, source_target_pairs={{0,1},{1,0},{2,3},{3,2},{4,5},{5,4},{6,7},{7,6},{8,9},{9,8},{10,11... | collective-permute-start | bytes 36872 | tf_op jit(solution)/shard_map/ppermute | solution.py:551

commit v5 on v4

v5 whole, which is shorter than its diff:
```python
import functools

import jax
import jax.numpy as jnp
from jax import lax
from jax.experimental import pallas as pl
from jax.experimental.pallas import tpu as pltpu
from jax.sharding import PartitionSpec as P

W = 48
STRIDE = 12
DYM = 3
GX = 16
GZX = 128
SHARP = 80.0
EPSILON = 1e-06

HALF = W // 2
BLOCK = W + 2
REACH = DYM + 1
LANES = 128
HOP = 64
CHUNK = 6
ROWS_A = 64
ROWS_B = 80
PAD_A = CHUNK
PAD_B = CHUNK + REACH
PIECES = 2
SLOT = 4
PLAN_ROWS = 16
FIELDS = 24
PAIR = 8
REST = 4
CLOSE = 2
FAR = 4096


def table_kernel(low_ref, gap_ref):
    row = lax.broadcasted_iota(jnp.int32, gap_ref.shape, 0)
    col = lax.broadcasted_iota(jnp.int32, gap_ref.shape, 1)
    lag = jnp.where(col >= ROWS_B, 1, 0) + jnp.where(col >= 2 * ROWS_B, 1, 0)
    gap_ref[...] = jnp.where(col < 3 * ROWS_B, col - lag * ROWS_B - row, FAR)


def send_kernel(win_ref, shift_ref, gap_ref, low_ref, high_ref, pair_ref, other_ref, plan_ref):
    reach, deep, along = low_ref.shape
    even = lax.axis_index("span") % 2 == 0
    node = win_ref[...]
    own = node.shape[1]
    plan_ref[...] = jnp.zeros(plan_ref.shape, jnp.int32)
    plan_ref[0:1, 0:own] = node >> 8
    plan_ref[1:2, 0:own] = node & 255
    plan_ref[2:5, 0:own] = shift_ref[...]
    plan = plan_ref[...].astype(jnp.float32).astype(jnp.bfloat16)
    for ref in (pair_ref, other_ref):
        ref[reach * deep:reach * deep + 8, 0:LANES] = plan

    def fill(to_low, to_high):
        for p in range(reach):
            to_low[p * deep:(p + 1) * deep, :] = low_ref[p]
            to_high[p * deep:(p + 1) * deep, :] = high_ref[p]

    @pl.when(even)
    def _():
        fill(other_ref, pair_ref)

    @pl.when(jnp.logical_not(even))
    def _():
        fill(pair_ref, other_ref)


def decode(plan, own, planes, deep, inner, table):
    device = lax.axis_index("span")
    last = lax.axis_size("span") - 1
    tile_rows = planes // STRIDE
    slot = lax.broadcasted_iota(jnp.int32, (1, LANES), 1)
    node = plan[0:1] * 256 + plan[1:2]
    dy, dz, dx = plan[2:3], plan[3:4], plan[4:5]
    row = (node >> (GZX.bit_length() - 1)) - device * tile_rows
    rest = node & (GZX - 1)
    cy = STRIDE * row + STRIDE // 2
    cz = STRIDE * (rest >> (GX.bit_length() - 1)) + STRIDE // 2
    cx = STRIDE * (rest & (GX - 1)) + STRIDE // 2
    start = jnp.maximum(cy - HALF, jnp.where(device == 0, -CHUNK, 0))
    stop = jnp.minimum(cy + HALF, jnp.where(device == last, planes + CHUNK, planes))
    mine = slot < own
    lower = (slot >= own) & (slot < 2 * own)
    upper = (slot >= 2 * own) & (slot < 3 * own)
    wanted = (
        mine | (lower & (row < 0) & (row >= -tile_rows))
        | (upper & (row >= tile_rows) & (row < 2 * tile_rows))
    )
    if inner:
        low = jnp.maximum(start, CHUNK)
        high = jnp.minimum(stop, planes - CHUNK)
        wanted = mine
    else:
        below = start < CHUNK
        low = jnp.where(mine & jnp.logical_not(below), planes - CHUNK, start)
        high = jnp.where(mine & below, CHUNK, stop)
    width = jnp.where(wanted, high - low, 0)
    count = sum([jnp.where(width > CHUNK * c, 1, 0) for c in range(W // CHUNK)])
    sx = cx + dx - HALF - 1
    sz = cz + dz - HALF - 1
    z_a = jnp.minimum(jnp.maximum(cz - HALF, 0) & -16, deep - ROWS_A)
    z_b = jnp.where(sz + BLOCK <= ROWS_B, 0, deep - ROWS_B)
    values = (
        jnp.where(cx + HALF <= LANES, 0, 1),
        z_a,
        jnp.where(sx + BLOCK <= LANES, 0, 1),
        z_b,
        dy,
        z_a + dz - z_b,
        (dx + LANES) & (LANES - 1),
        cz - HALF - z_a,
        start + dy - 1 + PAD_B,
        stop + dy + PAD_B,
        jnp.where(start == cy - HALF, 1, 0),
        jnp.where(stop == cy + HALF, 1, 0),
        low,
        count,
        cx - HALF,
        sx,
        sz - z_b,
    )
    for at, value in enumerate(values):
        table[at:at + 1, :] = jnp.where(slot < 3 * own, value, 0)
    return jnp.where(
        mine | (lower & (row == -1)) | (upper & (row == tile_rows)),
        (row + 1) * GZX + rest, -1)


def set_masks(masks, s, table):
    f_a, f_b = table[0, s], table[2, s]
    z_from, x_from = table[7, s], table[14, s]
    sx, zb_from = table[15, s], table[16, s]
    reach_x = sx + 1

    def in_x(rows, half, frame_at, low, high):
        lane = (lax.broadcasted_iota(jnp.int32, (rows, LANES), 1) + half * HOP) & (LANES - 1)
        x = lane + jnp.where(lane < HOP, LANES * frame_at, 0)
        return (x >= low) & (x < high)

    def in_z(rows, low, count):
        z = lax.broadcasted_iota(jnp.int32, (rows, LANES), 0)
        return (z >= low) & (z < low + count)

    row = lax.broadcasted_iota(jnp.int32, (16, LANES), 0)
    wide = row == 3
    low = jnp.where(wide, sx, reach_x + row - 1)
    high = low + jnp.where(wide, BLOCK, jnp.where(row < 3, W, 0))
    z_a = in_z(ROWS_A, z_from, W)
    z_b = in_z(ROWS_B, zb_from, BLOCK)
    at = 0
    for rows, frame_at, x_low, x_high, z in (
        (ROWS_A, f_a, x_from, x_from + W, z_a),
        (ROWS_B, f_b, sx, sx + BLOCK, z_b),
        (16, f_b, low, high, None),
    ):
        for half in range(2):
            inside = in_x(rows, half, frame_at, x_low, x_high)
            inside = inside if z is None else inside & z
            masks[s, at:at + rows] = jnp.where(inside, 1.0, 0.0).astype(jnp.bfloat16)
            at += rows


def set_units(units, total, s, low, count, most):
    for c in range(most):
        both = jnp.where(2 * c + 1 < count, 1, 0)
        units[total + c] = s + (low + 2 * CHUNK * c + 64) * 256 + both * 65536
    return total + ((count + 1) >> 1)


def frame(v, fr, at):
    low = v[:, :LANES]
    high = jnp.concatenate([v[:, LANES:], v[:, HOP:LANES]], axis=1)
    fr[0, 0, at] = low
    fr[0, 1, at] = high
    fr[1, 0, at] = pltpu.roll(low, HOP, 1)
    fr[1, 1, at] = pltpu.roll(high, HOP, 1)


def run_units(total, units, table, spare, fr_a, fr_b, acc, sq_a, sq_b, masks):
    for at in range(REST - 1):
        units[total + at] = spare + 64 * 256
    ones = jnp.where(
        lax.broadcasted_iota(jnp.int32, (16, CHUNK * LANES), 0) == 0, 1.0, 0.0
    ).astype(jnp.bfloat16)

    def step(first, width):
        for h in range(width):
            code = units[first + h]
            s = code & 255
            y = ((code >> 8) & 255) - 64
            both = code >> 16
            y_two = y + both * CHUNK
            keep = both.astype(jnp.float32).astype(jnp.bfloat16)
            f_a = table[0, s]
            z_a = pl.multiple_of(table[1, s], 16)
            f_b = table[2, s]
            z_b = pl.multiple_of(table[3, s], 16)
            dy = table[4, s]
            dx = table[6, s]
            one_a = masks[s, 0:ROWS_A]
            two_a = masks[s, ROWS_A:2 * ROWS_A] * keep
            at = 2 * ROWS_A
            one_b = masks[s, at:at + ROWS_B]
            two_b = masks[s, at + ROWS_B:at + 2 * ROWS_B] * keep
            at += 2 * ROWS_B
            rows = masks[s, at:at + 16] + masks[s, at + 16:at + 32] * keep
            a = [
                fr_a[0, f_a, y + PAD_A + p, pl.ds(z_a, ROWS_A), :] * one_a
                + fr_a[1, f_a, y_two + PAD_A + p, pl.ds(z_a, ROWS_A), :] * two_a
                for p in range(CHUNK)
            ]
            b = [
                fr_b[0, f_b, y + dy - 1 + PAD_B + p, pl.ds(z_b, ROWS_B), :] * one_b
                + fr_b[1, f_b, y_two + dy - 1 + PAD_B + p, pl.ds(z_b, ROWS_B), :] * two_b
                for p in range(CHUNK + 2)
            ]
            left = [
                jnp.concatenate(
                    [pltpu.roll(v, (dx + lag - 1 + LANES) & (LANES - 1), 1) for v in a], axis=1)
                for lag in range(3)
            ]
            left.append(jnp.concatenate([rows] * CHUNK, axis=1))
            left = jnp.concatenate(left, axis=0)
            right = [jnp.concatenate(b[lag:lag + CHUNK], axis=1) for lag in range(3)]
            right = jnp.concatenate(right + [ones], axis=0)
            acc[s] += lax.dot_general(
                left, right, (((1,), (1,)), ((), ())), preferred_element_type=jnp.float32)
            wide = [v.astype(jnp.float32) for v in a]
            sq_a[s] += sum([v * v for v in wide])
            wide = [v.astype(jnp.float32) for v in b[1:-1]]
            sq_b[s] += sum([v * v for v in wide])

    def wide_step(t, carry):
        step(PAIR * t, PAIR)
        return carry

    full = (total + REST - 1) // PAIR
    lax.fori_loop(0, full, wide_step, 0)

    @pl.when(total > PAIR * full)
    def _():
        step(PAIR * full, REST)


def edge_copies(edge_a, edge_b, fr_a, fr_b, planes, sem):
    far_a = edge_a.shape[2] // 2
    far_b = edge_b.shape[2] // 2
    return (
        (fr_a.at[:, :, pl.ds(PAD_A, far_a)], edge_a.at[:, :, pl.ds(0, far_a)], sem.at[0]),
        (fr_a.at[:, :, pl.ds(PAD_A + planes - far_a, far_a)],
         edge_a.at[:, :, pl.ds(far_a, far_a)], sem.at[1]),
        (fr_b.at[:, :, pl.ds(PAD_B, far_b)], edge_b.at[:, :, pl.ds(0, far_b)], sem.at[2]),
        (fr_b.at[:, :, pl.ds(PAD_B + planes - far_b, far_b)],
         edge_b.at[:, :, pl.ds(far_b, far_b)], sem.at[3]),
    )


def inner_kernel(
    plan_ref, first_ref, second_ref, edge_a, edge_b, edge_masks, acc, sq_a, sq_b,
    fr_a, fr_b, masks, table_v, table, units, sem_t, sem_e,
):
    planes, deep, along = first_ref.shape
    own = (acc.shape[0] - 1) // 3
    piece = planes // PIECES
    decode(plan_ref[...], own, planes, deep, True, table_v)
    to_scalar = pltpu.make_async_copy(table_v, table, sem_t)
    to_scalar.start()
    for ref, fr, pad in ((first_ref, fr_a, PAD_A), (second_ref, fr_b, PAD_B)):
        def body(i, carry, ref=ref, fr=fr, pad=pad):
            for p in range(piece):
                at = i * piece + p
                frame(ref[at], fr, at + pad)
            return carry

        lax.fori_loop(0, PIECES, body, 0)

    hand_on = [
        pltpu.make_async_copy(source, target, sem)
        for source, target, sem in edge_copies(edge_a, edge_b, fr_a, fr_b, planes, sem_e)
    ]
    for c in hand_on:
        c.start()
    to_scalar.wait()

    def prepare(s, total):
        set_masks(masks, s, table)
        for ref in (acc, sq_a, sq_b):
            ref[s] = jnp.zeros(ref.shape[1:], jnp.float32)
        return set_units(units, total, s, table[12, s], table[13, s], W // CHUNK // 2)

    total = lax.fori_loop(0, own, prepare, 0)
    masks_on = pltpu.make_async_copy(masks.at[pl.ds(0, own)], edge_masks, sem_e.at[4])
    masks_on.start()
    run_units(total, units, table, 3 * own, fr_a, fr_b, acc, sq_a, sq_b, masks)
    for c in hand_on:
        c.wait()
    masks_on.wait()


def outer_kernel(
    plan_ref, pair_ref, other_ref, gap_base, edge_a, edge_b, edge_masks, acc_in, sq_a_in, sq_b_in,
    out_ref, acc, sq_a, sq_b,
    fr_a, fr_b, masks, table_v, table, units, active, sem_t, sem_e,
):
    deep = fr_a.shape[3]
    planes = fr_a.shape[2] - 2 * PAD_A
    own = (acc.shape[0] - 1) // 3
    device = lax.axis_index("span")
    last = lax.axis_size("span") - 1
    even = device % 2 == 0
    base = REACH * deep
    bring_in = [
        pltpu.make_async_copy(source, target, sem)
        for target, source, sem in edge_copies(edge_a, edge_b, fr_a, fr_b, planes, sem_e)
    ] + [pltpu.make_async_copy(edge_masks, masks.at[pl.ds(0, own)], sem_e.at[4])]
    for c in bring_in:
        c.start()
    from_pair, from_other = [
        ref[base:base + 8, 0:LANES].astype(jnp.float32).astype(jnp.int32)
        for ref in (pair_ref, other_ref)
    ]
    below = jnp.where(even, from_other, from_pair)
    above = jnp.where(even, from_pair, from_other)
    plan = plan_ref[...] + pltpu.roll(below, own, 1) + pltpu.roll(above, 2 * own, 1)
    target = decode(plan, own, planes, deep, False, table_v)
    to_scalar = pltpu.make_async_copy(table_v, table, sem_t)
    to_scalar.start()
    out_ref[...] = jnp.zeros(out_ref.shape, jnp.float32)
    out_ref[22:23] = target.astype(jnp.float32)

    @pl.when((device == 0) | (device == last))
    def _():
        zero = jnp.zeros((2, 2, CHUNK, deep, LANES), jnp.bfloat16)
        fr_a[:, :, 0:PAD_A] = zero
        fr_a[:, :, PAD_A + planes:] = zero
        fr_b[:, :, 0:CHUNK] = zero
        fr_b[:, :, PAD_B + planes + REACH:] = zero

    low_at, high_at = CHUNK, PAD_B + planes
    pair_at = jnp.where(even, high_at, low_at)
    other_at = jnp.where(even, low_at, high_at)
    for p in range(REACH):
        frame(pair_ref[p * deep:(p + 1) * deep, :], fr_b, pair_at + p)
        frame(other_ref[p * deep:(p + 1) * deep, :], fr_b, other_at + p)
    to_scalar.wait()

    def prepare_own(s, total):
        active[s] = s
        return set_units(units, total, s, table[12, s], table[13, s], 1)

    total = lax.fori_loop(0, own, prepare_own, 0)
    for c in bring_in:
        c.wait()

    def prepare(s, carry):
        total, alive = carry
        count = table[13, s]

        @pl.when(count > 0)
        def _():
            set_masks(masks, s, table)
            for ref in (acc, sq_a, sq_b):
                ref[s] = jnp.zeros(ref.shape[1:], jnp.float32)
            active[alive] = s
            set_units(units, total, s, table[12, s], count, 2)

        return total + ((count + 1) >> 1), alive + jnp.where(count > 0, 1, 0)

    total, alive = lax.fori_loop(own, 3 * own, prepare, (total, own))
    spare = 3 * own
    for at in range(CLOSE - 1):
        active[alive + at] = spare
    run_units(total, units, table, spare, fr_a, fr_b, acc, sq_a, sq_b, masks)

    cols = 2 * LANES
    col_one = lax.broadcasted_iota(jnp.int32, (1, cols), 1)
    lag_one = jnp.where(col_one >= ROWS_B, 1, 0) + jnp.where(col_one >= 2 * ROWS_B, 1, 0)
    lag_one = lag_one + jnp.where(col_one >= 3 * ROWS_B, 1, 0)
    z_one = col_one - lag_one * ROWS_B
    lag_18 = jnp.broadcast_to(lag_one, (18, cols))
    lane_18 = lax.broadcasted_iota(jnp.int32, (18, LANES), 1)
    lane_4 = lax.broadcasted_iota(jnp.int32, (4, LANES), 1)
    slant = lax.broadcasted_iota(jnp.int32, (8, cols), 1)
    slant = slant - lax.broadcasted_iota(jnp.int32, (8, cols), 0)
    mean_lane = lax.broadcasted_iota(jnp.int32, (1, LANES), 1) == 3 * ROWS_B - LANES

    def finish(t, carry):
        for h in range(CLOSE):
            s = active[CLOSE * t + h]
            f_b = table[2, s]
            z_b = pl.multiple_of(table[3, s], 16)
            offset = table[5, s]
            low_z = table[16, s] + 1
            band = (gap_base[...] >= offset - 1) & (gap_base[...] <= offset + 1)
            tops = [None] * 9
            lows = []
            for lag_x in range(3):
                part = jnp.where(band, acc[s, lag_x * ROWS_A:(lag_x + 1) * ROWS_A, :], 0.0)
                part = sum([part[8 * i:8 * i + 8] for i in range(ROWS_A // 8)])
                for lag_z in range(3):
                    hit = ((slant - (offset + lag_z - 1)) & 7) == 0
                    tops[3 * lag_z + lag_x] = jnp.sum(
                        jnp.where(hit, part, 0.0), axis=0, keepdims=True)
            for lag_z in range(3):
                low = low_z + lag_z - 1
                inside = (z_one >= low) & (z_one < low + W)
                lows.append(jnp.where(inside, acc[s, 3 * ROWS_A:3 * ROWS_A + 3, :], 0.0))
            stack = jnp.concatenate(tops + lows, axis=0)

            at = 2 * ROWS_A
            mask = masks[s, at:at + ROWS_B].astype(jnp.float32)
            ends = [
                fr_b[0, f_b, table[8 + i, s], pl.ds(z_b, ROWS_B), :].astype(jnp.float32)
                * (mask * table[10 + i, s].astype(jnp.float32))
                for i in range(2)
            ]
            row_b = jnp.where(
                lag_one == 1, acc[s, 3 * ROWS_A + 3:3 * ROWS_A + 4, :], 0.0)
            row_a = jnp.sum(acc[s, ROWS_A:2 * ROWS_A, LANES:], axis=0, keepdims=True)
            sums = [
                jnp.where(mean_lane, row_a, 0.0),
                jnp.sum(sq_a[s], axis=0, keepdims=True),
                jnp.sum(ends[0] + ends[1], axis=0, keepdims=True)
                + row_b[:, :LANES] + row_b[:, LANES:],
                jnp.sum(
                    sq_b[s] + (ends[0] * ends[0] + ends[1] * ends[1]), axis=0, keepdims=True),
            ]
            sums = jnp.sum(jnp.concatenate(sums, axis=0), axis=1, keepdims=True)
            total_18 = jnp.zeros((18, LANES), jnp.float32)
            for lag_y in range(3):
                part = jnp.sum(jnp.where(lag_18 == lag_y, stack, 0.0), axis=1, keepdims=True)
                total_18 = total_18 + jnp.where(lane_18 == SLOT * s + lag_y, part, 0.0)
            out_ref[0:18] += total_18
            out_ref[18:22] += jnp.where(lane_4 == SLOT * s, sums, 0.0)
        return carry

    lax.fori_loop(0, (alive + CLOSE - 1) // CLOSE, finish, 0)


def update_kernel(own, mine_ref, pair_ref, other_ref, out_ref):
    tile_rows = out_ref.shape[0]
    even = lax.axis_index("span") % 2 == 0
    mine = mine_ref[...]
    pair = pair_ref[...]
    other = other_ref[...]
    below = jnp.where(even, other, pair)
    above = jnp.where(even, pair, other)
    span = SLOT * own
    lane = lax.broadcasted_iota(jnp.int32, mine.shape, 1)
    total = mine
    total = total + jnp.where(
        lane < span,
        pltpu.roll(below, LANES - 2 * span, 1) + pltpu.roll(above, LANES - span, 1),
        jnp.where(
            lane < 2 * span, pltpu.roll(below, span, 1),
            jnp.where(lane < 3 * span, pltpu.roll(above, 2 * span, 1), 0.0)))

    def lead(v):
        return v + pltpu.roll(v, LANES - 1, 1) + pltpu.roll(v, LANES - 2, 1)

    def spread(v):
        return v + pltpu.roll(v, 1, 1) + pltpu.roll(v, 2, 1)

    lag_lane = lane % SLOT
    stats = spread(jnp.where(lag_lane[0:4] == 0, total[18:22], 0.0))
    voxels = float(W) ** 3
    block_voxels = float(BLOCK) ** 3
    mean_a = stats[0:1] / voxels
    energy_a = jnp.maximum(stats[1:2] / voxels - mean_a * mean_a, 0.0)
    mean_b = stats[2:3] / block_voxels
    energy_b = jnp.maximum(stats[3:4] / block_voxels - mean_b * mean_b, 0.0)
    normaliser = voxels * jnp.sqrt((energy_a + EPSILON) * (energy_b + EPSILON))
    scaled = SHARP * ((total[0:9] - mean_a * total[9:18]) / normaliser)
    used = lag_lane[0:9] < 3
    scaled = jnp.where(used, scaled, -1e30)
    top = jnp.max(scaled, axis=0, keepdims=True)
    top = jnp.maximum(top, jnp.maximum(pltpu.roll(top, LANES - 1, 1), pltpu.roll(top, LANES - 2, 1)))
    top = spread(jnp.where(lag_lane[0:1] == 0, top, 0.0))
    weights = jnp.where(used, jnp.exp(scaled - top), 0.0)
    lag_row = lax.broadcasted_iota(jnp.int32, weights.shape, 0)
    lag_z = (lag_row // 3 - 1).astype(jnp.float32)
    lag_x = (lag_row % 3 - 1).astype(jnp.float32)
    column = jnp.sum(weights, axis=0, keepdims=True)
    weight_sum = lead(column)
    along_y = lead(column * (lag_lane[0:1] - 1).astype(jnp.float32)) / weight_sum
    along_z = lead(jnp.sum(weights * lag_z, axis=0, keepdims=True)) / weight_sum
    along_x = lead(jnp.sum(weights * lag_x, axis=0, keepdims=True)) / weight_sum
    corrections = (along_y, along_z, along_x)

    grid_lane = lax.broadcasted_iota(jnp.int32, (8, LANES), 1)
    place = lax.broadcasted_iota(jnp.int32, (8, LANES), 0) * GZX + grid_lane
    target = mine[22:23].astype(jnp.int32)
    fields = [jnp.zeros((8, LANES), jnp.float32) for _ in range(3)]
    for s in range(3 * own):
        hit = place == target[:, s:s + 1]
        for comp in range(3):
            fields[comp] = jnp.where(
                hit, corrections[comp][:, SLOT * s:SLOT * s + 1], fields[comp])
    lane_z = grid_lane // GX
    lane_x = grid_lane % GX
    for comp in range(3):
        field = fields[comp]
        near = jnp.where(lane_z >= 1, pltpu.roll(field, GX, 1), 0.0)
        near = near + jnp.where(lane_z < GZX // GX - 1, pltpu.roll(field, LANES - GX, 1), 0.0)
        near = near + jnp.where(lane_x >= 1, pltpu.roll(field, 1, 1), 0.0)
        near = near + jnp.where(lane_x < GX - 1, pltpu.roll(field, LANES - 1, 1), 0.0)
        near = near[1:1 + tile_rows] + field[0:tile_rows] + field[2:2 + tile_rows]
        out_ref[:, comp, :] = 0.4 * field[1:1 + tile_rows] + 0.1 * near


def shards(first, second, windows, shifts):
    planes, deep, along = first.shape
    own = windows.shape[0]
    slots = 3 * own + 1
    count = lax.axis_size("span")
    pairs = [(i, i ^ 1) for i in range(count)]
    others = [(i, i + 1) for i in range(1, count - 1, 2)]
    others = others + [(b, a) for a, b in others]
    vmem = pl.BlockSpec(memory_space=pltpu.VMEM)

    def limit(mib):
        return pltpu.CompilerParams(vmem_limit_bytes=mib << 20)

    busy = pl.CostEstimate(flops=20 * 10**9, bytes_accessed=0, transcendentals=0)
    low_planes, high_planes = second[:REACH], second[planes - REACH:]
    gap = pl.pallas_call(
        table_kernel,
        out_shape=jax.ShapeDtypeStruct((ROWS_A, 2 * LANES), jnp.int32),
        in_specs=[vmem],
        out_specs=vmem,
        compiler_params=limit(4),
        cost_estimate=busy,
        name="gap_table",
    )(low_planes)
    message = jax.ShapeDtypeStruct((REACH * deep + PLAN_ROWS, along), second.dtype)
    to_pair, to_other, plan = pl.pallas_call(
        send_kernel,
        out_shape=(message, message, jax.ShapeDtypeStruct((8, LANES), jnp.int32)),
        in_specs=[vmem] * 5,
        out_specs=(vmem,) * 3,
        compiler_params=limit(4),
        cost_estimate=busy,
        name="planes_to_send",
    )(windows[None], shifts, gap, low_planes, high_planes)
    from_other = lax.ppermute(to_other, "span", others)
    from_pair = lax.ppermute(to_pair, "span", pairs)
    mask_rows = 2 * (ROWS_A + ROWS_B + 16)
    far = W // 2 - STRIDE // 2
    state = (
        jax.ShapeDtypeStruct((slots, 3 * ROWS_A + 16, 2 * LANES), jnp.float32),
        jax.ShapeDtypeStruct((slots, ROWS_A, LANES), jnp.float32),
        jax.ShapeDtypeStruct((slots, ROWS_B, LANES), jnp.float32),
    )
    held = (
        jax.ShapeDtypeStruct((2, 2, 2 * far, deep, LANES), jnp.bfloat16),
        jax.ShapeDtypeStruct((2, 2, 2 * (far + REACH), deep, LANES), jnp.bfloat16),
        jax.ShapeDtypeStruct((own, mask_rows, LANES), jnp.bfloat16),
    )
    scratch = [
        pltpu.VMEM((2, 2, planes + 2 * PAD_A, deep, LANES), jnp.bfloat16),
        pltpu.VMEM((2, 2, planes + 2 * PAD_B, deep, LANES), jnp.bfloat16),
        pltpu.VMEM((slots, mask_rows, LANES), jnp.bfloat16),
        pltpu.VMEM((FIELDS, LANES), jnp.int32),
        pltpu.SMEM((FIELDS, LANES), jnp.int32),
        pltpu.SMEM((3 * own * (W // CHUNK) + PAIR,), jnp.int32),
    ]
    held = pl.pallas_call(
        inner_kernel,
        out_shape=(*held, *state),
        in_specs=[vmem] * 3,
        out_specs=(vmem,) * 6,
        scratch_shapes=[
            *scratch,
            pltpu.SemaphoreType.DMA,
            pltpu.SemaphoreType.DMA((5,)),
        ],
        compiler_params=limit(20),
        cost_estimate=busy,
        name="inner_sums",
    )(plan, first, second)
    sums, *_ = pl.pallas_call(
        outer_kernel,
        out_shape=(jax.ShapeDtypeStruct((24, LANES), jnp.float32), *state),
        in_specs=[vmem] * 10,
        out_specs=(vmem,) * 4,
        input_output_aliases={7 + i: 1 + i for i in range(3)},
        scratch_shapes=[
            *scratch,
            pltpu.SMEM((slots + CLOSE,), jnp.int32),
            pltpu.SemaphoreType.DMA,
            pltpu.SemaphoreType.DMA((5,)),
        ],
        compiler_params=limit(20),
        name="outer_sums",
    )(plan, from_pair, from_other, gap, *held)
    other_sums = lax.ppermute(sums, "span", others)
    pair_sums = lax.ppermute(sums, "span", pairs)
    field = pl.pallas_call(
        functools.partial(update_kernel, own),
        out_shape=jax.ShapeDtypeStruct((planes // STRIDE, 3, GZX), jnp.float32),
        in_specs=[vmem] * 3,
        out_specs=vmem,
        compiler_params=limit(4),
        name="smoothed_update",
    )(sums, pair_sums, other_sums)
    return jnp.transpose(field, (1, 0, 2))


def solution(mesh):
    in_specs = (
        P(("grp", "span"), None, None),
        P(("grp", "span"), None, None),
        P(("grp", "span")),
        P(None, ("grp", "span")),
    )
    out_specs = P(None, ("grp", "span"), None)
    return jax.shard_map(shards, mesh=mesh, in_specs=in_specs, out_specs=out_specs, check_vma=False)
```

time: 31.6 us -> 29.9 us (0.946)
  the two profiles are of different devices: /device:TPU:23 before, /device:TPU:21 now
where the time goes in v5:
time: 29.9 us; the launch traced here: 29.5 us
  Pallas kernels  17.8 us (60%)
  starting transfers between devices  6.09 us (20%)
  waiting for transfers between devices  3.87 us (13%)
  local copies, waits for them, and re-layouts  1.71 us (6%)
    pallas_call x1, Pallas kernels, shards(): pl.pallas_call(inner_kernel, out_shape=(*held, *state), in_specs=[vmem] *...  8.77 us
    pallas_call x1, Pallas kernels, shards(): pl.pallas_call(outer_kernel, out_shape=(jax.ShapeDtypeStruct((24, LANES),...  7.6 us
    ppermute x1, waiting for transfers between devices, shards(): other_sums = lax.ppermute(sums, 'span', others)  3.86 us
    ppermute x1, starting transfers between devices, shards(): from_other = lax.ppermute(to_other, 'span', others)  3.31 us
    ppermute x1, starting transfers between devices, shards(): other_sums = lax.ppermute(sums, 'span', others)  1.92 us
    pallas_call x1, Pallas kernels, shards(): pl.pallas_call(functools.partial(update_kernel, own), out_shape=jax.Shape...  1.33 us
    slice x1, local copies, waits for them, and re-layouts, shards(): low_planes, high_planes = (second[:REACH], second[planes - REACH:])  1.05 us
    ppermute x1, starting transfers between devices, shards(): from_pair = lax.ppermute(to_pair, 'span', pairs)  0.74 us
  transfers between devices with their start and end apart: 4, of which 1 were waited for; matrix products, arithmetic and copies ran while one was open for 0% of the time, Pallas kernels for 30%

profile of v5, /device:TPU:21, one launch (start us, length us, event | category | flops | bytes accessed | tf_op | source)
XLA Modules:
  0.0 29.5 jit_solution(4974904816420786096)
XLA Ops:
  0.0 1.0 %fusion = (bf16[4,96,192]{2,1,0:T(8,128)(2,1)S(1)}, bf16[4,96,192]{2,1,0:T(8,128)(2,1)S(1)}) fusion(bf16[60,96,192]{2,1,0:T(8,128)(2,1)} %second_ref.1), kind=kLoop, calls=%fused_computation | loop fusion | bytes 589824 | tf_op jit(solution)/shard_map/slice | solution.py:529
  1.1 0.0 copy-start.2
  1.1 0.0 copy-start.3
  1.1 0.6 %copy-done.2 = s32[3,8]{1,0:T(4,128)S(1)} copy-done((s32[3,8]{1,0:T(4,128)S(1)}, s32[3,8]{1,0:T(4,128)}, u32[]{:S(2)}) %copy-start.2) | copy-done | bytes 120
  1.7 0.0 copy-done.3
  1.7 0.0 copy-start
  1.7 0.0 copy-start.1
  1.8 0.7 %collective-permute-start = (bf16[400,192]{1,0:T(8,128)(2,1)S(1)}, bf16[400,192]{1,0:T(8,128)(2,1)S(1)}, u32[]{:S(2)}, u32[]{:S(2)}) collective-permute-start(bf16[400,192]{1,0:T(8,128)(2,1)S(1)} %get-tuple-element.16), channel_id=1, source_target_pairs={{0,1},{1,0},{2,3},{3,2},{4,5},{5,4},{6,7},{7,6},{8,9},{9,8},{10,11... | collective-permute-start | bytes 460808 | tf_op jit(solution)/shard_map/ppermute | solution.py:550
  2.5 3.3 %collective-permute-start.1 = (bf16[400,192]{1,0:T(8,128)(2,1)S(1)}, bf16[400,192]{1,0:T(8,128)(2,1)S(1)}, u32[]{:S(2)}, u32[]{:S(2)}) collective-permute-start(bf16[400,192]{1,0:T(8,128)(2,1)S(1)} %get-tuple-element.17), channel_id=1, source_target_pairs={{1,2},{3,4},{5,6},{7,8},{9,10},{11,12},{13,14},{2,1},{4,3},{6,5},{... | collective-permute-start | bytes 460808 | tf_op jit(solution)/shard_map/ppermute | solution.py:549
  5.8 0.0 copy-done
  5.9 0.0 copy-done.1
  5.9 8.8 %inner_sums.1 = (bf16[2,2,36,96,128]{4,3,2,1,0:T(8,128)(2,1)S(1)}, bf16[2,2,44,96,128]{4,3,2,1,0:T(8,128)(2,1)S(1)}, bf16[8,320,128]{2,1,0:T(8,128)(2,1)S(1)}, f...) custom-call(s32[8,128]{1,0:T(8,128)S(1)} %get-tuple-element.15.plan_ref, ...), custom_call_target="tpu_custom_call" | custom-call | flops 20000000000 | tf_op jit(solution)/shard_map/inner_sums/pallas_call | solution.py:571
  14.6 0.0 collective-permute-done.pair_ref
  14.7 0.0 collective-permute-done.1.other_ref
  14.7 7.6 %outer_sums.1 = (f32[24,128]{1,0:T(8,128)S(1)}, f32[25,208,256]{2,1,0:T(8,128)S(1)}, f32[25,64,128]{2,1,0:T(8,128)S(1)}, f32[25,80,128]{2,1,0:T(8,128)S(1)}) custom-call(s32[8,128]{1,0:T(8,128)S(1)} %get-tuple-element.15.plan_ref, bf16[400,192]{1,0:T(8,128)(2,1)S(1)} %collective-permute-done.pair_ref, ...), custom_call_target="tpu_custom_call", output_to_operand_aliasing={{1}: (7, {}), {2}: (8, {}), {3}: (9, {})} | custom-call | tf_op jit(solution)/shard_map/outer_sums/pallas_call | solution.py:585
  22.3 1.9 %collective-permute-start.3 = (f32[24,128]{1,0:T(8,128)S(1)}, f32[24,128]{1,0:T(8,128)S(1)}, u32[]{:S(2)}, u32[]{:S(2)}) collective-permute-start(f32[24,128]{1,0:T(8,128)S(1)} %get-tuple-element.24.mine_ref), channel_id=1, source_target_pairs={{1,2},{3,4},{5,6},{7,8},{9,10},{11,12},{13,14},{2,1},{4,3},{6,5},{... | collective-permute-start | bytes 36872 | tf_op jit(solution)/shard_map/ppermute | solution.py:600
  24.2 0.1 collective-permute-start.2
  24.3 3.9 %collective-permute-done.3.other_ref = f32[24,128]{1,0:T(8,128)S(1)} collective-permute-done((f32[24,128]{1,0:T(8,128)S(1)}, f32[24,128]{1,0:T(8,128)S(1)}, u32[]{:S(2)}, u32[]{:S(2)}) %collective-permute-start.3) | collective-permute-done | bytes 12320 | tf_op jit(solution)/shard_map/ppermute | solution.py:600
  28.2 0.0 collective-permute-done.2.pair_ref
  28.2 1.3 %smoothed_update.1 = f32[5,3,128]{2,1,0:T(4,128)} custom-call(f32[24,128]{1,0:T(8,128)S(1)} %get-tuple-element.24.mine_ref, f32[24,128]{1,0:T(8,128)S(1)} %collective-permute-done.2.pair_ref, f32[24,128]{1,0:T(8,128)S(1)} %collective-permute-done.3.other_ref), custom_call_target="tpu_custom_call" | custom-call | tf_op jit(solution)/shard_map/smoothed_update/pallas_call | solution.py:602
  (2 shorter events, 0.1 us)
Async XLA Ops:
  1.1 0.7 %copy-start.2 = (s32[3,8]{1,0:T(4,128)S(1)}, s32[3,8]{1,0:T(4,128)}, u32[]{:S(2)}) copy-start(s32[3,8]{1,0:T(4,128)} %shift_ref.1) | copy-start | bytes 292
  1.1 0.7 %copy-start.3 = (s32[8]{0:T(128)S(1)}, s32[8]{0:T(128)}, u32[]{:S(2)}) copy-start(s32[8]{0:T(128)} %param.6) | copy-start | bytes 100
  1.7 4.1 %copy-start = (bf16[60,96,192]{2,1,0:T(8,128)(2,1)S(1)}, bf16[60,96,192]{2,1,0:T(8,128)(2,1)}, u32[]{:S(2)}) copy-start(bf16[60,96,192]{2,1,0:T(8,128)(2,1)} %second_ref.1) | copy-start | bytes 6635524
  1.7 4.1 %copy-start.1 = (bf16[60,96,192]{2,1,0:T(8,128)(2,1)S(1)}, bf16[60,96,192]{2,1,0:T(8,128)(2,1)}, u32[]{:S(2)}) copy-start(bf16[60,96,192]{2,1,0:T(8,128)(2,1)} %first_ref.1) | copy-start | bytes 6635524
  1.8 12.9 %collective-permute-start = (bf16[400,192]{1,0:T(8,128)(2,1)S(1)}, bf16[400,192]{1,0:T(8,128)(2,1)S(1)}, u32[]{:S(2)}, u32[]{:S(2)}) collective-permute-start(bf16[400,192]{1,0:T(8,128)(2,1)S(1)} %get-tuple-element.16), channel_id=1, source_target_pairs={{0,1},{1,0},{2,3},{3,2},{4,5},{5,4},{6,7},{7,6},{8,9},{9,8},{10,11... | collective-permute-start | bytes 460808 | tf_op jit(solution)/shard_map/ppermute | solution.py:550
  2.5 12.1 %collective-permute-start.1 = (bf16[400,192]{1,0:T(8,128)(2,1)S(1)}, bf16[400,192]{1,0:T(8,128)(2,1)S(1)}, u32[]{:S(2)}, u32[]{:S(2)}) collective-permute-start(bf16[400,192]{1,0:T(8,128)(2,1)S(1)} %get-tuple-element.17), channel_id=1, source_target_pairs={{1,2},{3,4},{5,6},{7,8},{9,10},{11,12},{13,14},{2,1},{4,3},{6,5},{... | collective-permute-start | bytes 460808 | tf_op jit(solution)/shard_map/ppermute | solution.py:549
  22.3 5.9 %collective-permute-start.3 = (f32[24,128]{1,0:T(8,128)S(1)}, f32[24,128]{1,0:T(8,128)S(1)}, u32[]{:S(2)}, u32[]{:S(2)}) collective-permute-start(f32[24,128]{1,0:T(8,128)S(1)} %get-tuple-element.24.mine_ref), channel_id=1, source_target_pairs={{1,2},{3,4},{5,6},{7,8},{9,10},{11,12},{13,14},{2,1},{4,3},{6,5},{... | collective-permute-start | bytes 36872 | tf_op jit(solution)/shard_map/ppermute | solution.py:600
  24.2 4.0 %collective-permute-start.2 = (f32[24,128]{1,0:T(8,128)S(1)}, f32[24,128]{1,0:T(8,128)S(1)}, u32[]{:S(2)}, u32[]{:S(2)}) collective-permute-start(f32[24,128]{1,0:T(8,128)S(1)} %get-tuple-element.24.mine_ref), channel_id=1, source_target_pairs={{0,1},{1,0},{2,3},{3,2},{4,5},{5,4},{6,7},{7,6},{8,9},{9,8},{10,11... | collective-permute-start | bytes 36872 | tf_op jit(solution)/shard_map/ppermute | solution.py:601

commit v6 on v5

--- a/solution.py
+++ b/solution.py
@@ -35,7 +35,7 @@
 FAR = 4096
 
 
-def table_kernel(low_ref, gap_ref):
+def table_kernel(gap_ref):
     row = lax.broadcasted_iota(jnp.int32, gap_ref.shape, 0)
     col = lax.broadcasted_iota(jnp.int32, gap_ref.shape, 1)
     lag = jnp.where(col >= ROWS_B, 1, 0) + jnp.where(col >= 2 * ROWS_B, 1, 0)
@@ -164,11 +164,9 @@
             at += rows
 
 
-def set_units(units, total, s, low, count, most):
+def set_units(units, total, s, low, planes, most):
     for c in range(most):
-        both = jnp.where(2 * c + 1 < count, 1, 0)
-        units[total + c] = s + (low + 2 * CHUNK * c + 64) * 256 + both * 65536
-    return total + ((count + 1) >> 1)
+        units[total + c] = s + (low + planes * c + 64) * 256
 
 
 def frame(v, fr, at):
@@ -180,21 +178,19 @@
     fr[1, 1, at] = pltpu.roll(high, HOP, 1)
 
 
-def run_units(total, units, table, spare, fr_a, fr_b, acc, sq_a, sq_b, masks):
+def run_units(half, total, units, table, spare, fr_a, fr_b, acc, sq_a, sq_b, masks):
     for at in range(REST - 1):
         units[total + at] = spare + 64 * 256
     ones = jnp.where(
-        lax.broadcasted_iota(jnp.int32, (16, CHUNK * LANES), 0) == 0, 1.0, 0.0
+        lax.broadcasted_iota(jnp.int32, (16, half * LANES), 0) == 0, 1.0, 0.0
     ).astype(jnp.bfloat16)
 
     def step(first, width):
         for h in range(width):
             code = units[first + h]
             s = code & 255
-            y = ((code >> 8) & 255) - 64
-            both = code >> 16
-            y_two = y + both * CHUNK
-            keep = both.astype(jnp.float32).astype(jnp.bfloat16)
+            y = (code >> 8) - 64
+            y_two = y + half
             f_a = table[0, s]
             z_a = pl.multiple_of(table[1, s], 16)
             f_b = table[2, s]
@@ -202,30 +198,30 @@
             dy = table[4, s]
             dx = table[6, s]
             one_a = masks[s, 0:ROWS_A]
-            two_a = masks[s, ROWS_A:2 * ROWS_A] * keep
+            two_a = masks[s, ROWS_A:2 * ROWS_A]
             at = 2 * ROWS_A
             one_b = masks[s, at:at + ROWS_B]
-            two_b = masks[s, at + ROWS_B:at + 2 * ROWS_B] * keep
+            two_b = masks[s, at + ROWS_B:at + 2 * ROWS_B]
             at += 2 * ROWS_B
-            rows = masks[s, at:at + 16] + masks[s, at + 16:at + 32] * keep
+            rows = masks[s, at:at + 16] + masks[s, at + 16:at + 32]
             a = [
                 fr_a[0, f_a, y + PAD_A + p, pl.ds(z_a, ROWS_A), :] * one_a
                 + fr_a[1, f_a, y_two + PAD_A + p, pl.ds(z_a, ROWS_A), :] * two_a
-                for p in range(CHUNK)
+                for p in range(half)
             ]
             b = [
                 fr_b[0, f_b, y + dy - 1 + PAD_B + p, pl.ds(z_b, ROWS_B), :] * one_b
                 + fr_b[1, f_b, y_two + dy - 1 + PAD_B + p, pl.ds(z_b, ROWS_B), :] * two_b
-                for p in range(CHUNK + 2)
+                for p in range(half + 2)
             ]
             left = [
                 jnp.concatenate(
                     [pltpu.roll(v, (dx + lag - 1 + LANES) & (LANES - 1), 1) for v in a], axis=1)
                 for lag in range(3)
             ]
-            left.append(jnp.concatenate([rows] * CHUNK, axis=1))
+            left.append(jnp.concatenate([rows] * half, axis=1))
             left = jnp.concatenate(left, axis=0)
-            right = [jnp.concatenate(b[lag:lag + CHUNK], axis=1) for lag in range(3)]
+            right = [jnp.concatenate(b[lag:lag + half], axis=1) for lag in range(3)]
             right = jnp.concatenate(right + [ones], axis=0)
             acc[s] += lax.dot_general(
                 left, right, (((1,), (1,)), ((), ())), preferred_element_type=jnp.float32)
@@ -290,12 +286,13 @@
         set_masks(masks, s, table)
         for ref in (acc, sq_a, sq_b):
             ref[s] = jnp.zeros(ref.shape[1:], jnp.float32)
-        return set_units(units, total, s, table[12, s], table[13, s], W // CHUNK // 2)
+        set_units(units, total, s, table[12, s], 2 * CHUNK, W // CHUNK // 2)
+        return total + (table[13, s] >> 1)
 
     total = lax.fori_loop(0, own, prepare, 0)
     masks_on = pltpu.make_async_copy(masks.at[pl.ds(0, own)], edge_masks, sem_e.at[4])
     masks_on.start()
-    run_units(total, units, table, 3 * own, fr_a, fr_b, acc, sq_a, sq_b, masks)
+    run_units(CHUNK, total, units, table, 3 * own, fr_a, fr_b, acc, sq_a, sq_b, masks)
     for c in hand_on:
         c.wait()
     masks_on.wait()
@@ -350,7 +347,8 @@
 
     def prepare_own(s, total):
         active[s] = s
-        return set_units(units, total, s, table[12, s], table[13, s], 1)
+        set_units(units, total, s, table[12, s], CHUNK, 2)
+        return total + table[13, s]
 
     total = lax.fori_loop(0, own, prepare_own, 0)
     for c in bring_in:
@@ -366,15 +364,15 @@
             for ref in (acc, sq_a, sq_b):
                 ref[s] = jnp.zeros(ref.shape[1:], jnp.float32)
             active[alive] = s
-            set_units(units, total, s, table[12, s], count, 2)
-
-        return total + ((count + 1) >> 1), alive + jnp.where(count > 0, 1, 0)
+            set_units(units, total, s, table[12, s], CHUNK, W // CHUNK)
+
+        return total + count, alive + jnp.where(count > 0, 1, 0)
 
     total, alive = lax.fori_loop(own, 3 * own, prepare, (total, own))
     spare = 3 * own
     for at in range(CLOSE - 1):
         active[alive + at] = spare
-    run_units(total, units, table, spare, fr_a, fr_b, acc, sq_a, sq_b, masks)
+    run_units(CHUNK // 2, total, units, table, spare, fr_a, fr_b, acc, sq_a, sq_b, masks)
 
     cols = 2 * LANES
     col_one = lax.broadcasted_iota(jnp.int32, (1, cols), 1)
@@ -526,17 +524,17 @@
         return pltpu.CompilerParams(vmem_limit_bytes=mib << 20)
 
     busy = pl.CostEstimate(flops=20 * 10**9, bytes_accessed=0, transcendentals=0)
-    low_planes, high_planes = second[:REACH], second[planes - REACH:]
     gap = pl.pallas_call(
         table_kernel,
         out_shape=jax.ShapeDtypeStruct((ROWS_A, 2 * LANES), jnp.int32),
-        in_specs=[vmem],
         out_specs=vmem,
         compiler_params=limit(4),
-        cost_estimate=busy,
+        cost_estimate=pl.CostEstimate(flops=800000000, bytes_accessed=0, transcendentals=0),
         name="gap_table",
-    )(low_planes)
+    )()
     message = jax.ShapeDtypeStruct((REACH * deep + PLAN_ROWS, along), second.dtype)
+    tile, gap = lax.optimization_barrier((second, gap))
+    low_planes, high_planes = tile[:REACH], tile[planes - REACH:]
     to_pair, to_other, plan = pl.pallas_call(
         send_kernel,
         out_shape=(message, message, jax.ShapeDtypeStruct((8, LANES), jnp.int32)),
@@ -566,7 +564,7 @@
         pltpu.VMEM((slots, mask_rows, LANES), jnp.bfloat16),
         pltpu.VMEM((FIELDS, LANES), jnp.int32),
         pltpu.SMEM((FIELDS, LANES), jnp.int32),
-        pltpu.SMEM((3 * own * (W // CHUNK) + PAIR,), jnp.int32),
+        pltpu.SMEM(((3 * own + 1) * (W // CHUNK) + PAIR,), jnp.int32),
     ]
     held = pl.pallas_call(
         inner_kernel,

time: 29.9 us -> 28.7 us (0.960)
  the two profiles are of different devices: /device:TPU:21 before, /device:TPU:7 now
where the time goes in v6:
time: 28.7 us; the launch traced here: 28.5 us
  Pallas kernels  17.4 us (61%)
  starting transfers between devices  6.6 us (23%)
  waiting for transfers between devices  3.35 us (12%)
  local copies, waits for them, and re-layouts  1.08 us (4%)
    pallas_call x1, Pallas kernels, shards(): pl.pallas_call(outer_kernel, out_shape=(jax.ShapeDtypeStruct((24, LANES),...  8.13 us
    pallas_call x1, Pallas kernels, shards(): pl.pallas_call(inner_kernel, out_shape=(*held, *state), in_specs=[vmem] *...  7.85 us
    ppermute x1, waiting for transfers between devices, shards(): other_sums = lax.ppermute(sums, 'span', others)  3.34 us
    ppermute x1, starting transfers between devices, shards(): from_other = lax.ppermute(to_other, 'span', others)  3.31 us
    ppermute x1, starting transfers between devices, shards(): other_sums = lax.ppermute(sums, 'span', others)  2.48 us
    pallas_call x1, Pallas kernels, shards(): pl.pallas_call(functools.partial(update_kernel, own), out_shape=jax.Shape...  1.33 us
    slice x1, local copies, waits for them, and re-layouts, shards(): low_planes, high_planes = (tile[:REACH], tile[planes - REACH:])  1.06 us
    ppermute x1, starting transfers between devices, shards(): from_pair = lax.ppermute(to_pair, 'span', pairs)  0.74 us
  transfers between devices with their start and end apart: 4, of which 1 were waited for; matrix products, arithmetic and copies ran while one was open for 0% of the time, Pallas kernels for 28%

profile of v6, /device:TPU:7, one launch (start us, length us, event | category | flops | bytes accessed | tf_op | source)
XLA Modules:
  0.0 28.5 jit_solution(16808645731249863380)
XLA Ops:
  0.0 0.0 copy-start.2
  0.0 0.0 copy-start.3
  0.0 1.1 %fusion = (bf16[4,96,192]{2,1,0:T(8,128)(2,1)S(1)}, bf16[4,96,192]{2,1,0:T(8,128)(2,1)S(1)}) fusion(bf16[60,96,192]{2,1,0:T(8,128)(2,1)} %second_ref.1), kind=kLoop, calls=%fused_computation | loop fusion | bytes 589824 | tf_op jit(solution)/shard_map/slice | solution.py:537
  1.1 0.0 copy-done.2
  1.1 0.0 copy-done.3
  1.1 0.0 copy-start
  1.1 0.0 copy-start.1
  1.2 0.7 %collective-permute-start = (bf16[400,192]{1,0:T(8,128)(2,1)S(1)}, bf16[400,192]{1,0:T(8,128)(2,1)S(1)}, u32[]{:S(2)}, u32[]{:S(2)}) collective-permute-start(bf16[400,192]{1,0:T(8,128)(2,1)S(1)} %get-tuple-element.20), channel_id=1, source_target_pairs={{0,1},{1,0},{2,3},{3,2},{4,5},{5,4},{6,7},{7,6},{8,9},{9,8},{10,11... | collective-permute-start | bytes 460808 | tf_op jit(solution)/shard_map/ppermute | solution.py:548
  1.9 3.3 %collective-permute-start.1 = (bf16[400,192]{1,0:T(8,128)(2,1)S(1)}, bf16[400,192]{1,0:T(8,128)(2,1)S(1)}, u32[]{:S(2)}, u32[]{:S(2)}) collective-permute-start(bf16[400,192]{1,0:T(8,128)(2,1)S(1)} %get-tuple-element.21), channel_id=1, source_target_pairs={{1,2},{3,4},{5,6},{7,8},{9,10},{11,12},{13,14},{2,1},{4,3},{6,5},{... | collective-permute-start | bytes 460808 | tf_op jit(solution)/shard_map/ppermute | solution.py:547
  5.2 0.0 copy-done
  5.2 0.0 copy-done.1
  5.3 7.8 %inner_sums.1 = (bf16[2,2,36,96,128]{4,3,2,1,0:T(8,128)(2,1)S(1)}, bf16[2,2,44,96,128]{4,3,2,1,0:T(8,128)(2,1)S(1)}, bf16[8,320,128]{2,1,0:T(8,128)(2,1)S(1)}, f...) custom-call(s32[8,128]{1,0:T(8,128)S(1)} %get-tuple-element.19.plan_ref, ...), custom_call_target="tpu_custom_call" | custom-call | flops 20000000000 | tf_op jit(solution)/shard_map/inner_sums/pallas_call | solution.py:569
  13.1 0.0 collective-permute-done.pair_ref
  13.1 0.0 collective-permute-done.1.other_ref
  13.1 8.1 %outer_sums.1 = (f32[24,128]{1,0:T(8,128)S(1)}, f32[25,208,256]{2,1,0:T(8,128)S(1)}, f32[25,64,128]{2,1,0:T(8,128)S(1)}, f32[25,80,128]{2,1,0:T(8,128)S(1)}) custom-call(s32[8,128]{1,0:T(8,128)S(1)} %get-tuple-element.19.plan_ref, bf16[400,192]{1,0:T(8,128)(2,1)S(1)} %collective-permute-done.pair_ref, ...), custom_call_target="tpu_custom_call", output_to_operand_aliasing={{1}: (7, {}), {2}: (8, {}), {3}: (9, {})} | custom-call | tf_op jit(solution)/shard_map/outer_sums/pallas_call | solution.py:583
  21.3 2.5 %collective-permute-start.3 = (f32[24,128]{1,0:T(8,128)S(1)}, f32[24,128]{1,0:T(8,128)S(1)}, u32[]{:S(2)}, u32[]{:S(2)}) collective-permute-start(f32[24,128]{1,0:T(8,128)S(1)} %get-tuple-element.28.mine_ref), channel_id=1, source_target_pairs={{1,2},{3,4},{5,6},{7,8},{9,10},{11,12},{13,14},{2,1},{4,3},{6,5},{... | collective-permute-start | bytes 36872 | tf_op jit(solution)/shard_map/ppermute | solution.py:598
  23.8 0.1 collective-permute-start.2
  23.8 3.3 %collective-permute-done.3.other_ref = f32[24,128]{1,0:T(8,128)S(1)} collective-permute-done((f32[24,128]{1,0:T(8,128)S(1)}, f32[24,128]{1,0:T(8,128)S(1)}, u32[]{:S(2)}, u32[]{:S(2)}) %collective-permute-start.3) | collective-permute-done | bytes 12320 | tf_op jit(solution)/shard_map/ppermute | solution.py:598
  27.2 0.0 collective-permute-done.2.pair_ref
  27.2 1.3 %smoothed_update.1 = f32[5,3,128]{2,1,0:T(4,128)} custom-call(f32[24,128]{1,0:T(8,128)S(1)} %get-tuple-element.28.mine_ref, f32[24,128]{1,0:T(8,128)S(1)} %collective-permute-done.2.pair_ref, f32[24,128]{1,0:T(8,128)S(1)} %collective-permute-done.3.other_ref), custom_call_target="tpu_custom_call" | custom-call | tf_op jit(solution)/shard_map/smoothed_update/pallas_call | solution.py:600
  (2 shorter events, 0.1 us)
Async XLA Ops:
  0.0 1.1 %copy-start.2 = (s32[3,8]{1,0:T(4,128)S(1)}, s32[3,8]{1,0:T(4,128)}, u32[]{:S(2)}) copy-start(s32[3,8]{1,0:T(4,128)} %shift_ref.1) | copy-start | bytes 292
  0.0 1.1 %copy-start.3 = (s32[8]{0:T(128)S(1)}, s32[8]{0:T(128)}, u32[]{:S(2)}) copy-start(s32[8]{0:T(128)} %param.6) | copy-start | bytes 100
  1.1 4.1 %copy-start = (bf16[60,96,192]{2,1,0:T(8,128)(2,1)S(1)}, bf16[60,96,192]{2,1,0:T(8,128)(2,1)}, u32[]{:S(2)}) copy-start(bf16[60,96,192]{2,1,0:T(8,128)(2,1)} %second_ref.1) | copy-start | bytes 6635524
  1.1 4.1 %copy-start.1 = (bf16[60,96,192]{2,1,0:T(8,128)(2,1)S(1)}, bf16[60,96,192]{2,1,0:T(8,128)(2,1)}, u32[]{:S(2)}) copy-start(bf16[60,96,192]{2,1,0:T(8,128)(2,1)} %first_ref.1) | copy-start | bytes 6635524
  1.2 11.9 %collective-permute-start = (bf16[400,192]{1,0:T(8,128)(2,1)S(1)}, bf16[400,192]{1,0:T(8,128)(2,1)S(1)}, u32[]{:S(2)}, u32[]{:S(2)}) collective-permute-start(bf16[400,192]{1,0:T(8,128)(2,1)S(1)} %get-tuple-element.20), channel_id=1, source_target_pairs={{0,1},{1,0},{2,3},{3,2},{4,5},{5,4},{6,7},{7,6},{8,9},{9,8},{10,11... | collective-permute-start | bytes 460808 | tf_op jit(solution)/shard_map/ppermute | solution.py:548
  1.9 11.2 %collective-permute-start.1 = (bf16[400,192]{1,0:T(8,128)(2,1)S(1)}, bf16[400,192]{1,0:T(8,128)(2,1)S(1)}, u32[]{:S(2)}, u32[]{:S(2)}) collective-permute-start(bf16[400,192]{1,0:T(8,128)(2,1)S(1)} %get-tuple-element.21), channel_id=1, source_target_pairs={{1,2},{3,4},{5,6},{7,8},{9,10},{11,12},{13,14},{2,1},{4,3},{6,5},{... | collective-permute-start | bytes 460808 | tf_op jit(solution)/shard_map/ppermute | solution.py:547
  21.3 5.9 %collective-permute-start.3 = (f32[24,128]{1,0:T(8,128)S(1)}, f32[24,128]{1,0:T(8,128)S(1)}, u32[]{:S(2)}, u32[]{:S(2)}) collective-permute-start(f32[24,128]{1,0:T(8,128)S(1)} %get-tuple-element.28.mine_ref), channel_id=1, source_target_pairs={{1,2},{3,4},{5,6},{7,8},{9,10},{11,12},{13,14},{2,1},{4,3},{6,5},{... | collective-permute-start | bytes 36872 | tf_op jit(solution)/shard_map/ppermute | solution.py:598
  23.8 3.4 %collective-permute-start.2 = (f32[24,128]{1,0:T(8,128)S(1)}, f32[24,128]{1,0:T(8,128)S(1)}, u32[]{:S(2)}, u32[]{:S(2)}) collective-permute-start(f32[24,128]{1,0:T(8,128)S(1)} %get-tuple-element.28.mine_ref), channel_id=1, source_target_pairs={{0,1},{1,0},{2,3},{3,2},{4,5},{5,4},{6,7},{7,6},{8,9},{9,8},{10,11... | collective-permute-start | bytes 36872 | tf_op jit(solution)/shard_map/ppermute | solution.py:599

commit v7 on v6

--- a/solution.py
+++ b/solution.py
@@ -242,25 +242,14 @@
         step(PAIR * full, REST)
 
 
-def edge_copies(edge_a, edge_b, fr_a, fr_b, planes, sem):
-    far_a = edge_a.shape[2] // 2
-    far_b = edge_b.shape[2] // 2
-    return (
-        (fr_a.at[:, :, pl.ds(PAD_A, far_a)], edge_a.at[:, :, pl.ds(0, far_a)], sem.at[0]),
-        (fr_a.at[:, :, pl.ds(PAD_A + planes - far_a, far_a)],
-         edge_a.at[:, :, pl.ds(far_a, far_a)], sem.at[1]),
-        (fr_b.at[:, :, pl.ds(PAD_B, far_b)], edge_b.at[:, :, pl.ds(0, far_b)], sem.at[2]),
-        (fr_b.at[:, :, pl.ds(PAD_B + planes - far_b, far_b)],
-         edge_b.at[:, :, pl.ds(far_b, far_b)], sem.at[3]),
-    )
-
-
 def inner_kernel(
-    plan_ref, first_ref, second_ref, edge_a, edge_b, edge_masks, acc, sq_a, sq_b,
-    fr_a, fr_b, masks, table_v, table, units, sem_t, sem_e,
+    plan_ref, first_ref, second_ref, fr_a, fr_b, masks, acc, sq_a, sq_b,
+    table_v, table, units, sem_t,
 ):
     planes, deep, along = first_ref.shape
     own = (acc.shape[0] - 1) // 3
+    device = lax.axis_index("span")
+    last = lax.axis_size("span") - 1
     piece = planes // PIECES
     decode(plan_ref[...], own, planes, deep, True, table_v)
     to_scalar = pltpu.make_async_copy(table_v, table, sem_t)
@@ -274,12 +263,14 @@
 
         lax.fori_loop(0, PIECES, body, 0)
 
-    hand_on = [
-        pltpu.make_async_copy(source, target, sem)
-        for source, target, sem in edge_copies(edge_a, edge_b, fr_a, fr_b, planes, sem_e)
-    ]
-    for c in hand_on:
-        c.start()
+    @pl.when((device == 0) | (device == last))
+    def _():
+        zero = jnp.zeros((2, 2, CHUNK, deep, LANES), jnp.bfloat16)
+        fr_a[:, :, 0:PAD_A] = zero
+        fr_a[:, :, PAD_A + planes:] = zero
+        fr_b[:, :, 0:CHUNK] = zero
+        fr_b[:, :, PAD_B + planes + REACH:] = zero
+
     to_scalar.wait()
 
     def prepare(s, total):
@@ -290,32 +281,18 @@
         return total + (table[13, s] >> 1)
 
     total = lax.fori_loop(0, own, prepare, 0)
-    masks_on = pltpu.make_async_copy(masks.at[pl.ds(0, own)], edge_masks, sem_e.at[4])
-    masks_on.start()
     run_units(CHUNK, total, units, table, 3 * own, fr_a, fr_b, acc, sq_a, sq_b, masks)
-    for c in hand_on:
-        c.wait()
-    masks_on.wait()
 
 
 def outer_kernel(
-    plan_ref, pair_ref, other_ref, gap_base, edge_a, edge_b, edge_masks, acc_in, sq_a_in, sq_b_in,
-    out_ref, acc, sq_a, sq_b,
-    fr_a, fr_b, masks, table_v, table, units, active, sem_t, sem_e,
+    plan_ref, pair_ref, other_ref, gap_base, fr_a, fr_b_in, masks_in, acc_in, sq_a_in, sq_b_in,
+    out_ref, fr_b, masks, acc, sq_a, sq_b, table_v, table, units, active, sem_t,
 ):
     deep = fr_a.shape[3]
     planes = fr_a.shape[2] - 2 * PAD_A
     own = (acc.shape[0] - 1) // 3
-    device = lax.axis_index("span")
-    last = lax.axis_size("span") - 1
-    even = device % 2 == 0
+    even = lax.axis_index("span") % 2 == 0
     base = REACH * deep
-    bring_in = [
-        pltpu.make_async_copy(source, target, sem)
-        for target, source, sem in edge_copies(edge_a, edge_b, fr_a, fr_b, planes, sem_e)
-    ] + [pltpu.make_async_copy(edge_masks, masks.at[pl.ds(0, own)], sem_e.at[4])]
-    for c in bring_in:
-        c.start()
     from_pair, from_other = [
         ref[base:base + 8, 0:LANES].astype(jnp.float32).astype(jnp.int32)
         for ref in (pair_ref, other_ref)
@@ -329,14 +306,6 @@
     out_ref[...] = jnp.zeros(out_ref.shape, jnp.float32)
     out_ref[22:23] = target.astype(jnp.float32)
 
-    @pl.when((device == 0) | (device == last))
-    def _():
-        zero = jnp.zeros((2, 2, CHUNK, deep, LANES), jnp.bfloat16)
-        fr_a[:, :, 0:PAD_A] = zero
-        fr_a[:, :, PAD_A + planes:] = zero
-        fr_b[:, :, 0:CHUNK] = zero
-        fr_b[:, :, PAD_B + planes + REACH:] = zero
-
     low_at, high_at = CHUNK, PAD_B + planes
     pair_at = jnp.where(even, high_at, low_at)
     other_at = jnp.where(even, low_at, high_at)
@@ -351,8 +320,6 @@
         return total + table[13, s]
 
     total = lax.fori_loop(0, own, prepare_own, 0)
-    for c in bring_in:
-        c.wait()
 
     def prepare(s, carry):
         total, alive = carry
@@ -529,7 +496,7 @@
         out_shape=jax.ShapeDtypeStruct((ROWS_A, 2 * LANES), jnp.int32),
         out_specs=vmem,
         compiler_params=limit(4),
-        cost_estimate=pl.CostEstimate(flops=800000000, bytes_accessed=0, transcendentals=0),
+        cost_estimate=pl.CostEstimate(flops=13 * 10**8, bytes_accessed=0, transcendentals=0),
         name="gap_table",
     )()
     message = jax.ShapeDtypeStruct((REACH * deep + PLAN_ROWS, along), second.dtype)
@@ -547,36 +514,26 @@
     from_other = lax.ppermute(to_other, "span", others)
     from_pair = lax.ppermute(to_pair, "span", pairs)
     mask_rows = 2 * (ROWS_A + ROWS_B + 16)
-    far = W // 2 - STRIDE // 2
+    frames_a = jax.ShapeDtypeStruct((2, 2, planes + 2 * PAD_A, deep, LANES), jnp.bfloat16)
     state = (
+        jax.ShapeDtypeStruct((2, 2, planes + 2 * PAD_B, deep, LANES), jnp.bfloat16),
+        jax.ShapeDtypeStruct((slots, mask_rows, LANES), jnp.bfloat16),
         jax.ShapeDtypeStruct((slots, 3 * ROWS_A + 16, 2 * LANES), jnp.float32),
         jax.ShapeDtypeStruct((slots, ROWS_A, LANES), jnp.float32),
         jax.ShapeDtypeStruct((slots, ROWS_B, LANES), jnp.float32),
     )
-    held = (
-        jax.ShapeDtypeStruct((2, 2, 2 * far, deep, LANES), jnp.bfloat16),
-        jax.ShapeDtypeStruct((2, 2, 2 * (far + REACH), deep, LANES), jnp.bfloat16),
-        jax.ShapeDtypeStruct((own, mask_rows, LANES), jnp.bfloat16),
-    )
     scratch = [
-        pltpu.VMEM((2, 2, planes + 2 * PAD_A, deep, LANES), jnp.bfloat16),
-        pltpu.VMEM((2, 2, planes + 2 * PAD_B, deep, LANES), jnp.bfloat16),
-        pltpu.VMEM((slots, mask_rows, LANES), jnp.bfloat16),
         pltpu.VMEM((FIELDS, LANES), jnp.int32),
         pltpu.SMEM((FIELDS, LANES), jnp.int32),
         pltpu.SMEM(((3 * own + 1) * (W // CHUNK) + PAIR,), jnp.int32),
     ]
     held = pl.pallas_call(
         inner_kernel,
-        out_shape=(*held, *state),
+        out_shape=(frames_a, *state),
         in_specs=[vmem] * 3,
         out_specs=(vmem,) * 6,
-        scratch_shapes=[
-            *scratch,
-            pltpu.SemaphoreType.DMA,
-            pltpu.SemaphoreType.DMA((5,)),
-        ],
-        compiler_params=limit(20),
+        scratch_shapes=[*scratch, pltpu.SemaphoreType.DMA],
+        compiler_params=limit(8),
         cost_estimate=busy,
         name="inner_sums",
     )(plan, first, second)
@@ -584,15 +541,11 @@
         outer_kernel,
         out_shape=(jax.ShapeDtypeStruct((24, LANES), jnp.float32), *state),
         in_specs=[vmem] * 10,
-        out_specs=(vmem,) * 4,
-        input_output_aliases={7 + i: 1 + i for i in range(3)},
+        out_specs=(vmem,) * 6,
+        input_output_aliases={5 + i: 1 + i for i in range(5)},
         scratch_shapes=[
-            *scratch,
-            pltpu.SMEM((slots + CLOSE,), jnp.int32),
-            pltpu.SemaphoreType.DMA,
-            pltpu.SemaphoreType.DMA((5,)),
-        ],
-        compiler_params=limit(20),
+            *scratch, pltpu.SMEM((slots + CLOSE,), jnp.int32), pltpu.SemaphoreType.DMA],
+        compiler_params=limit(8),
         name="outer_sums",
     )(plan, from_pair, from_other, gap, *held)
     other_sums = lax.ppermute(sums, "span", others)

time: 28.7 us -> 27 us (0.941)
  the two profiles are of different devices: /device:TPU:7 before, /device:TPU:21 now
where the time goes in v7:
time: 27 us; the launch traced here: 26.8 us
  Pallas kernels  15.7 us (58%)
  starting transfers between devices  6.04 us (22%)
  waiting for transfers between devices  3.91 us (14%)
  local copies, waits for them, and re-layouts  1.08 us (4%)
    pallas_call x1, Pallas kernels, shards(): pl.pallas_call(inner_kernel, out_shape=(frames_a, *state), in_specs=[vmem...  7.82 us
    pallas_call x1, Pallas kernels, shards(): pl.pallas_call(outer_kernel, out_shape=(jax.ShapeDtypeStruct((24, LANES),...  6.46 us
    ppermute x1, waiting for transfers between devices, shards(): other_sums = lax.ppermute(sums, 'span', others)  3.91 us
    ppermute x1, starting transfers between devices, shards(): from_other = lax.ppermute(to_other, 'span', others)  3.31 us
    ppermute x1, starting transfers between devices, shards(): other_sums = lax.ppermute(sums, 'span', others)  1.92 us
    pallas_call x1, Pallas kernels, shards(): pl.pallas_call(functools.partial(update_kernel, own), out_shape=jax.Shape...  1.33 us
    slice x1, local copies, waits for them, and re-layouts, shards(): low_planes, high_planes = (tile[:REACH], tile[planes - REACH:])  1.06 us
    ppermute x1, starting transfers between devices, shards(): from_pair = lax.ppermute(to_pair, 'span', pairs)  0.74 us
  transfers between devices with their start and end apart: 4, of which 1 were waited for; matrix products, arithmetic and copies ran while one was open for 0% of the time, Pallas kernels for 29%

profile of v7, /device:TPU:21, one launch (start us, length us, event | category | flops | bytes accessed | tf_op | source)
XLA Modules:
  0.0 26.8 jit_solution(971609633120554092)
XLA Ops:
  0.0 0.0 copy-start.2
  0.0 0.0 copy-start.3
  0.0 1.1 %fusion = (bf16[4,96,192]{2,1,0:T(8,128)(2,1)S(1)}, bf16[4,96,192]{2,1,0:T(8,128)(2,1)S(1)}) fusion(bf16[60,96,192]{2,1,0:T(8,128)(2,1)} %second_ref.1), kind=kLoop, calls=%fused_computation | loop fusion | bytes 589824 | tf_op jit(solution)/shard_map/slice | solution.py:504
  1.1 0.0 copy-done.2
  1.1 0.0 copy-done.3
  1.1 0.0 copy-start
  1.1 0.0 copy-start.1
  1.2 0.7 %collective-permute-start = (bf16[400,192]{1,0:T(8,128)(2,1)S(1)}, bf16[400,192]{1,0:T(8,128)(2,1)S(1)}, u32[]{:S(2)}, u32[]{:S(2)}) collective-permute-start(bf16[400,192]{1,0:T(8,128)(2,1)S(1)} %get-tuple-element.20), channel_id=1, source_target_pairs={{0,1},{1,0},{2,3},{3,2},{4,5},{5,4},{6,7},{7,6},{8,9},{9,8},{10,11... | collective-permute-start | bytes 460808 | tf_op jit(solution)/shard_map/ppermute | solution.py:515
  1.9 3.3 %collective-permute-start.1 = (bf16[400,192]{1,0:T(8,128)(2,1)S(1)}, bf16[400,192]{1,0:T(8,128)(2,1)S(1)}, u32[]{:S(2)}, u32[]{:S(2)}) collective-permute-start(bf16[400,192]{1,0:T(8,128)(2,1)S(1)} %get-tuple-element.21), channel_id=1, source_target_pairs={{1,2},{3,4},{5,6},{7,8},{9,10},{11,12},{13,14},{2,1},{4,3},{6,5},{... | collective-permute-start | bytes 460808 | tf_op jit(solution)/shard_map/ppermute | solution.py:514
  5.2 0.0 copy-done
  5.2 0.0 copy-done.1
  5.3 7.8 %inner_sums.1 = (bf16[2,2,72,96,128]{4,3,2,1,0:T(8,128)(2,1)S(1)}, bf16[2,2,80,96,128]{4,3,2,1,0:T(8,128)(2,1)S(1)}, bf16[25,320,128]{2,1,0:T(8,128)(2,1)S(1)}, ...) custom-call(s32[8,128]{1,0:T(8,128)S(1)} %get-tuple-element.19.plan_ref, ...), custom_call_target="tpu_custom_call" | custom-call | flops 20000000000 | tf_op jit(solution)/shard_map/inner_sums/pallas_call | solution.py:530
  13.1 0.0 collective-permute-done.pair_ref
  13.1 0.0 collective-permute-done.1.other_ref
  13.1 6.5 %outer_sums.1 = (f32[24,128]{1,0:T(8,128)S(1)}, bf16[2,2,80,96,128]{4,3,2,1,0:T(8,128)(2,1)S(1)}, bf16[25,320,128]{2,1,0:T(8,128)(2,1)S(1)}, f32[25,208,256]{2,1...) custom-call(s32[8,128]{1,0:T(8,128)S(1)} %get-tuple-element.19.plan_, ...), custom_call_target="tpu_custom_call", output_to_operand_aliasing={{1}: (5, {}), {2}: (6, {}), {3}: (7, {}), {4}: (8, {}), {5}... | custom-call | tf_op jit(solution)/shard_map/outer_sums/pallas_call | solution.py:540
  19.6 1.9 %collective-permute-start.3 = (f32[24,128]{1,0:T(8,128)S(1)}, f32[24,128]{1,0:T(8,128)S(1)}, u32[]{:S(2)}, u32[]{:S(2)}) collective-permute-start(f32[24,128]{1,0:T(8,128)S(1)} %get-tuple-element.28.mine_ref), channel_id=1, source_target_pairs={{1,2},{3,4},{5,6},{7,8},{9,10},{11,12},{13,14},{2,1},{4,3},{6,5},{... | collective-permute-start | bytes 36872 | tf_op jit(solution)/shard_map/ppermute | solution.py:551
  21.5 0.1 collective-permute-start.2
  21.6 3.9 %collective-permute-done.3.other_ref = f32[24,128]{1,0:T(8,128)S(1)} collective-permute-done((f32[24,128]{1,0:T(8,128)S(1)}, f32[24,128]{1,0:T(8,128)S(1)}, u32[]{:S(2)}, u32[]{:S(2)}) %collective-permute-start.3) | collective-permute-done | bytes 12320 | tf_op jit(solution)/shard_map/ppermute | solution.py:551
  25.5 0.0 collective-permute-done.2.pair_ref
  25.5 1.3 %smoothed_update.1 = f32[5,3,128]{2,1,0:T(4,128)} custom-call(f32[24,128]{1,0:T(8,128)S(1)} %get-tuple-element.28.mine_ref, f32[24,128]{1,0:T(8,128)S(1)} %collective-permute-done.2.pair_ref, f32[24,128]{1,0:T(8,128)S(1)} %collective-permute-done.3.other_ref), custom_call_target="tpu_custom_call" | custom-call | tf_op jit(solution)/shard_map/smoothed_update/pallas_call | solution.py:553
  (2 shorter events, 0.1 us)
Async XLA Ops:
  0.0 1.1 %copy-start.2 = (s32[3,8]{1,0:T(4,128)S(1)}, s32[3,8]{1,0:T(4,128)}, u32[]{:S(2)}) copy-start(s32[3,8]{1,0:T(4,128)} %shift_ref.1) | copy-start | bytes 292
  0.0 1.1 %copy-start.3 = (s32[8]{0:T(128)S(1)}, s32[8]{0:T(128)}, u32[]{:S(2)}) copy-start(s32[8]{0:T(128)} %param.6) | copy-start | bytes 100
  1.1 4.1 %copy-start = (bf16[60,96,192]{2,1,0:T(8,128)(2,1)S(1)}, bf16[60,96,192]{2,1,0:T(8,128)(2,1)}, u32[]{:S(2)}) copy-start(bf16[60,96,192]{2,1,0:T(8,128)(2,1)} %second_ref.1) | copy-start | bytes 6635524
  1.1 4.1 %copy-start.1 = (bf16[60,96,192]{2,1,0:T(8,128)(2,1)S(1)}, bf16[60,96,192]{2,1,0:T(8,128)(2,1)}, u32[]{:S(2)}) copy-start(bf16[60,96,192]{2,1,0:T(8,128)(2,1)} %first_ref.1) | copy-start | bytes 6635524
  1.2 11.9 %collective-permute-start = (bf16[400,192]{1,0:T(8,128)(2,1)S(1)}, bf16[400,192]{1,0:T(8,128)(2,1)S(1)}, u32[]{:S(2)}, u32[]{:S(2)}) collective-permute-start(bf16[400,192]{1,0:T(8,128)(2,1)S(1)} %get-tuple-element.20), channel_id=1, source_target_pairs={{0,1},{1,0},{2,3},{3,2},{4,5},{5,4},{6,7},{7,6},{8,9},{9,8},{10,11... | collective-permute-start | bytes 460808 | tf_op jit(solution)/shard_map/ppermute | solution.py:515
  1.9 11.2 %collective-permute-start.1 = (bf16[400,192]{1,0:T(8,128)(2,1)S(1)}, bf16[400,192]{1,0:T(8,128)(2,1)S(1)}, u32[]{:S(2)}, u32[]{:S(2)}) collective-permute-start(bf16[400,192]{1,0:T(8,128)(2,1)S(1)} %get-tuple-element.21), channel_id=1, source_target_pairs={{1,2},{3,4},{5,6},{7,8},{9,10},{11,12},{13,14},{2,1},{4,3},{6,5},{... | collective-permute-start | bytes 460808 | tf_op jit(solution)/shard_map/ppermute | solution.py:514
  19.6 5.9 %collective-permute-start.3 = (f32[24,128]{1,0:T(8,128)S(1)}, f32[24,128]{1,0:T(8,128)S(1)}, u32[]{:S(2)}, u32[]{:S(2)}) collective-permute-start(f32[24,128]{1,0:T(8,128)S(1)} %get-tuple-element.28.mine_ref), channel_id=1, source_target_pairs={{1,2},{3,4},{5,6},{7,8},{9,10},{11,12},{13,14},{2,1},{4,3},{6,5},{... | collective-permute-start | bytes 36872 | tf_op jit(solution)/shard_map/ppermute | solution.py:551
  21.5 4.0 %collective-permute-start.2 = (f32[24,128]{1,0:T(8,128)S(1)}, f32[24,128]{1,0:T(8,128)S(1)}, u32[]{:S(2)}, u32[]{:S(2)}) collective-permute-start(f32[24,128]{1,0:T(8,128)S(1)} %get-tuple-element.28.mine_ref), channel_id=1, source_target_pairs={{0,1},{1,0},{2,3},{3,2},{4,5},{5,4},{6,7},{7,6},{8,9},{9,8},{10,11... | collective-permute-start | bytes 36872 | tf_op jit(solution)/shard_map/ppermute | solution.py:552

commit v8 on v7

--- a/solution.py
+++ b/solution.py
@@ -122,6 +122,7 @@
         cx - HALF,
         sx,
         sz - z_b,
+        jnp.where((row == 0) | (row == tile_rows - 1), 1, 0),
     )
     for at, value in enumerate(values):
         table[at:at + 1, :] = jnp.where(slot < 3 * own, value, 0)
@@ -284,63 +285,7 @@
     run_units(CHUNK, total, units, table, 3 * own, fr_a, fr_b, acc, sq_a, sq_b, masks)
 
 
-def outer_kernel(
-    plan_ref, pair_ref, other_ref, gap_base, fr_a, fr_b_in, masks_in, acc_in, sq_a_in, sq_b_in,
-    out_ref, fr_b, masks, acc, sq_a, sq_b, table_v, table, units, active, sem_t,
-):
-    deep = fr_a.shape[3]
-    planes = fr_a.shape[2] - 2 * PAD_A
-    own = (acc.shape[0] - 1) // 3
-    even = lax.axis_index("span") % 2 == 0
-    base = REACH * deep
-    from_pair, from_other = [
-        ref[base:base + 8, 0:LANES].astype(jnp.float32).astype(jnp.int32)
-        for ref in (pair_ref, other_ref)
-    ]
-    below = jnp.where(even, from_other, from_pair)
-    above = jnp.where(even, from_pair, from_other)
-    plan = plan_ref[...] + pltpu.roll(below, own, 1) + pltpu.roll(above, 2 * own, 1)
-    target = decode(plan, own, planes, deep, False, table_v)
-    to_scalar = pltpu.make_async_copy(table_v, table, sem_t)
-    to_scalar.start()
-    out_ref[...] = jnp.zeros(out_ref.shape, jnp.float32)
-    out_ref[22:23] = target.astype(jnp.float32)
-
-    low_at, high_at = CHUNK, PAD_B + planes
-    pair_at = jnp.where(even, high_at, low_at)
-    other_at = jnp.where(even, low_at, high_at)
-    for p in range(REACH):
-        frame(pair_ref[p * deep:(p + 1) * deep, :], fr_b, pair_at + p)
-        frame(other_ref[p * deep:(p + 1) * deep, :], fr_b, other_at + p)
-    to_scalar.wait()
-
-    def prepare_own(s, total):
-        active[s] = s
-        set_units(units, total, s, table[12, s], CHUNK, 2)
-        return total + table[13, s]
-
-    total = lax.fori_loop(0, own, prepare_own, 0)
-
-    def prepare(s, carry):
-        total, alive = carry
-        count = table[13, s]
-
-        @pl.when(count > 0)
-        def _():
-            set_masks(masks, s, table)
-            for ref in (acc, sq_a, sq_b):
-                ref[s] = jnp.zeros(ref.shape[1:], jnp.float32)
-            active[alive] = s
-            set_units(units, total, s, table[12, s], CHUNK, W // CHUNK)
-
-        return total + count, alive + jnp.where(count > 0, 1, 0)
-
-    total, alive = lax.fori_loop(own, 3 * own, prepare, (total, own))
-    spare = 3 * own
-    for at in range(CLOSE - 1):
-        active[alive + at] = spare
-    run_units(CHUNK // 2, total, units, table, spare, fr_a, fr_b, acc, sq_a, sq_b, masks)
-
+def finish_slots(alive, active, table, out_ref, gap_base, fr_b, masks, acc, sq_a, sq_b):
     cols = 2 * LANES
     col_one = lax.broadcasted_iota(jnp.int32, (1, cols), 1)
     lag_one = jnp.where(col_one >= ROWS_B, 1, 0) + jnp.where(col_one >= 2 * ROWS_B, 1, 0)
@@ -406,10 +351,89 @@
     lax.fori_loop(0, (alive + CLOSE - 1) // CLOSE, finish, 0)
 
 
-def update_kernel(own, mine_ref, pair_ref, other_ref, out_ref):
+def outer_kernel(
+    plan_ref, pair_ref, other_ref, gap_base, fr_a, fr_b_in, masks_in, acc_in, sq_a_in, sq_b_in,
+    out_ref, table_v, fr_b, masks, acc, sq_a, sq_b, table, units, active, sem_t,
+):
+    deep = fr_a.shape[3]
+    planes = fr_a.shape[2] - 2 * PAD_A
+    own = (acc.shape[0] - 1) // 3
+    even = lax.axis_index("span") % 2 == 0
+    base = REACH * deep
+    from_pair, from_other = [
+        ref[base:base + 8, 0:LANES].astype(jnp.float32).astype(jnp.int32)
+        for ref in (pair_ref, other_ref)
+    ]
+    below = jnp.where(even, from_other, from_pair)
+    above = jnp.where(even, from_pair, from_other)
+    plan = plan_ref[...] + pltpu.roll(below, own, 1) + pltpu.roll(above, 2 * own, 1)
+    target = decode(plan, own, planes, deep, False, table_v)
+    to_scalar = pltpu.make_async_copy(table_v, table, sem_t)
+    to_scalar.start()
+    out_ref[...] = jnp.zeros(out_ref.shape, jnp.float32)
+    out_ref[22:23] = target.astype(jnp.float32)
+
+    low_at, high_at = CHUNK, PAD_B + planes
+    pair_at = jnp.where(even, high_at, low_at)
+    other_at = jnp.where(even, low_at, high_at)
+    for p in range(REACH):
+        frame(pair_ref[p * deep:(p + 1) * deep, :], fr_b, pair_at + p)
+        frame(other_ref[p * deep:(p + 1) * deep, :], fr_b, other_at + p)
+    to_scalar.wait()
+
+    def prepare_own(s, carry):
+        total, alive = carry
+        active[alive] = s
+        set_units(units, total, s, table[12, s], CHUNK, 2)
+        return total + table[13, s], alive + table[17, s]
+
+    carry = lax.fori_loop(0, own, prepare_own, (0, 0))
+
+    def prepare(s, carry):
+        total, alive = carry
+        count = table[13, s]
+
+        @pl.when(count > 0)
+        def _():
+            set_masks(masks, s, table)
+            for ref in (acc, sq_a, sq_b):
+                ref[s] = jnp.zeros(ref.shape[1:], jnp.float32)
+            active[alive] = s
+            set_units(units, total, s, table[12, s], CHUNK, W // CHUNK)
+
+        return total + count, alive + jnp.where(count > 0, 1, 0)
+
+    total, alive = lax.fori_loop(own, 3 * own, prepare, carry)
+    spare = 3 * own
+    for at in range(CLOSE - 1):
+        active[alive + at] = spare
+    run_units(CHUNK // 2, total, units, table, spare, fr_a, fr_b, acc, sq_a, sq_b, masks)
+    finish_slots(alive, active, table, out_ref, gap_base, fr_b, masks, acc, sq_a, sq_b)
+
+
+def rest_kernel(
+    table_v, gap_base, fr_b, masks, acc, sq_a, sq_b, out_ref, table, active, sem_t,
+):
+    own = (acc.shape[0] - 1) // 3
+    to_scalar = pltpu.make_async_copy(table_v, table, sem_t)
+    to_scalar.start()
+    out_ref[...] = jnp.zeros(out_ref.shape, jnp.float32)
+    to_scalar.wait()
+
+    def listed(s, alive):
+        active[alive] = s
+        return alive + 1 - table[17, s]
+
+    alive = lax.fori_loop(0, own, listed, 0)
+    for at in range(CLOSE - 1):
+        active[alive + at] = 3 * own
+    finish_slots(alive, active, table, out_ref, gap_base, fr_b, masks, acc, sq_a, sq_b)
+
+
+def update_kernel(own, mine_ref, rest_ref, pair_ref, other_ref, out_ref):
     tile_rows = out_ref.shape[0]
     even = lax.axis_index("span") % 2 == 0
-    mine = mine_ref[...]
+    mine = mine_ref[...] + rest_ref[...]
     pair = pair_ref[...]
     other = other_ref[...]
     below = jnp.where(even, other, pair)
@@ -523,7 +547,6 @@
         jax.ShapeDtypeStruct((slots, ROWS_B, LANES), jnp.float32),
     )
     scratch = [
-        pltpu.VMEM((FIELDS, LANES), jnp.int32),
         pltpu.SMEM((FIELDS, LANES), jnp.int32),
         pltpu.SMEM(((3 * own + 1) * (W // CHUNK) + PAIR,), jnp.int32),
     ]
@@ -532,17 +555,20 @@
         out_shape=(frames_a, *state),
         in_specs=[vmem] * 3,
         out_specs=(vmem,) * 6,
-        scratch_shapes=[*scratch, pltpu.SemaphoreType.DMA],
+        scratch_shapes=[
+            pltpu.VMEM((FIELDS, LANES), jnp.int32), *scratch, pltpu.SemaphoreType.DMA],
         compiler_params=limit(8),
         cost_estimate=busy,
         name="inner_sums",
     )(plan, first, second)
-    sums, *_ = pl.pallas_call(
+    sums, fields, *held = pl.pallas_call(
         outer_kernel,
-        out_shape=(jax.ShapeDtypeStruct((24, LANES), jnp.float32), *state),
+        out_shape=(
+            jax.ShapeDtypeStruct((24, LANES), jnp.float32),
+            jax.ShapeDtypeStruct((FIELDS, LANES), jnp.int32), *state),
         in_specs=[vmem] * 10,
-        out_specs=(vmem,) * 6,
-        input_output_aliases={5 + i: 1 + i for i in range(5)},
+        out_specs=(vmem,) * 7,
+        input_output_aliases={5 + i: 2 + i for i in range(5)},
         scratch_shapes=[
             *scratch, pltpu.SMEM((slots + CLOSE,), jnp.int32), pltpu.SemaphoreType.DMA],
         compiler_params=limit(8),
@@ -550,14 +576,26 @@
     )(plan, from_pair, from_other, gap, *held)
     other_sums = lax.ppermute(sums, "span", others)
     pair_sums = lax.ppermute(sums, "span", pairs)
+    rest = pl.pallas_call(
+        rest_kernel,
+        out_shape=jax.ShapeDtypeStruct((24, LANES), jnp.float32),
+        in_specs=[vmem] * 7,
+        out_specs=vmem,
+        scratch_shapes=[
+            pltpu.SMEM((FIELDS, LANES), jnp.int32), pltpu.SMEM((slots + CLOSE,), jnp.int32),
+            pltpu.SemaphoreType.DMA],
+        compiler_params=limit(8),
+        cost_estimate=busy,
+        name="rest_of_sums",
+    )(fields, gap, *held)
     field = pl.pallas_call(
         functools.partial(update_kernel, own),
         out_shape=jax.ShapeDtypeStruct((planes // STRIDE, 3, GZX), jnp.float32),
-        in_specs=[vmem] * 3,
+        in_specs=[vmem] * 4,
         out_specs=vmem,
         compiler_params=limit(4),
         name="smoothed_update",
-    )(sums, pair_sums, other_sums)
+    )(sums, rest, pair_sums, other_sums)
     return jnp.transpose(field, (1, 0, 2))
 
 

time: 27 us -> 26.2 us (0.970)
  the two profiles are of different devices: /device:TPU:21 before, /device:TPU:23 now
where the time goes in v8:
time: 26.2 us; the launch traced here: 26.4 us
  Pallas kernels  16.6 us (63%)
  starting transfers between devices  6.97 us (27%)
  waiting for transfers between devices  1.64 us (6%)
  local copies, waits for them, and re-layouts  1.08 us (4%)
    pallas_call x1, Pallas kernels, shards(): pl.pallas_call(inner_kernel, out_shape=(frames_a, *state), in_specs=[vmem...  6.99 us
    pallas_call x1, Pallas kernels, shards(): pl.pallas_call(outer_kernel, out_shape=(jax.ShapeDtypeStruct((24, LANES),...  6.83 us
    ppermute x1, starting transfers between devices, shards(): from_other = lax.ppermute(to_other, 'span', others)  3.31 us
    ppermute x1, starting transfers between devices, shards(): other_sums = lax.ppermute(sums, 'span', others)  2.85 us
    ppermute x1, waiting for transfers between devices, shards(): other_sums = lax.ppermute(sums, 'span', others)  1.63 us
    pallas_call x1, Pallas kernels, shards(): pl.pallas_call(rest_kernel, out_shape=jax.ShapeDtypeStruct((24, LANES), j...  1.34 us
    pallas_call x1, Pallas kernels, shards(): pl.pallas_call(functools.partial(update_kernel, own), out_shape=jax.Shape...  1.33 us
    slice x1, local copies, waits for them, and re-layouts, shards(): low_planes, high_planes = (tile[:REACH], tile[planes - REACH:])  1.06 us
  transfers between devices with their start and end apart: 4, of which 1 were waited for; matrix products, arithmetic and copies ran while one was open for 0% of the time, Pallas kernels for 32%

profile of v8, /device:TPU:23, one launch (start us, length us, event | category | flops | bytes accessed | tf_op | source)
XLA Modules:
  0.0 26.4 jit_solution(18158309235099840345)
XLA Ops:
  0.0 0.0 copy-start.2
  0.0 0.0 copy-start.3
  0.0 1.1 %fusion = (bf16[4,96,192]{2,1,0:T(8,128)(2,1)S(1)}, bf16[4,96,192]{2,1,0:T(8,128)(2,1)S(1)}) fusion(bf16[60,96,192]{2,1,0:T(8,128)(2,1)} %second_ref.1), kind=kLoop, calls=%fused_computation | loop fusion | bytes 589824 | tf_op jit(solution)/shard_map/slice | solution.py:528
  1.1 0.0 copy-done.2
  1.1 0.0 copy-done.3
  1.1 0.0 copy-start
  1.1 0.0 copy-start.1
  1.2 0.7 %collective-permute-start = (bf16[400,192]{1,0:T(8,128)(2,1)S(1)}, bf16[400,192]{1,0:T(8,128)(2,1)S(1)}, u32[]{:S(2)}, u32[]{:S(2)}) collective-permute-start(bf16[400,192]{1,0:T(8,128)(2,1)S(1)} %get-tuple-element.26), channel_id=1, source_target_pairs={{0,1},{1,0},{2,3},{3,2},{4,5},{5,4},{6,7},{7,6},{8,9},{9,8},{10,11... | collective-permute-start | bytes 460808 | tf_op jit(solution)/shard_map/ppermute | solution.py:539
  1.9 3.3 %collective-permute-start.1 = (bf16[400,192]{1,0:T(8,128)(2,1)S(1)}, bf16[400,192]{1,0:T(8,128)(2,1)S(1)}, u32[]{:S(2)}, u32[]{:S(2)}) collective-permute-start(bf16[400,192]{1,0:T(8,128)(2,1)S(1)} %get-tuple-element.27), channel_id=1, source_target_pairs={{1,2},{3,4},{5,6},{7,8},{9,10},{11,12},{13,14},{2,1},{4,3},{6,5},{... | collective-permute-start | bytes 460808 | tf_op jit(solution)/shard_map/ppermute | solution.py:538
  5.2 0.0 copy-done
  5.2 0.0 copy-done.1
  5.3 7.0 %inner_sums.1 = (bf16[2,2,72,96,128]{4,3,2,1,0:T(8,128)(2,1)S(1)}, bf16[2,2,80,96,128]{4,3,2,1,0:T(8,128)(2,1)S(1)}, bf16[25,320,128]{2,1,0:T(8,128)(2,1)S(1)}, ...) custom-call(s32[8,128]{1,0:T(8,128)S(1)} %get-tuple-element.25.plan_ref, ...), custom_call_target="tpu_custom_call" | custom-call | flops 20000000000 | tf_op jit(solution)/shard_map/inner_sums/pallas_call | solution.py:553
  12.3 0.0 collective-permute-done.pair_ref
  12.3 0.0 collective-permute-done.1.other_ref
  12.3 6.8 %outer_sums.1 = (f32[24,128]{1,0:T(8,128)S(1)}, s32[24,128]{1,0:T(8,128)S(1)}, bf16[2,2,80,96,128]{4,3,2,1,0:T(8,128)(2,1)S(1)}, bf16[25,320,128]{2,1,0:T(8,128)...) custom-call(s32[8,128]{1,0:T(8,128)S(1)} %get-tuple-element.25.plan_, ...), custom_call_target="tpu_custom_call", output_to_operand_aliasing={{2}: (5, {}), {3}: (6, {}), {4}: (7, {}), {5}: (8, {}), {6}... | custom-call | tf_op jit(solution)/shard_map/outer_sums/pallas_call | solution.py:564
  19.1 2.8 %collective-permute-start.3 = (f32[24,128]{1,0:T(8,128)S(1)}, f32[24,128]{1,0:T(8,128)S(1)}, u32[]{:S(2)}, u32[]{:S(2)}) collective-permute-start(f32[24,128]{1,0:T(8,128)S(1)} %get-tuple-element.34.mine_ref), channel_id=1, source_target_pairs={{1,2},{3,4},{5,6},{7,8},{9,10},{11,12},{13,14},{2,1},{4,3},{6,5},{... | collective-permute-start | bytes 36872 | tf_op jit(solution)/shard_map/ppermute | solution.py:577
  22.0 0.1 collective-permute-start.2
  22.1 1.3 %rest_of_sums.1.rest_ref = f32[24,128]{1,0:T(8,128)S(1)} custom-call(s32[24,128]{1,0:T(8,128)S(1)} %get-tuple-element.35.table_v, s32[64,256]{1,0:T(8,128)S(1)} %gap_table.1.gap_ref.gap_base, bf16[2,2,80,96,128]{4,3,2,1,0:T(8,128)(2,1)S(1)} %get-tuple-element.36.fr_b, bf16[25,320,128]{2,1,0:T(8,128)(2,1)S(1)} %get-tuple-element.37.masks, ...), custom_call_target="tpu_custom_call" | custom-call | flops 20000000000 | tf_op jit(solution)/shard_map/rest_of_sums/pallas_call | solution.py:579
  23.4 1.6 %collective-permute-done.3.other_ref = f32[24,128]{1,0:T(8,128)S(1)} collective-permute-done((f32[24,128]{1,0:T(8,128)S(1)}, f32[24,128]{1,0:T(8,128)S(1)}, u32[]{:S(2)}, u32[]{:S(2)}) %collective-permute-start.3) | collective-permute-done | bytes 12320 | tf_op jit(solution)/shard_map/ppermute | solution.py:577
  25.0 0.0 collective-permute-done.2.pair_ref
  25.0 1.3 %smoothed_update.1 = f32[5,3,128]{2,1,0:T(4,128)} custom-call(f32[24,128]{1,0:T(8,128)S(1)} %get-tuple-element.34.mine_ref, f32[24,128]{1,0:T(8,128)S(1)} %rest_of_sums.1.rest_ref, f32[24,128]{1,0:T(8,128)S(1)} %collective-permute-done.2.pair_ref, f32[24,128]{1,0:T(8,128)S(1)} %collective-permute-done.3.other_ref), custom_call_target="tpu_custom_call" | custom-call | tf_op jit(solution)/shard_map/smoothed_update/pallas_call | solution.py:591
  (2 shorter events, 0.1 us)
Async XLA Ops:
  0.0 1.1 %copy-start.2 = (s32[3,8]{1,0:T(4,128)S(1)}, s32[3,8]{1,0:T(4,128)}, u32[]{:S(2)}) copy-start(s32[3,8]{1,0:T(4,128)} %shift_ref.1) | copy-start | bytes 292
  0.0 1.1 %copy-start.3 = (s32[8]{0:T(128)S(1)}, s32[8]{0:T(128)}, u32[]{:S(2)}) copy-start(s32[8]{0:T(128)} %param.6) | copy-start | bytes 100
  1.1 4.1 %copy-start = (bf16[60,96,192]{2,1,0:T(8,128)(2,1)S(1)}, bf16[60,96,192]{2,1,0:T(8,128)(2,1)}, u32[]{:S(2)}) copy-start(bf16[60,96,192]{2,1,0:T(8,128)(2,1)} %second_ref.1) | copy-start | bytes 6635524
  1.1 4.1 %copy-start.1 = (bf16[60,96,192]{2,1,0:T(8,128)(2,1)S(1)}, bf16[60,96,192]{2,1,0:T(8,128)(2,1)}, u32[]{:S(2)}) copy-start(bf16[60,96,192]{2,1,0:T(8,128)(2,1)} %first_ref.1) | copy-start | bytes 6635524
  1.2 11.1 %collective-permute-start = (bf16[400,192]{1,0:T(8,128)(2,1)S(1)}, bf16[400,192]{1,0:T(8,128)(2,1)S(1)}, u32[]{:S(2)}, u32[]{:S(2)}) collective-permute-start(bf16[400,192]{1,0:T(8,128)(2,1)S(1)} %get-tuple-element.26), channel_id=1, source_target_pairs={{0,1},{1,0},{2,3},{3,2},{4,5},{5,4},{6,7},{7,6},{8,9},{9,8},{10,11... | collective-permute-start | bytes 460808 | tf_op jit(solution)/shard_map/ppermute | solution.py:539
  1.9 10.4 %collective-permute-start.1 = (bf16[400,192]{1,0:T(8,128)(2,1)S(1)}, bf16[400,192]{1,0:T(8,128)(2,1)S(1)}, u32[]{:S(2)}, u32[]{:S(2)}) collective-permute-start(bf16[400,192]{1,0:T(8,128)(2,1)S(1)} %get-tuple-element.27), channel_id=1, source_target_pairs={{1,2},{3,4},{5,6},{7,8},{9,10},{11,12},{13,14},{2,1},{4,3},{6,5},{... | collective-permute-start | bytes 460808 | tf_op jit(solution)/shard_map/ppermute | solution.py:538
  19.1 5.9 %collective-permute-start.3 = (f32[24,128]{1,0:T(8,128)S(1)}, f32[24,128]{1,0:T(8,128)S(1)}, u32[]{:S(2)}, u32[]{:S(2)}) collective-permute-start(f32[24,128]{1,0:T(8,128)S(1)} %get-tuple-element.34.mine_ref), channel_id=1, source_target_pairs={{1,2},{3,4},{5,6},{7,8},{9,10},{11,12},{13,14},{2,1},{4,3},{6,5},{... | collective-permute-start | bytes 36872 | tf_op jit(solution)/shard_map/ppermute | solution.py:577
  22.0 3.1 %collective-permute-start.2 = (f32[24,128]{1,0:T(8,128)S(1)}, f32[24,128]{1,0:T(8,128)S(1)}, u32[]{:S(2)}, u32[]{:S(2)}) collective-permute-start(f32[24,128]{1,0:T(8,128)S(1)} %get-tuple-element.34.mine_ref), channel_id=1, source_target_pairs={{0,1},{1,0},{2,3},{3,2},{4,5},{5,4},{6,7},{7,6},{8,9},{9,8},{10,11... | collective-permute-start | bytes 36872 | tf_op jit(solution)/shard_map/ppermute | solution.py:578

commit v9 on v8

--- a/solution.py
+++ b/solution.py
@@ -26,12 +26,12 @@
 PAD_A = CHUNK
 PAD_B = CHUNK + REACH
 PIECES = 2
-SLOT = 4
+SPREAD = 32
 PLAN_ROWS = 16
 FIELDS = 24
 PAIR = 8
 REST = 4
-CLOSE = 2
+CLOSE = 4
 FAR = 4096
 
 
@@ -343,9 +343,9 @@
             total_18 = jnp.zeros((18, LANES), jnp.float32)
             for lag_y in range(3):
                 part = jnp.sum(jnp.where(lag_18 == lag_y, stack, 0.0), axis=1, keepdims=True)
-                total_18 = total_18 + jnp.where(lane_18 == SLOT * s + lag_y, part, 0.0)
+                total_18 = total_18 + jnp.where(lane_18 == s + SPREAD * lag_y, part, 0.0)
             out_ref[0:18] += total_18
-            out_ref[18:22] += jnp.where(lane_4 == SLOT * s, sums, 0.0)
+            out_ref[18:22] += jnp.where(lane_4 == s, sums, 0.0)
         return carry
 
     lax.fori_loop(0, (alive + CLOSE - 1) // CLOSE, finish, 0)
@@ -438,24 +438,23 @@
     other = other_ref[...]
     below = jnp.where(even, other, pair)
     above = jnp.where(even, pair, other)
-    span = SLOT * own
     lane = lax.broadcasted_iota(jnp.int32, mine.shape, 1)
-    total = mine
-    total = total + jnp.where(
-        lane < span,
-        pltpu.roll(below, LANES - 2 * span, 1) + pltpu.roll(above, LANES - span, 1),
+    slot = lane & (SPREAD - 1)
+    total = mine + jnp.where(
+        slot < own,
+        pltpu.roll(below, LANES - 2 * own, 1) + pltpu.roll(above, LANES - own, 1),
         jnp.where(
-            lane < 2 * span, pltpu.roll(below, span, 1),
-            jnp.where(lane < 3 * span, pltpu.roll(above, 2 * span, 1), 0.0)))
+            slot < 2 * own, pltpu.roll(below, own, 1),
+            jnp.where(slot < 3 * own, pltpu.roll(above, 2 * own, 1), 0.0)))
 
     def lead(v):
-        return v + pltpu.roll(v, LANES - 1, 1) + pltpu.roll(v, LANES - 2, 1)
+        return v + pltpu.roll(v, LANES - SPREAD, 1) + pltpu.roll(v, LANES - 2 * SPREAD, 1)
 
     def spread(v):
-        return v + pltpu.roll(v, 1, 1) + pltpu.roll(v, 2, 1)
-
-    lag_lane = lane % SLOT
-    stats = spread(jnp.where(lag_lane[0:4] == 0, total[18:22], 0.0))
+        v = jnp.where(lane[0:v.shape[0]] < SPREAD, v, 0.0)
+        return v + pltpu.roll(v, SPREAD, 1) + pltpu.roll(v, 2 * SPREAD, 1)
+
+    stats = spread(total[18:22])
     voxels = float(W) ** 3
     block_voxels = float(BLOCK) ** 3
     mean_a = stats[0:1] / voxels
@@ -464,41 +463,48 @@
     energy_b = jnp.maximum(stats[3:4] / block_voxels - mean_b * mean_b, 0.0)
     normaliser = voxels * jnp.sqrt((energy_a + EPSILON) * (energy_b + EPSILON))
     scaled = SHARP * ((total[0:9] - mean_a * total[9:18]) / normaliser)
-    used = lag_lane[0:9] < 3
+    used = lane[0:9] < 3 * SPREAD
     scaled = jnp.where(used, scaled, -1e30)
     top = jnp.max(scaled, axis=0, keepdims=True)
-    top = jnp.maximum(top, jnp.maximum(pltpu.roll(top, LANES - 1, 1), pltpu.roll(top, LANES - 2, 1)))
-    top = spread(jnp.where(lag_lane[0:1] == 0, top, 0.0))
-    weights = jnp.where(used, jnp.exp(scaled - top), 0.0)
+    top = jnp.maximum(top, jnp.maximum(
+        pltpu.roll(top, LANES - SPREAD, 1), pltpu.roll(top, LANES - 2 * SPREAD, 1)))
+    weights = jnp.where(used, jnp.exp(scaled - spread(top)), 0.0)
     lag_row = lax.broadcasted_iota(jnp.int32, weights.shape, 0)
-    lag_z = (lag_row // 3 - 1).astype(jnp.float32)
-    lag_x = (lag_row % 3 - 1).astype(jnp.float32)
+    lag_z = jnp.where(lag_row >= 6, 1.0, jnp.where(lag_row >= 3, 0.0, -1.0))
+    lag_x = jnp.where(
+        (lag_row == 0) | (lag_row == 3) | (lag_row == 6), -1.0,
+        jnp.where((lag_row == 2) | (lag_row == 5) | (lag_row == 8), 1.0, 0.0))
+    lag_y = jnp.where(lane[0:1] >= 2 * SPREAD, 1.0, jnp.where(lane[0:1] >= SPREAD, 0.0, -1.0))
     column = jnp.sum(weights, axis=0, keepdims=True)
-    weight_sum = lead(column)
-    along_y = lead(column * (lag_lane[0:1] - 1).astype(jnp.float32)) / weight_sum
-    along_z = lead(jnp.sum(weights * lag_z, axis=0, keepdims=True)) / weight_sum
-    along_x = lead(jnp.sum(weights * lag_x, axis=0, keepdims=True)) / weight_sum
-    corrections = (along_y, along_z, along_x)
-
-    grid_lane = lax.broadcasted_iota(jnp.int32, (8, LANES), 1)
-    place = lax.broadcasted_iota(jnp.int32, (8, LANES), 0) * GZX + grid_lane
-    target = mine[22:23].astype(jnp.int32)
-    fields = [jnp.zeros((8, LANES), jnp.float32) for _ in range(3)]
-    for s in range(3 * own):
-        hit = place == target[:, s:s + 1]
-        for comp in range(3):
-            fields[comp] = jnp.where(
-                hit, corrections[comp][:, SLOT * s:SLOT * s + 1], fields[comp])
-    lane_z = grid_lane // GX
-    lane_x = grid_lane % GX
-    for comp in range(3):
-        field = fields[comp]
-        near = jnp.where(lane_z >= 1, pltpu.roll(field, GX, 1), 0.0)
-        near = near + jnp.where(lane_z < GZX // GX - 1, pltpu.roll(field, LANES - GX, 1), 0.0)
-        near = near + jnp.where(lane_x >= 1, pltpu.roll(field, 1, 1), 0.0)
-        near = near + jnp.where(lane_x < GX - 1, pltpu.roll(field, LANES - 1, 1), 0.0)
-        near = near[1:1 + tile_rows] + field[0:tile_rows] + field[2:2 + tile_rows]
-        out_ref[:, comp, :] = 0.4 * field[1:1 + tile_rows] + 0.1 * near
+    moments = lead(jnp.concatenate([
+        column * lag_y,
+        jnp.sum(weights * lag_z, axis=0, keepdims=True),
+        jnp.sum(weights * lag_x, axis=0, keepdims=True),
+        column,
+        jnp.zeros((4, LANES), jnp.float32),
+    ], axis=0))
+    found = jnp.where(lane[0:8] < 3 * own, moments / moments[3:4], 0.0)
+    high = found.astype(jnp.bfloat16).astype(jnp.float32)
+    left = found - high
+    middle = left.astype(jnp.bfloat16).astype(jnp.float32)
+    parts = jnp.concatenate(
+        [high, middle, left - middle, jnp.zeros((8, LANES), jnp.float32)], axis=0
+    ).astype(jnp.bfloat16)
+    place = lax.broadcasted_iota(jnp.int32, ((tile_rows + 2) * GZX, LANES), 0)
+    node = jnp.where(place == mine[22:23].astype(jnp.int32), 1.0, 0.0).astype(jnp.bfloat16)
+    field = lax.dot_general(
+        parts, node, (((1,), (1,)), ((), ())), preferred_element_type=jnp.float32)
+    field = field[0:8] + field[8:16] + field[16:24]
+    lane_x = lane[0:8] & (GX - 1)
+    for row in range(tile_rows):
+        before, centre, after = [
+            field[:, (row + i) * GZX:(row + i + 1) * GZX] for i in range(3)]
+        near = before + after
+        near = near + jnp.where(lane[0:8] >= GX, pltpu.roll(centre, GX, 1), 0.0)
+        near = near + jnp.where(lane[0:8] < GZX - GX, pltpu.roll(centre, LANES - GX, 1), 0.0)
+        near = near + jnp.where(lane_x >= 1, pltpu.roll(centre, 1, 1), 0.0)
+        near = near + jnp.where(lane_x < GX - 1, pltpu.roll(centre, LANES - 1, 1), 0.0)
+        out_ref[row] = (0.4 * centre + 0.1 * near)[0:3]
 
 
 def shards(first, second, windows, shifts):

time: 26.2 us -> 26.2 us (level); the launches traced: 26.4 us -> 26.1 us
  waiting for transfers between devices: 1.64 us -> 0.71 us
  starting transfers between devices: 6.97 us -> 7.55 us
    ppermute x1, waiting for transfers between devices: 1.63 us -> 0.7 us  [shards(): other_sums = lax.ppermute(sums, 'span', others)]
    ppermute x1, starting transfers between devices: 2.85 us -> 3.43 us  [shards(): other_sums = lax.ppermute(sums, 'span', others)]
    pallas_call x1, Pallas kernels: 1.34 us -> 1.69 us  [shards(): pl.pallas_call(rest_kernel, out_shape=jax.ShapeDtypeStruct((24, LANES), j...]
  transfers between devices with their start and end apart: 4 -> 4, of which waited for: 1 -> 1; matrix products, arithmetic and copies ran while one was open for 0% -> 0% of each run, Pallas kernels for 32% -> 33%
where the time goes in v9:
time: 26.2 us; the launch traced here: 26.1 us
  Pallas kernels  16.6 us (63%)
  starting transfers between devices  7.55 us (29%)
  local copies, waits for them, and re-layouts  1.08 us (4%)
  waiting for transfers between devices  0.71 us (3%)
    pallas_call x1, Pallas kernels, shards(): pl.pallas_call(inner_kernel, out_shape=(frames_a, *state), in_specs=[vmem...  7 us
    pallas_call x1, Pallas kernels, shards(): pl.pallas_call(outer_kernel, out_shape=(jax.ShapeDtypeStruct((24, LANES),...  6.58 us
    ppermute x1, starting transfers between devices, shards(): other_sums = lax.ppermute(sums, 'span', others)  3.43 us
    ppermute x1, starting transfers between devices, shards(): from_other = lax.ppermute(to_other, 'span', others)  3.31 us
    pallas_call x1, Pallas kernels, shards(): pl.pallas_call(rest_kernel, out_shape=jax.ShapeDtypeStruct((24, LANES), j...  1.69 us
    pallas_call x1, Pallas kernels, shards(): pl.pallas_call(functools.partial(update_kernel, own), out_shape=jax.Shape...  1.27 us
    slice x1, local copies, waits for them, and re-layouts, shards(): low_planes, high_planes = (tile[:REACH], tile[planes - REACH:])  1.06 us
    ppermute x1, starting transfers between devices, shards(): from_pair = lax.ppermute(to_pair, 'span', pairs)  0.74 us
  transfers between devices with their start and end apart: 4, of which 1 were waited for; matrix products, arithmetic and copies ran while one was open for 0% of the time, Pallas kernels for 33%

profile of v9, /device:TPU:23, one launch (start us, length us, event | category | flops | bytes accessed | tf_op | source)
XLA Modules:
  0.0 26.1 jit_solution(10144202926759173803)
XLA Ops:
  0.0 0.0 copy-start.2
  0.0 0.0 copy-start.3
  0.0 1.1 %fusion = (bf16[4,96,192]{2,1,0:T(8,128)(2,1)S(1)}, bf16[4,96,192]{2,1,0:T(8,128)(2,1)S(1)}) fusion(bf16[60,96,192]{2,1,0:T(8,128)(2,1)} %second_ref.1), kind=kLoop, calls=%fused_computation | loop fusion | bytes 589824 | tf_op jit(solution)/shard_map/slice | solution.py:534
  1.1 0.0 copy-done.2
  1.1 0.0 copy-done.3
  1.1 0.0 copy-start
  1.1 0.0 copy-start.1
  1.2 0.7 %collective-permute-start = (bf16[400,192]{1,0:T(8,128)(2,1)S(1)}, bf16[400,192]{1,0:T(8,128)(2,1)S(1)}, u32[]{:S(2)}, u32[]{:S(2)}) collective-permute-start(bf16[400,192]{1,0:T(8,128)(2,1)S(1)} %get-tuple-element.26), channel_id=1, source_target_pairs={{0,1},{1,0},{2,3},{3,2},{4,5},{5,4},{6,7},{7,6},{8,9},{9,8},{10,11... | collective-permute-start | bytes 460808 | tf_op jit(solution)/shard_map/ppermute | solution.py:545
  1.9 3.3 %collective-permute-start.1 = (bf16[400,192]{1,0:T(8,128)(2,1)S(1)}, bf16[400,192]{1,0:T(8,128)(2,1)S(1)}, u32[]{:S(2)}, u32[]{:S(2)}) collective-permute-start(bf16[400,192]{1,0:T(8,128)(2,1)S(1)} %get-tuple-element.27), channel_id=1, source_target_pairs={{1,2},{3,4},{5,6},{7,8},{9,10},{11,12},{13,14},{2,1},{4,3},{6,5},{... | collective-permute-start | bytes 460808 | tf_op jit(solution)/shard_map/ppermute | solution.py:544
  5.2 0.0 copy-done
  5.2 0.0 copy-done.1
  5.3 7.0 %inner_sums.1 = (bf16[2,2,72,96,128]{4,3,2,1,0:T(8,128)(2,1)S(1)}, bf16[2,2,80,96,128]{4,3,2,1,0:T(8,128)(2,1)S(1)}, bf16[25,320,128]{2,1,0:T(8,128)(2,1)S(1)}, ...) custom-call(s32[8,128]{1,0:T(8,128)S(1)} %get-tuple-element.25.plan_ref, ...), custom_call_target="tpu_custom_call" | custom-call | flops 20000000000 | tf_op jit(solution)/shard_map/inner_sums/pallas_call | solution.py:559
  12.3 0.0 collective-permute-done.pair_ref
  12.3 0.0 collective-permute-done.1.other_ref
  12.3 6.6 %outer_sums.1 = (f32[24,128]{1,0:T(8,128)S(1)}, s32[24,128]{1,0:T(8,128)S(1)}, bf16[2,2,80,96,128]{4,3,2,1,0:T(8,128)(2,1)S(1)}, bf16[25,320,128]{2,1,0:T(8,128)...) custom-call(s32[8,128]{1,0:T(8,128)S(1)} %get-tuple-element.25.plan_, ...), custom_call_target="tpu_custom_call", output_to_operand_aliasing={{2}: (5, {}), {3}: (6, {}), {4}: (7, {}), {5}: (8, {}), {6}... | custom-call | tf_op jit(solution)/shard_map/outer_sums/pallas_call | solution.py:570
  18.9 3.4 %collective-permute-start.3 = (f32[24,128]{1,0:T(8,128)S(1)}, f32[24,128]{1,0:T(8,128)S(1)}, u32[]{:S(2)}, u32[]{:S(2)}) collective-permute-start(f32[24,128]{1,0:T(8,128)S(1)} %get-tuple-element.34.mine_ref), channel_id=1, source_target_pairs={{1,2},{3,4},{5,6},{7,8},{9,10},{11,12},{13,14},{2,1},{4,3},{6,5},{... | collective-permute-start | bytes 36872 | tf_op jit(solution)/shard_map/ppermute | solution.py:583
  22.3 0.1 collective-permute-start.2
  22.4 1.7 %rest_of_sums.1.rest_ref = f32[24,128]{1,0:T(8,128)S(1)} custom-call(s32[24,128]{1,0:T(8,128)S(1)} %get-tuple-element.35.table_v, s32[64,256]{1,0:T(8,128)S(1)} %gap_table.1.gap_ref.gap_base, bf16[2,2,80,96,128]{4,3,2,1,0:T(8,128)(2,1)S(1)} %get-tuple-element.36.fr_b, bf16[25,320,128]{2,1,0:T(8,128)(2,1)S(1)} %get-tuple-element.37.masks, ...), custom_call_target="tpu_custom_call" | custom-call | flops 20000000000 | tf_op jit(solution)/shard_map/rest_of_sums/pallas_call | solution.py:585
  24.1 0.7 %collective-permute-done.3.other_ref = f32[24,128]{1,0:T(8,128)S(1)} collective-permute-done((f32[24,128]{1,0:T(8,128)S(1)}, f32[24,128]{1,0:T(8,128)S(1)}, u32[]{:S(2)}, u32[]{:S(2)}) %collective-permute-start.3) | collective-permute-done | bytes 12320 | tf_op jit(solution)/shard_map/ppermute | solution.py:583
  24.8 0.0 collective-permute-done.2.pair_ref
  24.8 1.3 %smoothed_update.1 = f32[5,3,128]{2,1,0:T(4,128)} custom-call(f32[24,128]{1,0:T(8,128)S(1)} %get-tuple-element.34.mine_ref, f32[24,128]{1,0:T(8,128)S(1)} %rest_of_sums.1.rest_ref, f32[24,128]{1,0:T(8,128)S(1)} %collective-permute-done.2.pair_ref, f32[24,128]{1,0:T(8,128)S(1)} %collective-permute-done.3.other_ref), custom_call_target="tpu_custom_call" | custom-call | tf_op jit(solution)/shard_map/smoothed_update/pallas_call | solution.py:597
  (2 shorter events, 0.1 us)
Async XLA Ops:
  0.0 1.1 %copy-start.2 = (s32[3,8]{1,0:T(4,128)S(1)}, s32[3,8]{1,0:T(4,128)}, u32[]{:S(2)}) copy-start(s32[3,8]{1,0:T(4,128)} %shift_ref.1) | copy-start | bytes 292
  0.0 1.1 %copy-start.3 = (s32[8]{0:T(128)S(1)}, s32[8]{0:T(128)}, u32[]{:S(2)}) copy-start(s32[8]{0:T(128)} %param.6) | copy-start | bytes 100
  1.1 4.1 %copy-start = (bf16[60,96,192]{2,1,0:T(8,128)(2,1)S(1)}, bf16[60,96,192]{2,1,0:T(8,128)(2,1)}, u32[]{:S(2)}) copy-start(bf16[60,96,192]{2,1,0:T(8,128)(2,1)} %second_ref.1) | copy-start | bytes 6635524
  1.1 4.1 %copy-start.1 = (bf16[60,96,192]{2,1,0:T(8,128)(2,1)S(1)}, bf16[60,96,192]{2,1,0:T(8,128)(2,1)}, u32[]{:S(2)}) copy-start(bf16[60,96,192]{2,1,0:T(8,128)(2,1)} %first_ref.1) | copy-start | bytes 6635524
  1.2 11.1 %collective-permute-start = (bf16[400,192]{1,0:T(8,128)(2,1)S(1)}, bf16[400,192]{1,0:T(8,128)(2,1)S(1)}, u32[]{:S(2)}, u32[]{:S(2)}) collective-permute-start(bf16[400,192]{1,0:T(8,128)(2,1)S(1)} %get-tuple-element.26), channel_id=1, source_target_pairs={{0,1},{1,0},{2,3},{3,2},{4,5},{5,4},{6,7},{7,6},{8,9},{9,8},{10,11... | collective-permute-start | bytes 460808 | tf_op jit(solution)/shard_map/ppermute | solution.py:545
  1.9 10.4 %collective-permute-start.1 = (bf16[400,192]{1,0:T(8,128)(2,1)S(1)}, bf16[400,192]{1,0:T(8,128)(2,1)S(1)}, u32[]{:S(2)}, u32[]{:S(2)}) collective-permute-start(bf16[400,192]{1,0:T(8,128)(2,1)S(1)} %get-tuple-element.27), channel_id=1, source_target_pairs={{1,2},{3,4},{5,6},{7,8},{9,10},{11,12},{13,14},{2,1},{4,3},{6,5},{... | collective-permute-start | bytes 460808 | tf_op jit(solution)/shard_map/ppermute | solution.py:544
  18.9 5.9 %collective-permute-start.3 = (f32[24,128]{1,0:T(8,128)S(1)}, f32[24,128]{1,0:T(8,128)S(1)}, u32[]{:S(2)}, u32[]{:S(2)}) collective-permute-start(f32[24,128]{1,0:T(8,128)S(1)} %get-tuple-element.34.mine_ref), channel_id=1, source_target_pairs={{1,2},{3,4},{5,6},{7,8},{9,10},{11,12},{13,14},{2,1},{4,3},{6,5},{... | collective-permute-start | bytes 36872 | tf_op jit(solution)/shard_map/ppermute | solution.py:583
  22.3 2.5 %collective-permute-start.2 = (f32[24,128]{1,0:T(8,128)S(1)}, f32[24,128]{1,0:T(8,128)S(1)}, u32[]{:S(2)}, u32[]{:S(2)}) collective-permute-start(f32[24,128]{1,0:T(8,128)S(1)} %get-tuple-element.34.mine_ref), channel_id=1, source_target_pairs={{0,1},{1,0},{2,3},{3,2},{4,5},{5,4},{6,7},{7,6},{8,9},{9,8},{10,11... | collective-permute-start | bytes 36872 | tf_op jit(solution)/shard_map/ppermute | solution.py:584

commit v10 on v9

--- a/solution.py
+++ b/solution.py
@@ -385,7 +385,7 @@
         total, alive = carry
         active[alive] = s
         set_units(units, total, s, table[12, s], CHUNK, 2)
-        return total + table[13, s], alive + table[17, s]
+        return total + table[13, s] * table[17, s], alive + table[17, s]
 
     carry = lax.fori_loop(0, own, prepare_own, (0, 0))
 
@@ -412,7 +412,8 @@
 
 
 def rest_kernel(
-    table_v, gap_base, fr_b, masks, acc, sq_a, sq_b, out_ref, table, active, sem_t,
+    table_v, gap_base, fr_a, fr_b, masks, acc_in, sq_a_in, sq_b_in,
+    out_ref, acc, sq_a, sq_b, table, units, active, sem_t,
 ):
     own = (acc.shape[0] - 1) // 3
     to_scalar = pltpu.make_async_copy(table_v, table, sem_t)
@@ -420,13 +421,18 @@
     out_ref[...] = jnp.zeros(out_ref.shape, jnp.float32)
     to_scalar.wait()
 
-    def listed(s, alive):
+    def listed(s, carry):
+        total, alive = carry
         active[alive] = s
-        return alive + 1 - table[17, s]
-
-    alive = lax.fori_loop(0, own, listed, 0)
+        set_units(units, total, s, table[12, s], CHUNK, 2)
+        other = 1 - table[17, s]
+        return total + table[13, s] * other, alive + other
+
+    total, alive = lax.fori_loop(0, own, listed, (0, 0))
+    spare = 3 * own
     for at in range(CLOSE - 1):
-        active[alive + at] = 3 * own
+        active[alive + at] = spare
+    run_units(CHUNK // 2, total, units, table, spare, fr_a, fr_b, acc, sq_a, sq_b, masks)
     finish_slots(alive, active, table, out_ref, gap_base, fr_b, masks, acc, sq_a, sq_b)
 
 
@@ -556,7 +562,7 @@
         pltpu.SMEM((FIELDS, LANES), jnp.int32),
         pltpu.SMEM(((3 * own + 1) * (W // CHUNK) + PAIR,), jnp.int32),
     ]
-    held = pl.pallas_call(
+    fr_a, *held = pl.pallas_call(
         inner_kernel,
         out_shape=(frames_a, *state),
         in_specs=[vmem] * 3,
@@ -579,21 +585,21 @@
             *scratch, pltpu.SMEM((slots + CLOSE,), jnp.int32), pltpu.SemaphoreType.DMA],
         compiler_params=limit(8),
         name="outer_sums",
-    )(plan, from_pair, from_other, gap, *held)
+    )(plan, from_pair, from_other, gap, fr_a, *held)
     other_sums = lax.ppermute(sums, "span", others)
     pair_sums = lax.ppermute(sums, "span", pairs)
-    rest = pl.pallas_call(
+    rest, *_ = pl.pallas_call(
         rest_kernel,
-        out_shape=jax.ShapeDtypeStruct((24, LANES), jnp.float32),
-        in_specs=[vmem] * 7,
-        out_specs=vmem,
+        out_shape=(jax.ShapeDtypeStruct((24, LANES), jnp.float32), *state[2:]),
+        in_specs=[vmem] * 8,
+        out_specs=(vmem,) * 4,
+        input_output_aliases={5 + i: 1 + i for i in range(3)},
         scratch_shapes=[
-            pltpu.SMEM((FIELDS, LANES), jnp.int32), pltpu.SMEM((slots + CLOSE,), jnp.int32),
-            pltpu.SemaphoreType.DMA],
+            *scratch, pltpu.SMEM((slots + CLOSE,), jnp.int32), pltpu.SemaphoreType.DMA],
         compiler_params=limit(8),
         cost_estimate=busy,
         name="rest_of_sums",
-    )(fields, gap, *held)
+    )(fields, gap, fr_a, *held)
     field = pl.pallas_call(
         functools.partial(update_kernel, own),
         out_shape=jax.ShapeDtypeStruct((planes // STRIDE, 3, GZX), jnp.float32),

time: 26.2 us -> 26.1 us (level); the launches traced: 26.1 us -> 26.2 us
  starting transfers between devices: 7.55 us -> 8.43 us
  waiting for transfers between devices: 0.71 us -> 0.01 us
    pallas_call x1, Pallas kernels: 6.58 us -> 5.49 us  [shards(): pl.pallas_call(outer_kernel, out_shape=(jax.ShapeDtypeStruct((24, LANES),...]
    pallas_call x1, Pallas kernels: 1.69 us -> 2.77 us  [shards(): pl.pallas_call(rest_kernel, out_shape=(jax.ShapeDtypeStruct((24, LANES),...]
    ppermute x1, starting transfers between devices: 3.43 us -> 4.3 us  [shards(): other_sums = lax.ppermute(sums, 'span', others)]
    ppermute x1, waiting for transfers between devices: 0.7 us -> 0.01 us  [shards(): other_sums = lax.ppermute(sums, 'span', others)]
  transfers between devices with their start and end apart: 4 -> 4, of which waited for: 1 -> 0; matrix products, arithmetic and copies ran while one was open for 0% -> 0% of each run, Pallas kernels for 33% -> 37%
where the time goes in v10:
time: 26.1 us; the launch traced here: 26.2 us
  Pallas kernels  16.6 us (64%)
  starting transfers between devices  8.43 us (32%)
  local copies, waits for them, and re-layouts  1.08 us (4%)
    pallas_call x1, Pallas kernels, shards(): pl.pallas_call(inner_kernel, out_shape=(frames_a, *state), in_specs=[vmem...  6.98 us
    pallas_call x1, Pallas kernels, shards(): pl.pallas_call(outer_kernel, out_shape=(jax.ShapeDtypeStruct((24, LANES),...  5.49 us
    ppermute x1, starting transfers between devices, shards(): other_sums = lax.ppermute(sums, 'span', others)  4.3 us
    ppermute x1, starting transfers between devices, shards(): from_other = lax.ppermute(to_other, 'span', others)  3.31 us
    pallas_call x1, Pallas kernels, shards(): pl.pallas_call(rest_kernel, out_shape=(jax.ShapeDtypeStruct((24, LANES),...  2.77 us
    pallas_call x1, Pallas kernels, shards(): pl.pallas_call(functools.partial(update_kernel, own), out_shape=jax.Shape...  1.27 us
    slice x1, local copies, waits for them, and re-layouts, shards(): low_planes, high_planes = (tile[:REACH], tile[planes - REACH:])  1.06 us
    ppermute x1, starting transfers between devices, shards(): from_pair = lax.ppermute(to_pair, 'span', pairs)  0.74 us
  transfers between devices with their start and end apart: 4, of which 0 were waited for; matrix products, arithmetic and copies ran while one was open for 0% of the time, Pallas kernels for 37%

profile of v10, /device:TPU:23, one launch (start us, length us, event | category | flops | bytes accessed | tf_op | source)
XLA Modules:
  0.0 26.2 jit_solution(2947003607582117155)
XLA Ops:
  0.0 0.0 copy-start.2
  0.0 0.0 copy-start.3
  0.0 1.1 %fusion = (bf16[4,96,192]{2,1,0:T(8,128)(2,1)S(1)}, bf16[4,96,192]{2,1,0:T(8,128)(2,1)S(1)}) fusion(bf16[60,96,192]{2,1,0:T(8,128)(2,1)} %second_ref.1), kind=kLoop, calls=%fused_computation | loop fusion | bytes 589824 | tf_op jit(solution)/shard_map/slice | solution.py:540
  1.1 0.0 copy-done.2
  1.1 0.0 copy-done.3
  1.1 0.0 copy-start
  1.1 0.0 copy-start.1
  1.2 0.7 %collective-permute-start = (bf16[400,192]{1,0:T(8,128)(2,1)S(1)}, bf16[400,192]{1,0:T(8,128)(2,1)S(1)}, u32[]{:S(2)}, u32[]{:S(2)}) collective-permute-start(bf16[400,192]{1,0:T(8,128)(2,1)S(1)} %get-tuple-element.27), channel_id=1, source_target_pairs={{0,1},{1,0},{2,3},{3,2},{4,5},{5,4},{6,7},{7,6},{8,9},{9,8},{10,11... | collective-permute-start | bytes 460808 | tf_op jit(solution)/shard_map/ppermute | solution.py:551
  1.9 3.3 %collective-permute-start.1 = (bf16[400,192]{1,0:T(8,128)(2,1)S(1)}, bf16[400,192]{1,0:T(8,128)(2,1)S(1)}, u32[]{:S(2)}, u32[]{:S(2)}) collective-permute-start(bf16[400,192]{1,0:T(8,128)(2,1)S(1)} %get-tuple-element.28), channel_id=1, source_target_pairs={{1,2},{3,4},{5,6},{7,8},{9,10},{11,12},{13,14},{2,1},{4,3},{6,5},{... | collective-permute-start | bytes 460808 | tf_op jit(solution)/shard_map/ppermute | solution.py:550
  5.2 0.0 copy-done
  5.2 0.0 copy-done.1
  5.3 7.0 %inner_sums.1 = (bf16[2,2,72,96,128]{4,3,2,1,0:T(8,128)(2,1)S(1)}, bf16[2,2,80,96,128]{4,3,2,1,0:T(8,128)(2,1)S(1)}, bf16[25,320,128]{2,1,0:T(8,128)(2,1)S(1)}, ...) custom-call(s32[8,128]{1,0:T(8,128)S(1)} %get-tuple-element.26.plan_ref, ...), custom_call_target="tpu_custom_call" | custom-call | flops 20000000000 | tf_op jit(solution)/shard_map/inner_sums/pallas_call | solution.py:565
  12.2 0.0 collective-permute-done.pair_ref
  12.3 0.0 collective-permute-done.1.other_ref
  12.3 5.5 %outer_sums.1 = (f32[24,128]{1,0:T(8,128)S(1)}, s32[24,128]{1,0:T(8,128)S(1)}, bf16[2,2,80,96,128]{4,3,2,1,0:T(8,128)(2,1)S(1)}, bf16[25,320,128]{2,1,0:T(8,128)...) custom-call(s32[8,128]{1,0:T(8,128)S(1)} %get-tuple-element.26.plan_, ...), custom_call_target="tpu_custom_call", output_to_operand_aliasing={{2}: (5, {}), {3}: (6, {}), {4}: (7, {}), {5}: (8, {}), {6}... | custom-call | tf_op jit(solution)/shard_map/outer_sums/pallas_call | solution.py:576
  17.8 4.3 %collective-permute-start.3 = (f32[24,128]{1,0:T(8,128)S(1)}, f32[24,128]{1,0:T(8,128)S(1)}, u32[]{:S(2)}, u32[]{:S(2)}) collective-permute-start(f32[24,128]{1,0:T(8,128)S(1)} %get-tuple-element.35.mine_ref), channel_id=1, source_target_pairs={{1,2},{3,4},{5,6},{7,8},{9,10},{11,12},{13,14},{2,1},{4,3},{6,5},{... | collective-permute-start | bytes 36872 | tf_op jit(solution)/shard_map/ppermute | solution.py:589
  22.1 0.1 collective-permute-start.2
  22.2 2.8 %rest_of_sums.1 = (f32[24,128]{1,0:T(8,128)S(1)}, f32[25,208,256]{2,1,0:T(8,128)S(1)}, f32[25,64,128]{2,1,0:T(8,128)S(1)}, f32[25,80,128]{2,1,0:T(8,128)S(1)}) custom-call(s32[24,128]{1,0:T(8,128)S(1)} %get-tuple-element.36.table_v, s32[64,256]{1,0:T(8,128)S(1)} %gap_table.1.gap_ref.gap_base, ...), custom_call_target="tpu_custom_call", output_to_operand_aliasing={{1}: (5, {}), {2}: (6, {}), {3}: (7, {})} | custom-call | flops 20000000000 | tf_op jit(solution)/shard_map/rest_of_sums/pallas_call | solution.py:591
  24.9 0.0 collective-permute-done.3.other_ref
  24.9 0.0 collective-permute-done.2.pair_ref
  25.0 1.3 %smoothed_update.1 = f32[5,3,128]{2,1,0:T(4,128)} custom-call(f32[24,128]{1,0:T(8,128)S(1)} %get-tuple-element.35.mine_ref, f32[24,128]{1,0:T(8,128)S(1)} %get-tuple-element.42.rest_ref, f32[24,128]{1,0:T(8,128)S(1)} %collective-permute-done.2.pair_ref, f32[24,128]{1,0:T(8,128)S(1)} %collective-permute-done.3.other_ref), custom_call_target="tpu_custom_call" | custom-call | tf_op jit(solution)/shard_map/smoothed_update/pallas_call | solution.py:603
  (2 shorter events, 0.1 us)
Async XLA Ops:
  0.0 1.1 %copy-start.2 = (s32[3,8]{1,0:T(4,128)S(1)}, s32[3,8]{1,0:T(4,128)}, u32[]{:S(2)}) copy-start(s32[3,8]{1,0:T(4,128)} %shift_ref.1) | copy-start | bytes 292
  0.0 1.1 %copy-start.3 = (s32[8]{0:T(128)S(1)}, s32[8]{0:T(128)}, u32[]{:S(2)}) copy-start(s32[8]{0:T(128)} %param.6) | copy-start | bytes 100
  1.1 4.1 %copy-start = (bf16[60,96,192]{2,1,0:T(8,128)(2,1)S(1)}, bf16[60,96,192]{2,1,0:T(8,128)(2,1)}, u32[]{:S(2)}) copy-start(bf16[60,96,192]{2,1,0:T(8,128)(2,1)} %second_ref.1) | copy-start | bytes 6635524
  1.1 4.1 %copy-start.1 = (bf16[60,96,192]{2,1,0:T(8,128)(2,1)S(1)}, bf16[60,96,192]{2,1,0:T(8,128)(2,1)}, u32[]{:S(2)}) copy-start(bf16[60,96,192]{2,1,0:T(8,128)(2,1)} %first_ref.1) | copy-start | bytes 6635524
  1.2 11.1 %collective-permute-start = (bf16[400,192]{1,0:T(8,128)(2,1)S(1)}, bf16[400,192]{1,0:T(8,128)(2,1)S(1)}, u32[]{:S(2)}, u32[]{:S(2)}) collective-permute-start(bf16[400,192]{1,0:T(8,128)(2,1)S(1)} %get-tuple-element.27), channel_id=1, source_target_pairs={{0,1},{1,0},{2,3},{3,2},{4,5},{5,4},{6,7},{7,6},{8,9},{9,8},{10,11... | collective-permute-start | bytes 460808 | tf_op jit(solution)/shard_map/ppermute | solution.py:551
  1.9 10.3 %collective-permute-start.1 = (bf16[400,192]{1,0:T(8,128)(2,1)S(1)}, bf16[400,192]{1,0:T(8,128)(2,1)S(1)}, u32[]{:S(2)}, u32[]{:S(2)}) collective-permute-start(bf16[400,192]{1,0:T(8,128)(2,1)S(1)} %get-tuple-element.28), channel_id=1, source_target_pairs={{1,2},{3,4},{5,6},{7,8},{9,10},{11,12},{13,14},{2,1},{4,3},{6,5},{... | collective-permute-start | bytes 460808 | tf_op jit(solution)/shard_map/ppermute | solution.py:550
  17.8 7.2 %collective-permute-start.3 = (f32[24,128]{1,0:T(8,128)S(1)}, f32[24,128]{1,0:T(8,128)S(1)}, u32[]{:S(2)}, u32[]{:S(2)}) collective-permute-start(f32[24,128]{1,0:T(8,128)S(1)} %get-tuple-element.35.mine_ref), channel_id=1, source_target_pairs={{1,2},{3,4},{5,6},{7,8},{9,10},{11,12},{13,14},{2,1},{4,3},{6,5},{... | collective-permute-start | bytes 36872 | tf_op jit(solution)/shard_map/ppermute | solution.py:589
  22.1 2.9 %collective-permute-start.2 = (f32[24,128]{1,0:T(8,128)S(1)}, f32[24,128]{1,0:T(8,128)S(1)}, u32[]{:S(2)}, u32[]{:S(2)}) collective-permute-start(f32[24,128]{1,0:T(8,128)S(1)} %get-tuple-element.35.mine_ref), channel_id=1, source_target_pairs={{0,1},{1,0},{2,3},{3,2},{4,5},{5,4},{6,7},{7,6},{8,9},{9,8},{10,11... | collective-permute-start | bytes 36872 | tf_op jit(solution)/shard_map/ppermute | solution.py:590

commit v11 on v10

--- a/solution.py
+++ b/solution.py
@@ -32,6 +32,7 @@
 PAIR = 8
 REST = 4
 CLOSE = 4
+CLOSE_REST = 3
 FAR = 4096
 
 
@@ -285,7 +286,7 @@
     run_units(CHUNK, total, units, table, 3 * own, fr_a, fr_b, acc, sq_a, sq_b, masks)
 
 
-def finish_slots(alive, active, table, out_ref, gap_base, fr_b, masks, acc, sq_a, sq_b):
+def finish_slots(width, alive, active, table, out_ref, gap_base, fr_b, masks, acc, sq_a, sq_b):
     cols = 2 * LANES
     col_one = lax.broadcasted_iota(jnp.int32, (1, cols), 1)
     lag_one = jnp.where(col_one >= ROWS_B, 1, 0) + jnp.where(col_one >= 2 * ROWS_B, 1, 0)
@@ -299,8 +300,8 @@
     mean_lane = lax.broadcasted_iota(jnp.int32, (1, LANES), 1) == 3 * ROWS_B - LANES
 
     def finish(t, carry):
-        for h in range(CLOSE):
-            s = active[CLOSE * t + h]
+        for h in range(width):
+            s = active[width * t + h]
             f_b = table[2, s]
             z_b = pl.multiple_of(table[3, s], 16)
             offset = table[5, s]
@@ -348,7 +349,7 @@
             out_ref[18:22] += jnp.where(lane_4 == s, sums, 0.0)
         return carry
 
-    lax.fori_loop(0, (alive + CLOSE - 1) // CLOSE, finish, 0)
+    lax.fori_loop(0, (alive + width - 1) // width, finish, 0)
 
 
 def outer_kernel(
@@ -408,7 +409,7 @@
     for at in range(CLOSE - 1):
         active[alive + at] = spare
     run_units(CHUNK // 2, total, units, table, spare, fr_a, fr_b, acc, sq_a, sq_b, masks)
-    finish_slots(alive, active, table, out_ref, gap_base, fr_b, masks, acc, sq_a, sq_b)
+    finish_slots(CLOSE, alive, active, table, out_ref, gap_base, fr_b, masks, acc, sq_a, sq_b)
 
 
 def rest_kernel(
@@ -433,7 +434,7 @@
     for at in range(CLOSE - 1):
         active[alive + at] = spare
     run_units(CHUNK // 2, total, units, table, spare, fr_a, fr_b, acc, sq_a, sq_b, masks)
-    finish_slots(alive, active, table, out_ref, gap_base, fr_b, masks, acc, sq_a, sq_b)
+    finish_slots(CLOSE_REST, alive, active, table, out_ref, gap_base, fr_b, masks, acc, sq_a, sq_b)
 
 
 def update_kernel(own, mine_ref, rest_ref, pair_ref, other_ref, out_ref):

time: 26.1 us -> 25.9 us (level)
  the two profiles are of different devices: /device:TPU:23 before, /device:TPU:17 now
where the time goes in v11:
time: 25.9 us; the launch traced here: 25.5 us
  Pallas kernels  16 us (62%)
  starting transfers between devices  8.27 us (32%)
  local copies, waits for them, and re-layouts  1.08 us (4%)
    pallas_call x1, Pallas kernels, shards(): pl.pallas_call(inner_kernel, out_shape=(frames_a, *state), in_specs=[vmem...  7.76 us
    pallas_call x1, Pallas kernels, shards(): pl.pallas_call(outer_kernel, out_shape=(jax.ShapeDtypeStruct((24, LANES),...  3.96 us
    ppermute x1, starting transfers between devices, shards(): from_other = lax.ppermute(to_other, 'span', others)  3.31 us
    pallas_call x1, Pallas kernels, shards(): pl.pallas_call(rest_kernel, out_shape=(jax.ShapeDtypeStruct((24, LANES),...  2.95 us
    ppermute x1, starting transfers between devices, shards(): other_sums = lax.ppermute(sums, 'span', others)  2.57 us
    ppermute x1, starting transfers between devices, shards(): pair_sums = lax.ppermute(sums, 'span', pairs)  1.65 us
    pallas_call x1, Pallas kernels, shards(): pl.pallas_call(functools.partial(update_kernel, own), out_shape=jax.Shape...  1.27 us
    slice x1, local copies, waits for them, and re-layouts, shards(): low_planes, high_planes = (tile[:REACH], tile[planes - REACH:])  1.06 us
  transfers between devices with their start and end apart: 4, of which 0 were waited for; matrix products, arithmetic and copies ran while one was open for 0% of the time, Pallas kernels for 42%

profile of v11, /device:TPU:17, one launch (start us, length us, event | category | flops | bytes accessed | tf_op | source)
XLA Modules:
  0.0 25.5 jit_solution(4581582539370676044)
XLA Ops:
  0.0 0.0 copy-start.2
  0.0 0.0 copy-start.3
  0.0 1.1 %fusion = (bf16[4,96,192]{2,1,0:T(8,128)(2,1)S(1)}, bf16[4,96,192]{2,1,0:T(8,128)(2,1)S(1)}) fusion(bf16[60,96,192]{2,1,0:T(8,128)(2,1)} %second_ref.1), kind=kLoop, calls=%fused_computation | loop fusion | bytes 589824 | tf_op jit(solution)/shard_map/slice | solution.py:541
  1.1 0.0 copy-done.2
  1.1 0.0 copy-done.3
  1.1 0.0 copy-start
  1.1 0.0 copy-start.1
  1.2 0.7 %collective-permute-start = (bf16[400,192]{1,0:T(8,128)(2,1)S(1)}, bf16[400,192]{1,0:T(8,128)(2,1)S(1)}, u32[]{:S(2)}, u32[]{:S(2)}) collective-permute-start(bf16[400,192]{1,0:T(8,128)(2,1)S(1)} %get-tuple-element.27), channel_id=1, source_target_pairs={{0,1},{1,0},{2,3},{3,2},{4,5},{5,4},{6,7},{7,6},{8,9},{9,8},{10,11... | collective-permute-start | bytes 460808 | tf_op jit(solution)/shard_map/ppermute | solution.py:552
  1.9 3.3 %collective-permute-start.1 = (bf16[400,192]{1,0:T(8,128)(2,1)S(1)}, bf16[400,192]{1,0:T(8,128)(2,1)S(1)}, u32[]{:S(2)}, u32[]{:S(2)}) collective-permute-start(bf16[400,192]{1,0:T(8,128)(2,1)S(1)} %get-tuple-element.28), channel_id=1, source_target_pairs={{1,2},{3,4},{5,6},{7,8},{9,10},{11,12},{13,14},{2,1},{4,3},{6,5},{... | collective-permute-start | bytes 460808 | tf_op jit(solution)/shard_map/ppermute | solution.py:551
  5.2 0.0 copy-done
  5.2 0.0 copy-done.1
  5.3 7.8 %inner_sums.1 = (bf16[2,2,72,96,128]{4,3,2,1,0:T(8,128)(2,1)S(1)}, bf16[2,2,80,96,128]{4,3,2,1,0:T(8,128)(2,1)S(1)}, bf16[25,320,128]{2,1,0:T(8,128)(2,1)S(1)}, ...) custom-call(s32[8,128]{1,0:T(8,128)S(1)} %get-tuple-element.26.plan_ref, ...), custom_call_target="tpu_custom_call" | custom-call | flops 20000000000 | tf_op jit(solution)/shard_map/inner_sums/pallas_call | solution.py:566
  13.0 0.0 collective-permute-done.pair_ref
  13.0 0.0 collective-permute-done.1.other_ref
  13.0 4.0 %outer_sums.1 = (f32[24,128]{1,0:T(8,128)S(1)}, s32[24,128]{1,0:T(8,128)S(1)}, bf16[2,2,80,96,128]{4,3,2,1,0:T(8,128)(2,1)S(1)}, bf16[25,320,128]{2,1,0:T(8,128)...) custom-call(s32[8,128]{1,0:T(8,128)S(1)} %get-tuple-element.26.plan_, ...), custom_call_target="tpu_custom_call", output_to_operand_aliasing={{2}: (5, {}), {3}: (6, {}), {4}: (7, {}), {5}: (8, {}), {6}... | custom-call | tf_op jit(solution)/shard_map/outer_sums/pallas_call | solution.py:577
  17.0 2.6 %collective-permute-start.3 = (f32[24,128]{1,0:T(8,128)S(1)}, f32[24,128]{1,0:T(8,128)S(1)}, u32[]{:S(2)}, u32[]{:S(2)}) collective-permute-start(f32[24,128]{1,0:T(8,128)S(1)} %get-tuple-element.35.mine_ref), channel_id=1, source_target_pairs={{1,2},{3,4},{5,6},{7,8},{9,10},{11,12},{13,14},{2,1},{4,3},{6,5},{... | collective-permute-start | bytes 36872 | tf_op jit(solution)/shard_map/ppermute | solution.py:590
  19.6 1.7 %collective-permute-start.2 = (f32[24,128]{1,0:T(8,128)S(1)}, f32[24,128]{1,0:T(8,128)S(1)}, u32[]{:S(2)}, u32[]{:S(2)}) collective-permute-start(f32[24,128]{1,0:T(8,128)S(1)} %get-tuple-element.35.mine_ref), channel_id=1, source_target_pairs={{0,1},{1,0},{2,3},{3,2},{4,5},{5,4},{6,7},{7,6},{8,9},{9,8},{10,11... | collective-permute-start | bytes 36872 | tf_op jit(solution)/shard_map/ppermute | solution.py:591
  21.2 3.0 %rest_of_sums.1 = (f32[24,128]{1,0:T(8,128)S(1)}, f32[25,208,256]{2,1,0:T(8,128)S(1)}, f32[25,64,128]{2,1,0:T(8,128)S(1)}, f32[25,80,128]{2,1,0:T(8,128)S(1)}) custom-call(s32[24,128]{1,0:T(8,128)S(1)} %get-tuple-element.36.table_v, s32[64,256]{1,0:T(8,128)S(1)} %gap_table.1.gap_ref.gap_base, ...), custom_call_target="tpu_custom_call", output_to_operand_aliasing={{1}: (5, {}), {2}: (6, {}), {3}: (7, {})} | custom-call | flops 20000000000 | tf_op jit(solution)/shard_map/rest_of_sums/pallas_call | solution.py:592
  24.2 0.0 collective-permute-done.3.other_ref
  24.2 0.0 collective-permute-done.2.pair_ref
  24.2 1.3 %smoothed_update.1 = f32[5,3,128]{2,1,0:T(4,128)} custom-call(f32[24,128]{1,0:T(8,128)S(1)} %get-tuple-element.35.mine_ref, f32[24,128]{1,0:T(8,128)S(1)} %get-tuple-element.42.rest_ref, f32[24,128]{1,0:T(8,128)S(1)} %collective-permute-done.2.pair_ref, f32[24,128]{1,0:T(8,128)S(1)} %collective-permute-done.3.other_ref), custom_call_target="tpu_custom_call" | custom-call | tf_op jit(solution)/shard_map/smoothed_update/pallas_call | solution.py:604
  (2 shorter events, 0.1 us)
Async XLA Ops:
  0.0 1.1 %copy-start.2 = (s32[3,8]{1,0:T(4,128)S(1)}, s32[3,8]{1,0:T(4,128)}, u32[]{:S(2)}) copy-start(s32[3,8]{1,0:T(4,128)} %shift_ref.1) | copy-start | bytes 292
  0.0 1.1 %copy-start.3 = (s32[8]{0:T(128)S(1)}, s32[8]{0:T(128)}, u32[]{:S(2)}) copy-start(s32[8]{0:T(128)} %param.6) | copy-start | bytes 100
  1.1 4.1 %copy-start = (bf16[60,96,192]{2,1,0:T(8,128)(2,1)S(1)}, bf16[60,96,192]{2,1,0:T(8,128)(2,1)}, u32[]{:S(2)}) copy-start(bf16[60,96,192]{2,1,0:T(8,128)(2,1)} %second_ref.1) | copy-start | bytes 6635524
  1.1 4.1 %copy-start.1 = (bf16[60,96,192]{2,1,0:T(8,128)(2,1)S(1)}, bf16[60,96,192]{2,1,0:T(8,128)(2,1)}, u32[]{:S(2)}) copy-start(bf16[60,96,192]{2,1,0:T(8,128)(2,1)} %first_ref.1) | copy-start | bytes 6635524
  1.2 11.8 %collective-permute-start = (bf16[400,192]{1,0:T(8,128)(2,1)S(1)}, bf16[400,192]{1,0:T(8,128)(2,1)S(1)}, u32[]{:S(2)}, u32[]{:S(2)}) collective-permute-start(bf16[400,192]{1,0:T(8,128)(2,1)S(1)} %get-tuple-element.27), channel_id=1, source_target_pairs={{0,1},{1,0},{2,3},{3,2},{4,5},{5,4},{6,7},{7,6},{8,9},{9,8},{10,11... | collective-permute-start | bytes 460808 | tf_op jit(solution)/shard_map/ppermute | solution.py:552
  1.9 11.1 %collective-permute-start.1 = (bf16[400,192]{1,0:T(8,128)(2,1)S(1)}, bf16[400,192]{1,0:T(8,128)(2,1)S(1)}, u32[]{:S(2)}, u32[]{:S(2)}) collective-permute-start(bf16[400,192]{1,0:T(8,128)(2,1)S(1)} %get-tuple-element.28), channel_id=1, source_target_pairs={{1,2},{3,4},{5,6},{7,8},{9,10},{11,12},{13,14},{2,1},{4,3},{6,5},{... | collective-permute-start | bytes 460808 | tf_op jit(solution)/shard_map/ppermute | solution.py:551
  17.0 7.2 %collective-permute-start.3 = (f32[24,128]{1,0:T(8,128)S(1)}, f32[24,128]{1,0:T(8,128)S(1)}, u32[]{:S(2)}, u32[]{:S(2)}) collective-permute-start(f32[24,128]{1,0:T(8,128)S(1)} %get-tuple-element.35.mine_ref), channel_id=1, source_target_pairs={{1,2},{3,4},{5,6},{7,8},{9,10},{11,12},{13,14},{2,1},{4,3},{6,5},{... | collective-permute-start | bytes 36872 | tf_op jit(solution)/shard_map/ppermute | solution.py:590
  19.6 4.6 %collective-permute-start.2 = (f32[24,128]{1,0:T(8,128)S(1)}, f32[24,128]{1,0:T(8,128)S(1)}, u32[]{:S(2)}, u32[]{:S(2)}) collective-permute-start(f32[24,128]{1,0:T(8,128)S(1)} %get-tuple-element.35.mine_ref), channel_id=1, source_target_pairs={{0,1},{1,0},{2,3},{3,2},{4,5},{5,4},{6,7},{7,6},{8,9},{9,8},{10,11... | collective-permute-start | bytes 36872 | tf_op jit(solution)/shard_map/ppermute | solution.py:591
